TPU v7x, 256 devices: a whole 4x4x8 slice. The times are simulated.
256 devices in a mesh: orb: 64 (over z, x, core), grp: 4 (over y).
Axes of the slice: x: 4, y: 4, z: 8, core: 2. Of those that a mesh axis runs over, the one named last changes fastest.
Arguments:
- orbitals: float32 [256, 262144], P(('orb', 'grp')), may hold values from -10 to 10
- potential: float32 [4096, 64], replicated, may hold values from -2 to 2
- occupation: float32 [256], replicated, may hold values from 0.5 to 2
- region_bounds: int32 [256, 2], replicated, may hold values from 0 to 64, as said below
Outputs:
- orthonormal: float32 [256, 262144], P(('orb', 'grp'))
- gradient: float32 [256, 262144], P(('orb', 'grp'))
- subspace: float32 [256, 256], replicated
- density: float32 [4096, 64], P(('orb', 'grp'))
Inputs may be any that keep to these rules, and one draw needn't show every extreme that they name: Orbital i's region is planes region_bounds[i,0] to region_bounds[i,1] - 1, at least 16 planes.
All inputs are finite; a program needn't handle non-finite values.
Results may differ from a plain program's by a relative error of at most 0.0003.
Values sent between devices are 32-bit elements; how exact they have to be, the bound alone decides.
No kernel may reach another device: no remote copies, remote signals or barrier semaphores. Data moves between devices by JAX's collectives and lax.ppermute only.
A program may use at most 128 MiB of HBM per device.

v0:
```python
import functools

import jax
import jax.numpy as jnp
import ml_dtypes
import numpy as np
from jax import lax
from jax.experimental import pallas as pl
from jax.experimental.pallas import tpu as pltpu
from jax.sharding import PartitionSpec as P

G = 64
LANES = 128
PAIRS = G * G // LANES
PAD = 8
SHIFT = 2
STRIP = 16
ROWS = 8
BLOCK = 32

magic_taps = (0.0028, -0.0236, 0.1026, 0.8364, 0.1026, -0.0236, 0.0028)
kinetic_taps = (
    -1.0 / 560.0,
    8.0 / 315.0,
    -0.2,
    1.6,
    -205.0 / 72.0,
    1.6,
    -0.2,
    8.0 / 315.0,
    -1.0 / 560.0,
)
precise = lax.Precision.HIGHEST
AXES = ("orb", "grp")


def banded(extent, taps):
    radius = len(taps) // 2
    matrix = np.zeros((extent, extent))
    for position, weight in enumerate(taps):
        matrix += weight * np.eye(extent, k=position - radius)
    return matrix


def shifted_blocks(along_y, along_z):
    radius = len(along_y) // 2
    blocks = np.zeros((2 * SHIFT + 1, 2, G, 2, G))
    for shift in range(-SHIFT, SHIFT + 1):
        for source in range(2):
            for target in range(2):
                offset = 2 * shift + source - target
                if abs(offset) <= radius:
                    blocks[shift + SHIFT, source, :, target, :] = (
                        along_y[offset + radius] * along_z.T
                    )
    return blocks.reshape((2 * SHIFT + 1) * LANES, LANES)


def split_constant(matrix):
    high = matrix.astype(ml_dtypes.bfloat16)
    low = (matrix - high.astype(np.float64)).astype(ml_dtypes.bfloat16)
    return high, low


def filter_constants():
    magic = shifted_blocks(magic_taps, banded(G, magic_taps))
    kinetic = shifted_blocks(kinetic_taps, np.eye(G)) + shifted_blocks(
        (1.0,), banded(G, kinetic_taps)
    )
    return (
        split_constant(np.concatenate([magic, kinetic], axis=1)),
        split_constant(magic),
    )


def plane_filter(read, first, taps):
    radius = len(taps) // 2
    total = taps[radius] * read(first)
    for step in range(1, radius + 1):
        total += taps[radius + step] * (read(first + step) + read(first - step))
    return total


def hamiltonian_kernel(
    place_ref,
    bounds_ref,
    occupation_ref,
    orbital_ref,
    potential_ref,
    both_high_ref,
    both_low_ref,
    magic_high_ref,
    magic_low_ref,
    keep_ref,
    give_ref,
    density_ref,
    source,
    filtered,
    kinetic,
):
    margin = len(kinetic_taps) // 2
    position, core = place_ref[0], place_ref[1]

    zeros = jnp.zeros((margin, PAIRS + 2 * PAD, LANES), jnp.float32)
    source[:margin] = zeros
    source[margin + G :] = zeros
    edge = jnp.zeros((G + 2 * margin, PAD, LANES), jnp.float32)
    source[:, :PAD] = edge
    source[:, PAD + PAIRS :] = edge
    zeros = jnp.zeros((margin, PAIRS, LANES), jnp.float32)
    filtered[:margin] = zeros
    filtered[margin + G :] = zeros

    def product(x, high_ref, low_ref):
        shifted = jnp.concatenate(
            [
                source[pl.ds(margin + x, STRIP), PAD + s : PAD + s + PAIRS].reshape(
                    STRIP * PAIRS, LANES
                )
                for s in range(-SHIFT, SHIFT + 1)
            ],
            axis=1,
        )
        high = shifted.astype(jnp.bfloat16)
        low = (shifted - high.astype(jnp.float32)).astype(jnp.bfloat16)
        dot = functools.partial(jnp.dot, preferred_element_type=jnp.float32)
        return dot(high, high_ref[...]) + (dot(low, high_ref[...]) + dot(high, low_ref[...]))

    def own(x):
        return source[pl.ds(margin + x, STRIP), PAD : PAD + PAIRS]

    def half(x):
        return filtered[pl.ds(margin + x, STRIP)]

    planes = lax.broadcasted_iota(jnp.int32, (STRIP, PAIRS, LANES), 0)
    begin, end = bounds_ref[position, 0], bounds_ref[position, 1]
    blocks = STRIP * PAIRS // ROWS
    half_planes = G // 2

    def tiled(strip):
        return strip.reshape(blocks, ROWS, LANES)

    for side, out_ref in ((core, keep_ref), (1 - core, give_ref)):
        for strip in range(0, half_planes, STRIP):
            x = half_planes * side + strip
            inside = (planes + x >= begin) & (planes + x < end)
            masked = jnp.where(inside, orbital_ref[pl.ds(x, STRIP)], 0.0)
            source[pl.ds(margin + x, STRIP), PAD : PAD + PAIRS] = masked
            first = strip * PAIRS // ROWS
            out_ref[first : first + blocks, :ROWS, :] = tiled(masked)

    @pl.loop(0, G, step=STRIP)
    def _(x):
        both = product(x, both_high_ref, both_low_ref)
        filtered[pl.ds(margin + x, STRIP)] = both[:, :LANES].reshape(STRIP, PAIRS, LANES)
        kinetic[pl.ds(x, STRIP)] = both[:, LANES:].reshape(STRIP, PAIRS, LANES) + plane_filter(
            own, x, kinetic_taps
        )

    scale = occupation_ref[position] * (1.0 / occupation_ref.shape[0])
    lines = STRIP * G // 2

    @pl.loop(0, G, step=STRIP)
    def _(x):
        realspace = plane_filter(half, x, magic_taps)
        density_ref[pl.ds(x, STRIP)] = scale * realspace * realspace
        potential = jnp.concatenate(
            [potential_ref[pl.ds(x * G + odd, lines, stride=2), :] for odd in range(2)], axis=1
        ).reshape(STRIP, PAIRS, LANES)
        source[pl.ds(margin + x, STRIP), PAD : PAD + PAIRS] = realspace * potential

    @pl.loop(0, G, step=STRIP)
    def _(x):
        filtered[pl.ds(margin + x, STRIP)] = product(x, magic_high_ref, magic_low_ref).reshape(
            STRIP, PAIRS, LANES
        )

    for side, out_ref in ((core, keep_ref), (1 - core, give_ref)):
        for strip in range(0, half_planes, STRIP):
            x = half_planes * side + strip
            images = plane_filter(half, x, magic_taps) - 0.5 * kinetic[pl.ds(x, STRIP)]
            first = strip * PAIRS // ROWS
            out_ref[first : first + blocks, ROWS:, :] = tiled(images)


def vmem():
    return pl.BlockSpec(memory_space=pltpu.VMEM)


def smem():
    return pl.BlockSpec(memory_space=pltpu.SMEM)


def apply_hamiltonian(place, region_bounds, occupation, orbital, potential):
    (both_high, both_low), (magic_high, magic_low) = filter_constants()
    margin = len(kinetic_taps) // 2
    side = jax.ShapeDtypeStruct((G * PAIRS // ROWS // 2, 2 * ROWS, LANES), jnp.float32)
    grid = jax.ShapeDtypeStruct((G, PAIRS, LANES), jnp.float32)
    return pl.pallas_call(
        hamiltonian_kernel,
        out_shape=(side, side, grid),
        in_specs=[smem()] * 3 + [vmem()] * 6,
        out_specs=(vmem(),) * 3,
        scratch_shapes=[
            pltpu.VMEM((G + 2 * margin, PAIRS + 2 * PAD, LANES), jnp.float32),
            pltpu.VMEM((G + 2 * margin, PAIRS, LANES), jnp.float32),
            pltpu.VMEM((G, PAIRS, LANES), jnp.float32),
        ],
        compiler_params=pltpu.CompilerParams(vmem_limit_bytes=40 * 2**20),
        cost_estimate=pl.CostEstimate(
            flops=6 * 2048 * 640 * 384, bytes_accessed=5 * 2**20, transcendentals=0
        ),
        name="hamiltonian",
    )(
        place,
        region_bounds,
        occupation,
        orbital,
        potential,
        jnp.asarray(both_high),
        jnp.asarray(both_low),
        jnp.asarray(magic_high),
        jnp.asarray(magic_low),
    )


def transposed_dot(a, b):
    return lax.dot_general(
        a, b, (((1,), (1,)), ((), ())), precision=precise, preferred_element_type=jnp.float32
    )


CORES = 2
LINES = 4


def natural_rows(flat_ref, natural_ref, core, gather):
    planes, orbitals, _ = natural_ref.shape
    groups = orbitals // (CORES * LINES)
    stride = CORES * LINES * planes
    for slot in range(CORES):
        for line in range(LINES):
            for plane in range(planes):
                inner = pl.ds((line * CORES + slot) * planes + plane, groups, stride=stride)
                outer = pl.ds((slot ^ core) * LINES + line, groups, stride=CORES * LINES)
                if gather:
                    natural_ref[plane, outer, :] = flat_ref[inner, :]
                else:
                    flat_ref[inner, :] = natural_ref[plane, outer, :]


def overlap_kernel(core_ref, flat_ref, natural_ref, packed_ref):
    for core in range(CORES):

        @pl.when(core_ref[0] == core)
        def _(core=core):
            natural_rows(flat_ref, natural_ref, core, True)

    planes, size, _ = natural_ref.shape
    half = planes // 2
    total = None
    for plane in range(0, half, 2):
        psi = jnp.concatenate([natural_ref[plane], natural_ref[plane + 1]], axis=1)
        images = jnp.concatenate(
            [natural_ref[half + plane], natural_ref[half + plane + 1]], axis=1
        )
        term = transposed_dot(psi, jnp.concatenate([psi, images], axis=0))
        total = term if total is None else total + term
    row = lax.broadcasted_iota(jnp.int32, (size, size), 0)
    column = lax.broadcasted_iota(jnp.int32, (size, size), 1)
    hamilton = total[:, size:]
    packed = jnp.where(row <= column, total[:, :size], hamilton)
    diagonal = jnp.sum(jnp.where(row == column, hamilton, 0.0), axis=1, keepdims=True)
    chunks = size // ROWS
    for part in range(size // LANES):
        packed_ref[:, part * ROWS : (part + 1) * ROWS, :] = packed[
            :, part * LANES : (part + 1) * LANES
        ].reshape(chunks, ROWS, LANES)
    packed_ref[:, size // LANES * ROWS :, :] = jnp.broadcast_to(
        diagonal, (size, LANES)
    ).reshape(chunks, ROWS, LANES)


def overlap(core, arrived):
    rows, lanes = arrived.shape
    planes = 2 * ROWS
    size = rows // planes
    return pl.pallas_call(
        overlap_kernel,
        out_shape=(
            jax.ShapeDtypeStruct((planes, size, lanes), jnp.float32),
            jax.ShapeDtypeStruct((size // ROWS, (size // LANES + 1) * ROWS, LANES), jnp.float32),
        ),
        in_specs=[smem(), vmem()],
        out_specs=(vmem(), vmem()),
        compiler_params=pltpu.CompilerParams(vmem_limit_bytes=40 * 2**20),
        cost_estimate=pl.CostEstimate(
            flops=24 * 256 * 256 * 1024, bytes_accessed=4 * 2**20, transcendentals=0
        ),
        name="overlap",
    )(core, arrived)


def eliminate(work):
    size = work.shape[0]
    sub = lax.broadcasted_iota(jnp.int32, (ROWS, LANES), 0)

    def row_of(tile, j):
        return jnp.broadcast_to(tile[j : j + 1, :], tile.shape)

    for start in range(0, size, BLOCK):
        stop = start + BLOCK
        first = start // LANES * LANES
        last = size + (stop + LANES - 1) // LANES * LANES
        lanes = range(first, last, LANES)
        groups = BLOCK // ROWS
        tiles = [
            {c: work[start + g * ROWS : start + (g + 1) * ROWS, c : c + LANES] for c in lanes}
            for g in range(groups)
        ]
        for q in range(groups):
            base = start + q * ROWS
            home, at = base // LANES * LANES, base % LANES
            spread = [
                [
                    jnp.broadcast_to(tiles[g][home][:, at + m : at + m + 1], (ROWS, LANES))
                    for m in range(ROWS)
                ]
                if g >= q
                else None
                for g in range(groups)
            ]
            scales = jnp.ones((ROWS, LANES), jnp.float32)
            for j in range(ROWS):
                pivot = row_of(spread[q][j], j)
                root = lax.rsqrt(pivot)
                root = root * (1.5 - 0.5 * pivot * root * root)
                scales = jnp.where(sub == j, root, scales)
                weight = {}
                for g in range(q, groups):
                    weight[g] = spread[g][j] * root
                weight[q] = jnp.where(sub > j, weight[q], 0.0)
                for m in range(j + 1, ROWS):
                    top = row_of(spread[q][m], j) * root
                    for g in range(q, groups):
                        spread[g][m] = spread[g][m] - weight[g] * top
                for c in lanes:
                    top = row_of(tiles[q][c], j) * root
                    for g in range(q, groups):
                        tiles[g][c] = tiles[g][c] - weight[g] * top
            for c in lanes:
                tiles[q][c] = tiles[q][c] * scales
        for g in range(groups):
            for c in lanes:
                work[start + g * ROWS : start + (g + 1) * ROWS, c : c + LANES] = tiles[g][c]
        if stop < size:
            low = stop // LANES * LANES
            done = work[start:stop, :]
            update = lax.dot_general(
                done[:, low:size],
                done[:, low:last],
                (((0,), (0,)), ((), ())),
                precision=precise,
                preferred_element_type=jnp.float32,
            )
            work[stop:, low:last] = work[stop:, low:last] - update[stop - low :, :]


def solve_kernel(cells, summed_ref, natural_ref, flat_ref, subspace_ref, work, mixed):
    def dot(a, b):
        return jnp.dot(a, b, precision=precise, preferred_element_type=jnp.float32)

    size = work.shape[0]
    parts = size // LANES
    tiles = [
        summed_ref[:, part * ROWS : (part + 1) * ROWS, :].reshape(size, LANES)
        for part in range(parts + 1)
    ]
    packed = jnp.concatenate(tiles[:parts], axis=1) * (1.0 / cells)
    diagonal = jnp.concatenate(tiles[parts:] * parts, axis=1) * (1.0 / cells)
    row = lax.broadcasted_iota(jnp.int32, (size, size), 0)
    column = lax.broadcasted_iota(jnp.int32, (size, size), 1)
    turned = packed.T
    work[:, :size] = jnp.where(row <= column, packed, turned)
    work[:, size:] = jnp.where(row == column, 1.0, 0.0)
    hamilton = jnp.where(row > column, packed, jnp.where(row == column, diagonal, turned))
    eliminate(work)
    inverse = jnp.where(row >= column, work[:, size:], 0.0)
    subspace = transposed_dot(dot(inverse, hamilton), inverse)
    subspace_ref[...] = subspace
    planes = natural_ref.shape[0]
    half = planes // 2
    for plane in range(0, half, 2):
        both = [
            dot(
                inverse,
                jnp.concatenate([natural_ref[plane + k], natural_ref[half + plane + k]], axis=1),
            )
            for k in range(2)
        ]
        product = dot(subspace, jnp.concatenate([part[:, :LANES] for part in both], axis=1))
        for k, part in enumerate(both):
            mixed[plane + k] = part[:, :LANES]
            mixed[half + plane + k] = part[:, LANES:] - product[:, k * LANES : (k + 1) * LANES]
    natural_rows(flat_ref, mixed, 0, False)


def solve(summed, natural, cells):
    planes, size, lanes = natural.shape
    return pl.pallas_call(
        functools.partial(solve_kernel, cells),
        out_shape=(
            jax.ShapeDtypeStruct((planes * size, lanes), jnp.float32),
            jax.ShapeDtypeStruct((size, size), jnp.float32),
        ),
        in_specs=[vmem()] * 2,
        out_specs=(vmem(), vmem()),
        scratch_shapes=[
            pltpu.VMEM((size, 2 * size), jnp.float32),
            pltpu.VMEM(natural.shape, jnp.float32),
        ],
        compiler_params=pltpu.CompilerParams(vmem_limit_bytes=48 * 2**20),
        cost_estimate=pl.CostEstimate(
            flops=20_000_000_000, bytes_accessed=6 * 2**20, transcendentals=256
        ),
        name="solve",
    )(summed, natural)


def assemble_kernel(core_ref, arrived_ref, received_ref, first_ref, second_ref, sems):
    core = core_ref[0]
    blocks = received_ref.shape[0]
    copies = []
    for which, out_ref in enumerate((first_ref, second_ref)):
        rows = pl.ds(which * ROWS, ROWS)
        copies.append(
            pltpu.make_async_copy(
                arrived_ref.at[:, pl.ds((core * 2 + which) * ROWS, ROWS)],
                out_ref.at[pl.ds(core * blocks, blocks)],
                sems.at[2 * which],
            )
        )
        copies.append(
            pltpu.make_async_copy(
                received_ref.at[:, rows],
                out_ref.at[pl.ds((1 - core) * blocks, blocks)],
                sems.at[2 * which + 1],
            )
        )
    for copy in copies:
        copy.start()
    for copy in copies:
        copy.wait()


def assemble(core, arrived, received):
    blocks, _, lanes = received.shape
    out = jax.ShapeDtypeStruct((CORES * blocks, ROWS, lanes), jnp.float32)
    anywhere = pl.BlockSpec(memory_space=pl.ANY)
    return pl.pallas_call(
        assemble_kernel,
        out_shape=(out, out),
        in_specs=[smem(), anywhere, anywhere],
        out_specs=(anywhere, anywhere),
        scratch_shapes=[pltpu.SemaphoreType.DMA((4,))],
        cost_estimate=pl.CostEstimate(flops=0, bytes_accessed=4 * 2**20, transcendentals=0),
        name="assemble",
    )(core, arrived, received)


def exchange(blocks, groups, axes=AXES):
    return lax.all_to_all(
        blocks, axes, split_axis=0, concat_axis=0, tiled=True, axis_index_groups=groups
    )


class Layout:
    def __init__(self, orb, grp):
        self.x, self.core, self.y = 4, CORES, grp
        self.z = orb // (self.x * self.core)
        self.total = orb * grp

    def orb(self, z, x, core):
        return ((z % self.z) * self.x + x % self.x) * self.core + core % self.core

    def device(self, z, x, core, y):
        return self.orb(z, x, core) * self.y + y

    def places(self):
        return [
            (z, x, core)
            for z in range(self.z)
            for x in range(self.x)
            for core in range(self.core)
        ]

    def chips(self):
        return [
            [
                self.device(z, x, core, y)
                for z in range(self.z)
                for x in range(self.x)
                for y in range(self.y)
            ]
            for core in range(self.core)
        ]

    def planes(self):
        return [
            [
                self.device(z, x, core, y)
                for x in range(self.x)
                for core in range(self.core)
                for y in range(self.y)
            ]
            for z in range(self.z)
        ]

    def columns(self):
        return [
            [self.orb(z, x, core) for z in range(self.z)]
            for x in range(self.x)
            for core in range(self.core)
        ]

    def swap_cores(self, values):
        pairs = [(self.orb(z, x, c), self.orb(z, x, c + 1)) for z, x, c in self.places()]
        return lax.ppermute(values, "orb", pairs)


def reduce_slab(partial, layout):
    me = lax.axis_index("orb")
    core = me % layout.core
    x = me // layout.core % layout.x
    z = me // (layout.core * layout.x)
    y = lax.axis_index("grp")

    def stage(values, dim, count, index, axis, pairs):
        total = lax.dynamic_index_in_dim(values, index, dim, keepdims=False)
        arrived = [
            lax.ppermute(
                lax.dynamic_index_in_dim(values, (index + k) % count, dim, keepdims=False),
                axis,
                pairs(k),
            )
            for k in range(1, count)
        ]
        for term in arrived:
            total = total + term
        return total

    def along(dz, dx, dc):
        return lambda k: [
            (layout.orb(a, b, c), layout.orb(a + dz * k, b + dx * k, c + dc * k))
            for a, b, c in layout.places()
        ]

    def lines(k):
        return [(i, (i + k) % layout.y) for i in range(layout.y)]

    values = partial.reshape(layout.z, layout.x, layout.core, layout.y, -1, LANES)
    values = stage(values, 2, layout.core, core, "orb", along(0, 0, 1))
    values = stage(values, 2, layout.y, y, "grp", lines)
    values = stage(values, 1, layout.x, x, "orb", along(0, 1, 0))
    return stage(values, 0, layout.z, z, "orb", along(1, 0, 0))


def sum_everywhere(chunks, layout):
    count, rows, lanes = chunks.shape

    def spread(values, copies):
        return jnp.broadcast_to(jnp.sum(values, axis=0, keepdims=True), (copies, rows, lanes))

    part = spread(exchange(chunks, layout.planes()), layout.z)
    part = spread(exchange(part, layout.columns(), "orb"), count)
    return exchange(part, layout.planes())


def on_device(layout, orbitals, potential, occupation, region_bounds):
    cell_total = orbitals.shape[1]
    orb, grp = lax.axis_index("orb"), lax.axis_index("grp")
    position = orb * layout.y + grp
    core = orb % layout.core
    place = jnp.stack([position, core]).astype(jnp.int32)
    core = core.reshape(1).astype(jnp.int32)
    keep, give, density_part = apply_hamiltonian(
        place, region_bounds, occupation, orbitals.reshape(G, PAIRS, LANES), potential
    )
    sent = jnp.concatenate([keep, layout.swap_cores(give)], axis=1)
    density = reduce_slab(density_part, layout)
    arrived = exchange(sent, layout.chips())
    arrived, density = lax.optimization_barrier((arrived, density))
    natural, packed = overlap(core, arrived.reshape(-1, LANES))
    summed = sum_everywhere(packed, layout)
    mixed, subspace = solve(summed, natural, cell_total)
    back = exchange(mixed.reshape(-1, 4 * ROWS, LANES), layout.chips())
    other = lax.dynamic_slice_in_dim(back, (1 - core[0]) * 2 * ROWS, 2 * ROWS, 1)
    orthonormal, gradient = assemble(core, back, layout.swap_cores(other))
    return (
        orthonormal.reshape(1, cell_total),
        gradient.reshape(1, cell_total),
        subspace,
        density.reshape(-1, G),
    )


def solution(mesh):
    in_specs = (P(AXES, None), P(), P(), P())
    out_specs = (P(AXES, None), P(AXES, None), P(), P(AXES, None))
    step = functools.partial(on_device, Layout(mesh.shape["orb"], mesh.shape["grp"]))
    return jax.shard_map(
        step, mesh=mesh, in_specs=in_specs, out_specs=out_specs, check_vma=False
    )
```

profile of v0, /device:TPU:1, one launch (start us, length us, event | category | flops | bytes accessed | tf_op | source)
XLA Modules:
  0.0 288.2 jit_solution(1240573790810712893)
XLA Ops:
  0.7 1.9 copy.20.potential_ref
  6.9 9.7 %hamiltonian.1 = (f32[128,16,128]{2,1,0:T(8,128)S(1)}, f32[128,16,128]{2,1,0:T(8,128)S(1)}, f32[64,32,128]{2,1,0:T(8,128)S(1)}) custom-call(s32[2]{0:T(128)S(1)} %pad_add_fusion.place_ref, s32[256,2]{1,0:T(8,128)S(1)} %copy.19.bounds_ref, f32[256]{0:T(256)S(1)} %copy-done.1, f32[64,32,128]{2,1,0:T(8,128)S(1)} %bitcast.69, ...), custom_call_target="tpu_custom_call" | custom-call | flops 3019898880 | bytes 5242880 | tf_op jit(solution)/shard_map/hamiltonian/pallas_call | solution.py:199
  16.6 3.3 %collective-permute-start = (f32[128,16,128]{2,1,0:T(8,128)S(1)}, f32[128,16,128]{2,1,0:T(8,128)S(1)}, u32[]{:S(2)}, u32[]{:S(2)}) collective-permute-start(f32[128,16,128]{2,1,0:T(8,128)S(1)} %get-tuple-element.16), channel_id=1, source_target_pairs={{0,4},{4,0},{8,12},{12,8},{16,20},{20,16},{24,28},{28,24},{32,36},... | collective-permute-start | bytes 3145736 | tf_op jit(solution)/shard_map/ppermute | solution.py:528
  19.9 2.3 collective-permute-done
  23.9 13.8 %all-to-all-start = ((f32[128,32,128]{2,1,0:T(8,128)}), f32[128,32,128]{2,1,0:T(8,128)S(1)}, u32[]{:S(2)}, u32[]{:S(2)}) async-start(f32[128,32,128]{2,1,0:T(8,128)} %pad_maximum_fusion), calls=%async_computation | async-start | bytes 4194304 | tf_op jit(solution)/shard_map/all_to_all | solution.py:472
  43.0 2.4 collective-permute-start.3
  46.6 3.4 %collective-permute-done.2 = f32[8,4,8,128]{3,2,1,0:T(8,128)S(1)} collective-permute-done((f32[8,4,8,128]{3,2,1,0:T(8,128)S(1)}, f32[8,4,8,128]{3,2,1,0:T(8,128)S(1)}, u32[]{:S(2)}, u32[]{:S(2)}) %collective-permute-start.2) | collective-permute-done | bytes 131104 | tf_op jit(solution)/shard_map/ppermute | solution.py:541
  50.0 5.4 %collective-permute-done.3 = f32[8,4,8,128]{3,2,1,0:T(8,128)S(1)} collective-permute-done((f32[8,4,8,128]{3,2,1,0:T(8,128)S(1)}, f32[8,4,8,128]{3,2,1,0:T(8,128)S(1)}, u32[]{:S(2)}, u32[]{:S(2)}) %collective-permute-start.3) | collective-permute-done | bytes 131104 | tf_op jit(solution)/shard_map/ppermute | solution.py:541
  57.2 1.7 collective-permute-start.6
  62.7 4.1 %collective-permute-start.10 = (f32[8,128]{1,0:T(8,128)S(1)}, f32[8,128]{1,0:T(8,128)S(1)}, u32[]{:S(2)}, u32[]{:S(2)}) collective-permute-start(f32[8,128]{1,0:T(8,128)S(1)} %get-tuple-element.39), channel_id=1, source_target_pairs={{0,96},{4,100},{8,104},{12,108},{16,112},{20,116},{24,120},{28,124... | collective-permute-start | bytes 12296 | tf_op jit(solution)/shard_map/ppermute | solution.py:541
  66.8 3.5 %collective-permute-start.11 = (f32[8,128]{1,0:T(8,128)S(1)}, f32[8,128]{1,0:T(8,128)S(1)}, u32[]{:S(2)}, u32[]{:S(2)}) collective-permute-start(f32[8,128]{1,0:T(8,128)S(1)} %get-tuple-element.38), channel_id=1, source_target_pairs={{0,128},{4,132},{8,136},{12,140},{16,144},{20,148},{24,152},{28,15... | collective-permute-start | bytes 12296 | tf_op jit(solution)/shard_map/ppermute | solution.py:541
  70.3 3.1 %collective-permute-start.12 = (f32[8,128]{1,0:T(8,128)S(1)}, f32[8,128]{1,0:T(8,128)S(1)}, u32[]{:S(2)}, u32[]{:S(2)}) collective-permute-start(f32[8,128]{1,0:T(8,128)S(1)} %get-tuple-element.37), channel_id=1, source_target_pairs={{0,160},{4,164},{8,168},{12,172},{16,176},{20,180},{24,184},{28,18... | collective-permute-start | bytes 12296 | tf_op jit(solution)/shard_map/ppermute | solution.py:541
  74.7 9.7 %collective-permute-done.10 = f32[8,128]{1,0:T(8,128)S(1)} collective-permute-done((f32[8,128]{1,0:T(8,128)S(1)}, f32[8,128]{1,0:T(8,128)S(1)}, u32[]{:S(2)}, u32[]{:S(2)}) %collective-permute-start.10) | collective-permute-done | bytes 4128 | tf_op jit(solution)/shard_map/ppermute | solution.py:541
  88.5 3.1 %collective-permute-done.9 = f32[8,128]{1,0:T(8,128)S(1)} collective-permute-done((f32[8,128]{1,0:T(8,128)S(1)}, f32[8,128]{1,0:T(8,128)S(1)}, u32[]{:S(2)}, u32[]{:S(2)}) %collective-permute-start.9) | collective-permute-done | bytes 4128 | tf_op jit(solution)/shard_map/ppermute | solution.py:541
  91.6 3.3 %overlap.1 = (f32[16,256,128]{2,1,0:T(8,128)S(1)}, f32[32,24,128]{2,1,0:T(8,128)S(1)}) custom-call(s32[1]{0:T(128)} %bitcast.core_ref, f32[4096,128]{1,0:T(8,128)S(1)} %bitcast.67), custom_call_target="tpu_custom_call" | custom-call | flops 1610612736 | bytes 4194304 | tf_op jit(solution)/shard_map/overlap/pallas_call | solution.py:288
  96.3 19.7 %all_to_all.25 = f32[32,24,128]{2,1,0:T(8,128)S(1)} all-to-all(f32[32,24,128]{2,1,0:T(8,128)S(1)} %get-tuple-element.19), channel_id=1, replica_groups={{0,1,2,3,4,5,6,7,8,9,10,11,12,13,14,15,16,17,18,19,20,21,22,23,24,25,26..., dimensions={0} | all-to-all | bytes 786432 | tf_op jit(solution)/shard_map/all_to_all | solution.py:472
  116.0 10.3 %all_to_all.26 = f32[8,24,128]{2,1,0:T(8,128)S(1)} all-to-all(f32[8,24,128]{2,1,0:T(8,128)S(1)} %broadcast_in_dim.4), channel_id=1, replica_groups={{0,32,64,96,128,160,192,224},{4,36,68,100,132,164,196,228},{8,40,72,104..., dimensions={0} | all-to-all | bytes 196608 | tf_op jit(solution)/shard_map/all_to_all | solution.py:472
  126.3 15.4 %all_to_all.27.summed_ref = f32[32,24,128]{2,1,0:T(8,128)S(1)} all-to-all(f32[32,24,128]{2,1,0:T(8,128)S(1)} %broadcast_in_dim.5), channel_id=1, replica_groups={{0,1,2,3,4,5,6,7,8,9,10,11,12,13,14,15,16,17,18,19,20,21,22,23,24,25,26..., dimensions={0} | all-to-all | bytes 786432 | tf_op jit(solution)/shard_map/all_to_all | solution.py:472
  141.7 18.8 %solve.1 = (f32[4096,128]{1,0:T(8,128)}, f32[256,256]{1,0:T(8,128)}) custom-call(f32[32,24,128]{2,1,0:T(8,128)S(1)} %all_to_all.27.summed_ref, f32[16,256,128]{2,1,0:T(8,128)S(1)} %copy-done.7), custom_call_target="tpu_custom_call" | custom-call | flops 20000000000 | bytes 6291456 | tf_op jit(solution)/shard_map/solve/pallas_call | solution.py:410
  160.5 6.2 %all-to-all-start.4 = ((f32[128,32,128]{2,1,0:T(8,128)}), f32[128,32,128]{2,1,0:T(8,128)S(1)}, u32[]{:S(2)}, u32[]{:S(2)}) async-start(f32[128,32,128]{2,1,0:T(8,128)} %bitcast.23), calls=%async_computation.4 | async-start | bytes 4194304 | tf_op jit(solution)/shard_map/all_to_all | solution.py:472
  166.7 49.8 %all-to-all-done.4.arrived_ref = f32[128,32,128]{2,1,0:T(8,128)S(1)} async-done(((f32[128,32,128]{2,1,0:T(8,128)}), f32[128,32,128]{2,1,0:T(8,128)S(1)}, u32[]{:S(2)}, u32[]{:S(2)}) %all-to-all-start.4) | async-done | bytes 2097184 | tf_op jit(solution)/shard_map/all_to_all | solution.py:472
  216.6 4.3 %collective-permute-start.15 = (f32[128,16,128]{2,1,0:T(8,128)S(1)}, f32[128,16,128]{2,1,0:T(8,128)}, u32[]{:S(2)}, u32[]{:S(2)}) collective-permute-start(f32[128,16,128]{2,1,0:T(8,128)S(1)} %constant_dynamic-slice_fusion), channel_id=1, source_target_pairs={{0,4},{4,0},{8,12},{12,8},{16,20},{20,16},{24,28},{28,24},{32,36},... | collective-permute-start | bytes 3145736 | tf_op jit(solution)/shard_map/ppermute | solution.py:528
  221.6 1.8 collective-permute-done.15.received_ref
  223.4 64.7 %assemble.1 = (f32[256,8,128]{2,1,0:T(8,128)}, f32[256,8,128]{2,1,0:T(8,128)}) custom-call(s32[1]{0:T(128)} %bitcast.core_ref, f32[128,32,128]{2,1,0:T(8,128)} %copy-done.8, f32[128,16,128]{2,1,0:T(8,128)} %collective-permute-done.15.received_ref), custom_call_target="tpu_custom_call" | custom-call | bytes 4194304 | tf_op jit(solution)/shard_map/assemble/pallas_call | solution.py:460
  (58 shorter events, 25.5 us)
Async XLA Ops:
  0.6 2.2 copy-start.4
  0.6 1.9 copy-start.9
  0.7 2.1 copy-start.1
  16.6 5.6 %collective-permute-start = (f32[128,16,128]{2,1,0:T(8,128)S(1)}, f32[128,16,128]{2,1,0:T(8,128)S(1)}, u32[]{:S(2)}, u32[]{:S(2)}) collective-permute-start(f32[128,16,128]{2,1,0:T(8,128)S(1)} %get-tuple-element.16), channel_id=1, source_target_pairs={{0,4},{4,0},{8,12},{12,8},{16,20},{20,16},{24,28},{28,24},{32,36},... | collective-permute-start | bytes 3145736 | tf_op jit(solution)/shard_map/ppermute | solution.py:528
  23.9 67.7 %all-to-all-start = ((f32[128,32,128]{2,1,0:T(8,128)}), f32[128,32,128]{2,1,0:T(8,128)S(1)}, u32[]{:S(2)}, u32[]{:S(2)}) async-start(f32[128,32,128]{2,1,0:T(8,128)} %pad_maximum_fusion), calls=%async_computation | async-start | bytes 4194304 | tf_op jit(solution)/shard_map/all_to_all | solution.py:472
  38.7 2.3 collective-permute-start.1
  42.1 7.9 %collective-permute-start.2 = (f32[8,4,8,128]{3,2,1,0:T(8,128)S(1)}, f32[8,4,8,128]{3,2,1,0:T(8,128)S(1)}, u32[]{:S(2)}, u32[]{:S(2)}) collective-permute-start(f32[8,4,8,128]{3,2,1,0:T(8,128)S(1)} %get-tuple-element.28), channel_id=1, source_target_pairs={{0,1},{1,2},{2,3},{3,0},{4,5},{5,6},{6,7},{7,4},{8,9},{9,10},{10,1... | collective-permute-start | bytes 393224 | tf_op jit(solution)/shard_map/ppermute | solution.py:541
  43.0 12.4 %collective-permute-start.3 = (f32[8,4,8,128]{3,2,1,0:T(8,128)S(1)}, f32[8,4,8,128]{3,2,1,0:T(8,128)S(1)}, u32[]{:S(2)}, u32[]{:S(2)}) collective-permute-start(f32[8,4,8,128]{3,2,1,0:T(8,128)S(1)} %get-tuple-element.30), channel_id=1, source_target_pairs={{0,2},{1,3},{2,0},{3,1},{4,6},{5,7},{6,4},{7,5},{8,10},{9,11},{10,... | collective-permute-start | bytes 393224 | tf_op jit(solution)/shard_map/ppermute | solution.py:541
  45.4 11.6 %collective-permute-start.4 = (f32[8,4,8,128]{3,2,1,0:T(8,128)S(1)}, f32[8,4,8,128]{3,2,1,0:T(8,128)S(1)}, u32[]{:S(2)}, u32[]{:S(2)}) collective-permute-start(f32[8,4,8,128]{3,2,1,0:T(8,128)S(1)} %get-tuple-element.29), channel_id=1, source_target_pairs={{0,3},{1,0},{2,1},{3,2},{4,7},{5,4},{6,5},{7,6},{8,11},{9,8},{10,9... | collective-permute-start | bytes 393224 | tf_op jit(solution)/shard_map/ppermute | solution.py:541
  57.1 4.4 %collective-permute-start.5 = (f32[8,8,128]{2,1,0:T(8,128)S(1)}, f32[8,8,128]{2,1,0:T(8,128)S(1)}, u32[]{:S(2)}, u32[]{:S(2)}) collective-permute-start(f32[8,8,128]{2,1,0:T(8,128)S(1)} %get-tuple-element.31), channel_id=1, source_target_pairs={{0,8},{4,12},{8,16},{12,20},{16,24},{20,28},{24,0},{28,4},{32,40},... | collective-permute-start | bytes 98312 | tf_op jit(solution)/shard_map/ppermute | solution.py:541
  57.2 5.1 %collective-permute-start.6 = (f32[8,8,128]{2,1,0:T(8,128)S(1)}, f32[8,8,128]{2,1,0:T(8,128)S(1)}, u32[]{:S(2)}, u32[]{:S(2)}) collective-permute-start(f32[8,8,128]{2,1,0:T(8,128)S(1)} %get-tuple-element.33), channel_id=1, source_target_pairs={{0,16},{4,20},{8,24},{12,28},{16,0},{20,4},{24,8},{28,12},{32,48},... | collective-permute-start | bytes 98312 | tf_op jit(solution)/shard_map/ppermute | solution.py:541
  58.9 3.7 %collective-permute-start.7 = (f32[8,8,128]{2,1,0:T(8,128)S(1)}, f32[8,8,128]{2,1,0:T(8,128)S(1)}, u32[]{:S(2)}, u32[]{:S(2)}) collective-permute-start(f32[8,8,128]{2,1,0:T(8,128)S(1)} %get-tuple-element.32), channel_id=1, source_target_pairs={{0,24},{4,28},{8,0},{12,4},{16,8},{20,12},{24,16},{28,20},{32,56},... | collective-permute-start | bytes 98312 | tf_op jit(solution)/shard_map/ppermute | solution.py:541
  62.7 21.8 %collective-permute-start.10 = (f32[8,128]{1,0:T(8,128)S(1)}, f32[8,128]{1,0:T(8,128)S(1)}, u32[]{:S(2)}, u32[]{:S(2)}) collective-permute-start(f32[8,128]{1,0:T(8,128)S(1)} %get-tuple-element.39), channel_id=1, source_target_pairs={{0,96},{4,100},{8,104},{12,108},{16,112},{20,116},{24,120},{28,124... | collective-permute-start | bytes 12296 | tf_op jit(solution)/shard_map/ppermute | solution.py:541
  66.8 20.2 %collective-permute-start.11 = (f32[8,128]{1,0:T(8,128)S(1)}, f32[8,128]{1,0:T(8,128)S(1)}, u32[]{:S(2)}, u32[]{:S(2)}) collective-permute-start(f32[8,128]{1,0:T(8,128)S(1)} %get-tuple-element.38), channel_id=1, source_target_pairs={{0,128},{4,132},{8,136},{12,140},{16,144},{20,148},{24,152},{28,15... | collective-permute-start | bytes 12296 | tf_op jit(solution)/shard_map/ppermute | solution.py:541
  70.3 16.7 %collective-permute-start.12 = (f32[8,128]{1,0:T(8,128)S(1)}, f32[8,128]{1,0:T(8,128)S(1)}, u32[]{:S(2)}, u32[]{:S(2)}) collective-permute-start(f32[8,128]{1,0:T(8,128)S(1)} %get-tuple-element.37), channel_id=1, source_target_pairs={{0,160},{4,164},{8,168},{12,172},{16,176},{20,180},{24,184},{28,18... | collective-permute-start | bytes 12296 | tf_op jit(solution)/shard_map/ppermute | solution.py:541
  73.5 13.5 %collective-permute-start.13 = (f32[8,128]{1,0:T(8,128)S(1)}, f32[8,128]{1,0:T(8,128)S(1)}, u32[]{:S(2)}, u32[]{:S(2)}) collective-permute-start(f32[8,128]{1,0:T(8,128)S(1)} %get-tuple-element.36), channel_id=1, source_target_pairs={{0,192},{4,196},{8,200},{12,204},{16,208},{20,212},{24,216},{28,22... | collective-permute-start | bytes 12296 | tf_op jit(solution)/shard_map/ppermute | solution.py:541
  73.9 13.1 %collective-permute-start.14 = (f32[8,128]{1,0:T(8,128)S(1)}, f32[8,128]{1,0:T(8,128)S(1)}, u32[]{:S(2)}, u32[]{:S(2)}) collective-permute-start(f32[8,128]{1,0:T(8,128)S(1)} %get-tuple-element.35), channel_id=1, source_target_pairs={{0,224},{4,228},{8,232},{12,236},{16,240},{20,244},{24,248},{28,25... | collective-permute-start | bytes 12296 | tf_op jit(solution)/shard_map/ppermute | solution.py:541
  84.4 4.0 %collective-permute-start.8 = (f32[8,128]{1,0:T(8,128)S(1)}, f32[8,128]{1,0:T(8,128)S(1)}, u32[]{:S(2)}, u32[]{:S(2)}) collective-permute-start(f32[8,128]{1,0:T(8,128)S(1)} %get-tuple-element.34), channel_id=1, source_target_pairs={{0,32},{4,36},{8,40},{12,44},{16,48},{20,52},{24,56},{28,60},{32,6... | collective-permute-start | bytes 12296 | tf_op jit(solution)/shard_map/ppermute | solution.py:541
  87.0 4.6 %collective-permute-start.9 = (f32[8,128]{1,0:T(8,128)S(1)}, f32[8,128]{1,0:T(8,128)S(1)}, u32[]{:S(2)}, u32[]{:S(2)}) collective-permute-start(f32[8,128]{1,0:T(8,128)S(1)} %get-tuple-element.40), channel_id=1, source_target_pairs={{0,64},{4,68},{8,72},{12,76},{16,80},{20,84},{24,88},{28,92},{32,9... | collective-permute-start | bytes 12296 | tf_op jit(solution)/shard_map/ppermute | solution.py:541
  94.9 1.4 copy-start.6
  96.3 45.4 %copy-start.7 = (f32[16,256,128]{2,1,0:T(8,128)S(1)}, f32[16,256,128]{2,1,0:T(8,128)}, u32[]{:S(2)}) copy-start(f32[16,256,128]{2,1,0:T(8,128)} %copy-done.6) | copy-start | bytes 6291460
  160.5 56.0 %all-to-all-start.4 = ((f32[128,32,128]{2,1,0:T(8,128)}), f32[128,32,128]{2,1,0:T(8,128)S(1)}, u32[]{:S(2)}, u32[]{:S(2)}) async-start(f32[128,32,128]{2,1,0:T(8,128)} %bitcast.23), calls=%async_computation.4 | async-start | bytes 4194304 | tf_op jit(solution)/shard_map/all_to_all | solution.py:472
  216.5 6.9 %copy-start.8 = (f32[128,32,128]{2,1,0:T(8,128)}, f32[128,32,128]{2,1,0:T(8,128)S(1)}, u32[]{:S(2)}) copy-start(f32[128,32,128]{2,1,0:T(8,128)S(1)} %all-to-all-done.4.arrived_ref) | copy-start | bytes 6291460
  216.6 6.8 %collective-permute-start.15 = (f32[128,16,128]{2,1,0:T(8,128)S(1)}, f32[128,16,128]{2,1,0:T(8,128)}, u32[]{:S(2)}, u32[]{:S(2)}) collective-permute-start(f32[128,16,128]{2,1,0:T(8,128)S(1)} %constant_dynamic-slice_fusion), channel_id=1, source_target_pairs={{0,4},{4,0},{8,12},{12,8},{16,20},{20,16},{24,28},{28,24},{32,36},... | collective-permute-start | bytes 3145736 | tf_op jit(solution)/shard_map/ppermute | solution.py:528
  (4 other events, 4.1 us)
where the time goes:
time: 289 us; the launch traced here: 288 us
  Pallas kernels  96.5 us (33%)
  waiting for transfers between devices  84.3 us (29%)
  starting transfers between devices  48.8 us (17%)
  blocking collectives  45.3 us (16%)
  local copies, waits for them, and re-layouts  9.31 us (3%)
  other arithmetic  2.97 us (1%)
    pallas_call x1, Pallas kernels, assemble(): pl.pallas_call(assemble_kernel, out_shape=(out, out), in_specs=[smem(), a...  64.7 us
    all_to_all x2, waiting for transfers between devices, exchange(): lax.all_to_all(blocks, axes, split_axis=0, concat_axis=0, tiled=True, axi...  49.8 us
    all_to_all x3, blocking collectives, exchange(): lax.all_to_all(blocks, axes, split_axis=0, concat_axis=0, tiled=True, axi...  45.3 us
    ppermute x14, waiting for transfers between devices, stage(): lax.ppermute(lax.dynamic_index_in_dim(values, (index + k) % count, dim, k...  30.5 us
    ppermute x14, starting transfers between devices, stage(): lax.ppermute(lax.dynamic_index_in_dim(values, (index + k) % count, dim, k...  21.1 us
    all_to_all x2, starting transfers between devices, exchange(): lax.all_to_all(blocks, axes, split_axis=0, concat_axis=0, tiled=True, axi...  20 us
    pallas_call x1, Pallas kernels, solve(): pl.pallas_call(functools.partial(solve_kernel, cells), out_shape=(jax.Sha...  18.8 us
    pallas_call x1, Pallas kernels, apply_hamiltonian(): pl.pallas_call(hamiltonian_kernel, out_shape=(side, side, grid), in_specs...  9.73 us
  transfers between devices with their start and end apart: 18, of which 14 were waited for; matrix products, arithmetic and copies ran while one was open for 1% of the time, Pallas kernels for 0%

commit v1 on v0

--- a/solution.py
+++ b/solution.py
@@ -427,28 +427,23 @@
     )(summed, natural)
 
 
-def assemble_kernel(core_ref, arrived_ref, received_ref, first_ref, second_ref, sems):
+def assemble_kernel(core_ref, arrived_ref, received_ref, first_ref, second_ref, staged, sems):
     core = core_ref[0]
     blocks = received_ref.shape[0]
     copies = []
     for which, out_ref in enumerate((first_ref, second_ref)):
-        rows = pl.ds(which * ROWS, ROWS)
-        copies.append(
-            pltpu.make_async_copy(
-                arrived_ref.at[:, pl.ds((core * 2 + which) * ROWS, ROWS)],
-                out_ref.at[pl.ds(core * blocks, blocks)],
-                sems.at[2 * which],
+        for own in range(2):
+            slot = 2 * which + own
+            if own:
+                staged[slot] = arrived_ref[:, pl.ds((core * 2 + which) * ROWS, ROWS), :]
+            else:
+                staged[slot] = received_ref[:, which * ROWS : (which + 1) * ROWS, :]
+            side = core if own else 1 - core
+            copy = pltpu.make_async_copy(
+                staged.at[slot], out_ref.at[pl.ds(side * blocks, blocks)], sems.at[slot]
             )
-        )
-        copies.append(
-            pltpu.make_async_copy(
-                received_ref.at[:, rows],
-                out_ref.at[pl.ds((1 - core) * blocks, blocks)],
-                sems.at[2 * which + 1],
-            )
-        )
-    for copy in copies:
-        copy.start()
+            copy.start()
+            copies.append(copy)
     for copy in copies:
         copy.wait()
 
@@ -460,9 +455,13 @@
     return pl.pallas_call(
         assemble_kernel,
         out_shape=(out, out),
-        in_specs=[smem(), anywhere, anywhere],
+        in_specs=[smem(), vmem(), vmem()],
         out_specs=(anywhere, anywhere),
-        scratch_shapes=[pltpu.SemaphoreType.DMA((4,))],
+        scratch_shapes=[
+            pltpu.VMEM((4, blocks, ROWS, lanes), jnp.float32),
+            pltpu.SemaphoreType.DMA((4,)),
+        ],
+        compiler_params=pltpu.CompilerParams(vmem_limit_bytes=32 * 2**20),
         cost_estimate=pl.CostEstimate(flops=0, bytes_accessed=4 * 2**20, transcendentals=0),
         name="assemble",
     )(core, arrived, received)
@@ -562,7 +561,7 @@
     values = stage(values, 2, layout.core, core, "orb", along(0, 0, 1))
     values = stage(values, 2, layout.y, y, "grp", lines)
     values = stage(values, 1, layout.x, x, "orb", along(0, 1, 0))
-    return stage(values, 0, layout.z, z, "orb", along(1, 0, 0))
+    return values, lambda values: stage(values, 0, layout.z, z, "orb", along(1, 0, 0))
 
 
 def sum_everywhere(chunks, layout):
@@ -587,12 +586,14 @@
         place, region_bounds, occupation, orbitals.reshape(G, PAIRS, LANES), potential
     )
     sent = jnp.concatenate([keep, layout.swap_cores(give)], axis=1)
-    density = reduce_slab(density_part, layout)
+    plane_density, along_z = reduce_slab(density_part, layout)
     arrived = exchange(sent, layout.chips())
-    arrived, density = lax.optimization_barrier((arrived, density))
+    arrived, plane_density = lax.optimization_barrier((arrived, plane_density))
     natural, packed = overlap(core, arrived.reshape(-1, LANES))
     summed = sum_everywhere(packed, layout)
     mixed, subspace = solve(summed, natural, cell_total)
+    mixed, plane_density = lax.optimization_barrier((mixed, plane_density))
+    density = along_z(plane_density)
     back = exchange(mixed.reshape(-1, 4 * ROWS, LANES), layout.chips())
     other = lax.dynamic_slice_in_dim(back, (1 - core[0]) * 2 * ROWS, 2 * ROWS, 1)
     orthonormal, gradient = assemble(core, back, layout.swap_cores(other))

time: 289 us -> 234 us (0.81)
  Pallas kernels: 96.5 us -> 31.7 us
  waiting for transfers between devices: 84.3 us -> 96.2 us
  starting transfers between devices: 48.8 us -> 45.5 us
  local copies, waits for them, and re-layouts: 9.31 us -> 12.3 us
    pallas_call x1, Pallas kernels: 64.7 us -> 1.38 us  [assemble(): pl.pallas_call(assemble_kernel, out_shape=(out, out), in_specs=[smem(), v...]
    all_to_all x2, waiting for transfers between devices: 49.8 us -> 74.1 us  [exchange(): lax.all_to_all(blocks, axes, split_axis=0, concat_axis=0, tiled=True, axi...]
    ppermute x14, waiting for transfers between devices: 30.5 us -> 19.8 us  [stage(): lax.ppermute(lax.dynamic_index_in_dim(values, (index + k) % count, dim, k...]
    ppermute x14, starting transfers between devices: 21.1 us -> 17.8 us  [stage(): lax.ppermute(lax.dynamic_index_in_dim(values, (index + k) % count, dim, k...]
    unnamed x22 -> x20, local copies, waits for them, and re-layouts: 7.48 us -> 9.47 us
  transfers between devices with their start and end apart: 18 -> 18, of which waited for: 14 -> 12; matrix products, arithmetic and copies ran while one was open for 1% -> 1% of each run, Pallas kernels for 0% -> 0%
where the time goes in v1:
time: 234 us; the launch traced here: 233 us
  waiting for transfers between devices  96.2 us (41%)
  starting transfers between devices  45.5 us (19%)
  blocking collectives  43.2 us (18%)
  Pallas kernels  31.7 us (14%)
  local copies, waits for them, and re-layouts  12.3 us (5%)
  other arithmetic  2.96 us (1%)
    all_to_all x2, waiting for transfers between devices, exchange(): lax.all_to_all(blocks, axes, split_axis=0, concat_axis=0, tiled=True, axi...  74.1 us
    all_to_all x3, blocking collectives, exchange(): lax.all_to_all(blocks, axes, split_axis=0, concat_axis=0, tiled=True, axi...  43.2 us
    all_to_all x2, starting transfers between devices, exchange(): lax.all_to_all(blocks, axes, split_axis=0, concat_axis=0, tiled=True, axi...  20.2 us
    ppermute x14, waiting for transfers between devices, stage(): lax.ppermute(lax.dynamic_index_in_dim(values, (index + k) % count, dim, k...  19.8 us
    ppermute x14, starting transfers between devices, stage(): lax.ppermute(lax.dynamic_index_in_dim(values, (index + k) % count, dim, k...  17.8 us
    pallas_call x1, Pallas kernels, solve(): pl.pallas_call(functools.partial(solve_kernel, cells), out_shape=(jax.Sha...  17.5 us
    pallas_call x1, Pallas kernels, apply_hamiltonian(): pl.pallas_call(hamiltonian_kernel, out_shape=(side, side, grid), in_specs...  9.59 us
    unnamed x20, local copies, waits for them, and re-layouts  9.47 us
  transfers between devices with their start and end apart: 18, of which 12 were waited for; matrix products, arithmetic and copies ran while one was open for 1% of the time, Pallas kernels for 0%

profile of v1, /device:TPU:1, one launch (start us, length us, event | category | flops | bytes accessed | tf_op | source)
XLA Modules:
  0.0 232.8 jit_solution(8239978229621782615)
XLA Ops:
  1.5 1.8 copy.20.potential_ref
  7.5 9.6 %hamiltonian.1 = (f32[128,16,128]{2,1,0:T(8,128)S(1)}, f32[128,16,128]{2,1,0:T(8,128)S(1)}, f32[64,32,128]{2,1,0:T(8,128)S(1)}) custom-call(s32[2]{0:T(128)S(1)} %pad_add_fusion.place_ref, s32[256,2]{1,0:T(8,128)S(1)} %copy.19.bounds_ref, f32[256]{0:T(256)S(1)} %copy-done.2, f32[64,32,128]{2,1,0:T(8,128)S(1)} %bitcast.70, ...), custom_call_target="tpu_custom_call" | custom-call | flops 3019898880 | bytes 5242880 | tf_op jit(solution)/shard_map/hamiltonian/pallas_call | solution.py:199
  17.1 3.3 %collective-permute-start = (f32[128,16,128]{2,1,0:T(8,128)S(1)}, f32[128,16,128]{2,1,0:T(8,128)S(1)}, u32[]{:S(2)}, u32[]{:S(2)}) collective-permute-start(f32[128,16,128]{2,1,0:T(8,128)S(1)} %get-tuple-element.18), channel_id=1, source_target_pairs={{0,4},{4,0},{8,12},{12,8},{16,20},{20,16},{24,28},{28,24},{32,36},... | collective-permute-start | bytes 3145736 | tf_op jit(solution)/shard_map/ppermute | solution.py:527
  20.5 2.3 collective-permute-done
  22.8 1.7 pad_maximum_fusion
  24.4 13.8 %all-to-all-start = ((f32[128,32,128]{2,1,0:T(8,128)}), f32[128,32,128]{2,1,0:T(8,128)S(1)}, u32[]{:S(2)}, u32[]{:S(2)}) async-start(f32[128,32,128]{2,1,0:T(8,128)} %pad_maximum_fusion), calls=%async_computation | async-start | bytes 4194304 | tf_op jit(solution)/shard_map/all_to_all | solution.py:471
  39.9 1.5 collective-permute-done.1
  43.5 1.8 collective-permute-start.4
  46.5 4.0 %collective-permute-done.2 = f32[8,4,8,128]{3,2,1,0:T(8,128)S(1)} collective-permute-done((f32[8,4,8,128]{3,2,1,0:T(8,128)S(1)}, f32[8,4,8,128]{3,2,1,0:T(8,128)S(1)}, u32[]{:S(2)}, u32[]{:S(2)}) %collective-permute-start.2) | collective-permute-done | bytes 131104 | tf_op jit(solution)/shard_map/ppermute | solution.py:540
  52.0 3.9 %collective-permute-done.3 = f32[8,4,8,128]{3,2,1,0:T(8,128)S(1)} collective-permute-done((f32[8,4,8,128]{3,2,1,0:T(8,128)S(1)}, f32[8,4,8,128]{3,2,1,0:T(8,128)S(1)}, u32[]{:S(2)}, u32[]{:S(2)}) %collective-permute-start.3) | collective-permute-done | bytes 131104 | tf_op jit(solution)/shard_map/ppermute | solution.py:540
  56.1 2.7 %collective-permute-start.7 = (f32[8,8,128]{2,1,0:T(8,128)S(1)}, f32[8,8,128]{2,1,0:T(8,128)S(1)}, u32[]{:S(2)}, u32[]{:S(2)}) collective-permute-start(f32[8,8,128]{2,1,0:T(8,128)S(1)} %get-tuple-element.36), channel_id=1, source_target_pairs={{0,24},{4,28},{8,0},{12,4},{16,8},{20,12},{24,16},{28,20},{32,56},... | collective-permute-start | bytes 98312 | tf_op jit(solution)/shard_map/ppermute | solution.py:540
  60.5 3.6 %collective-permute-done.6 = f32[8,8,128]{2,1,0:T(8,128)S(1)} collective-permute-done((f32[8,8,128]{2,1,0:T(8,128)S(1)}, f32[8,8,128]{2,1,0:T(8,128)S(1)}, u32[]{:S(2)}, u32[]{:S(2)}) %collective-permute-start.6) | collective-permute-done | bytes 32800 | tf_op jit(solution)/shard_map/ppermute | solution.py:540
  64.1 24.2 %all-to-all-done = f32[128,32,128]{2,1,0:T(8,128)S(1)} async-done(((f32[128,32,128]{2,1,0:T(8,128)}), f32[128,32,128]{2,1,0:T(8,128)S(1)}, u32[]{:S(2)}, u32[]{:S(2)}) %all-to-all-start) | async-done | bytes 2097184 | tf_op jit(solution)/shard_map/all_to_all | solution.py:471
  88.3 3.3 %overlap.1 = (f32[16,256,128]{2,1,0:T(8,128)S(1)}, f32[32,24,128]{2,1,0:T(8,128)S(1)}) custom-call(s32[1]{0:T(128)} %bitcast.core_ref, f32[4096,128]{1,0:T(8,128)S(1)} %bitcast.67), custom_call_target="tpu_custom_call" | custom-call | flops 1610612736 | bytes 4194304 | tf_op jit(solution)/shard_map/overlap/pallas_call | solution.py:288
  92.9 17.5 %all_to_all.25 = f32[32,24,128]{2,1,0:T(8,128)S(1)} all-to-all(f32[32,24,128]{2,1,0:T(8,128)S(1)} %get-tuple-element.21), channel_id=1, replica_groups={{0,1,2,3,4,5,6,7,8,9,10,11,12,13,14,15,16,17,18,19,20,21,22,23,24,25,26..., dimensions={0} | all-to-all | bytes 786432 | tf_op jit(solution)/shard_map/all_to_all | solution.py:471
  110.5 10.3 %all_to_all.26 = f32[8,24,128]{2,1,0:T(8,128)S(1)} all-to-all(f32[8,24,128]{2,1,0:T(8,128)S(1)} %broadcast_in_dim.4), channel_id=1, replica_groups={{0,32,64,96,128,160,192,224},{4,36,68,100,132,164,196,228},{8,40,72,104..., dimensions={0} | all-to-all | bytes 196608 | tf_op jit(solution)/shard_map/all_to_all | solution.py:471
  120.9 15.4 %all_to_all.27.summed_ref = f32[32,24,128]{2,1,0:T(8,128)S(1)} all-to-all(f32[32,24,128]{2,1,0:T(8,128)S(1)} %broadcast_in_dim.5), channel_id=1, replica_groups={{0,1,2,3,4,5,6,7,8,9,10,11,12,13,14,15,16,17,18,19,20,21,22,23,24,25,26..., dimensions={0} | all-to-all | bytes 786432 | tf_op jit(solution)/shard_map/all_to_all | solution.py:471
  136.2 17.5 %solve.1 = (f32[4096,128]{1,0:T(8,128)S(1)}, f32[256,256]{1,0:T(8,128)}) custom-call(f32[32,24,128]{2,1,0:T(8,128)S(1)} %all_to_all.27.summed_ref, f32[16,256,128]{2,1,0:T(8,128)S(1)} %copy-done.8), custom_call_target="tpu_custom_call" | custom-call | flops 20000000000 | bytes 6291456 | tf_op jit(solution)/shard_map/solve/pallas_call | solution.py:410
  155.0 6.4 %all-to-all-start.4 = ((f32[128,32,128]{2,1,0:T(8,128)}), f32[128,32,128]{2,1,0:T(8,128)S(1)}, u32[]{:S(2)}, u32[]{:S(2)}) async-start(f32[128,32,128]{2,1,0:T(8,128)} %bitcast.68), calls=%async_computation.4 | async-start | bytes 4194304 | tf_op jit(solution)/shard_map/all_to_all | solution.py:471
  161.5 49.9 %all-to-all-done.4.arrived_ref = f32[128,32,128]{2,1,0:T(8,128)S(1)} async-done(((f32[128,32,128]{2,1,0:T(8,128)}), f32[128,32,128]{2,1,0:T(8,128)S(1)}, u32[]{:S(2)}, u32[]{:S(2)}) %all-to-all-start.4) | async-done | bytes 2097184 | tf_op jit(solution)/shard_map/all_to_all | solution.py:471
  212.5 4.2 %collective-permute-start.8 = (f32[128,16,128]{2,1,0:T(8,128)}, f32[128,16,128]{2,1,0:T(8,128)S(1)}, u32[]{:S(2)}, u32[]{:S(2)}) collective-permute-start(f32[128,16,128]{2,1,0:T(8,128)} %constant_dynamic-slice_fusion.8), channel_id=1, source_target_pairs={{0,4},{4,0},{8,12},{12,8},{16,20},{20,16},{24,28},{28,24},{32,36},... | collective-permute-start | bytes 3145736 | tf_op jit(solution)/shard_map/ppermute | solution.py:527
  217.7 1.6 collective-permute-start.15
  220.7 4.0 %collective-permute-start.12 = (f32[8,128]{1,0:T(8,128)S(1)}, f32[8,128]{1,0:T(8,128)S(1)}, u32[]{:S(2)}, u32[]{:S(2)}) collective-permute-start(f32[8,128]{1,0:T(8,128)S(1)} %get-tuple-element.42), channel_id=1, source_target_pairs={{0,128},{4,132},{8,136},{12,140},{16,144},{20,148},{24,152},{28,15... | collective-permute-start | bytes 12296 | tf_op jit(solution)/shard_map/ppermute | solution.py:540
  227.1 3.1 %collective-permute-done.11 = f32[8,128]{1,0:T(8,128)S(1)} collective-permute-done((f32[8,128]{1,0:T(8,128)S(1)}, f32[8,128]{1,0:T(8,128)S(1)}, u32[]{:S(2)}, u32[]{:S(2)}) %collective-permute-start.11) | collective-permute-done | bytes 4128 | tf_op jit(solution)/shard_map/ppermute | solution.py:540
  (56 shorter events, 24.4 us)
Async XLA Ops:
  0.6 2.8 %copy-start.5 = (bf16[640,128]{1,0:T(8,128)(2,1)S(1)}, bf16[640,128]{1,0:T(8,128)(2,1)}, u32[]{:S(2)}) copy-start(bf16[640,128]{1,0:T(8,128)(2,1)} %constant.184.clone.magic_low_ref) | copy-start | bytes 491524
  0.6 2.8 %copy-start.2 = (f32[256]{0:T(256)S(1)}, f32[256]{0:T(256)}, u32[]{:S(2)}) copy-start(f32[256]{0:T(256)} %occupation_ref.1) | copy-start | bytes 3076
  3.4 1.2 copy-start.1
  17.1 5.6 %collective-permute-start = (f32[128,16,128]{2,1,0:T(8,128)S(1)}, f32[128,16,128]{2,1,0:T(8,128)S(1)}, u32[]{:S(2)}, u32[]{:S(2)}) collective-permute-start(f32[128,16,128]{2,1,0:T(8,128)S(1)} %get-tuple-element.18), channel_id=1, source_target_pairs={{0,4},{4,0},{8,12},{12,8},{16,20},{20,16},{24,28},{28,24},{32,36},... | collective-permute-start | bytes 3145736 | tf_op jit(solution)/shard_map/ppermute | solution.py:527
  24.4 63.9 %all-to-all-start = ((f32[128,32,128]{2,1,0:T(8,128)}), f32[128,32,128]{2,1,0:T(8,128)S(1)}, u32[]{:S(2)}, u32[]{:S(2)}) async-start(f32[128,32,128]{2,1,0:T(8,128)} %pad_maximum_fusion), calls=%async_computation | async-start | bytes 4194304 | tf_op jit(solution)/shard_map/all_to_all | solution.py:471
  39.2 2.3 collective-permute-start.1
  42.6 7.9 %collective-permute-start.2 = (f32[8,4,8,128]{3,2,1,0:T(8,128)S(1)}, f32[8,4,8,128]{3,2,1,0:T(8,128)S(1)}, u32[]{:S(2)}, u32[]{:S(2)}) collective-permute-start(f32[8,4,8,128]{3,2,1,0:T(8,128)S(1)} %get-tuple-element.32), channel_id=1, source_target_pairs={{0,1},{1,2},{2,3},{3,0},{4,5},{5,6},{6,7},{7,4},{8,9},{9,10},{10,1... | collective-permute-start | bytes 393224 | tf_op jit(solution)/shard_map/ppermute | solution.py:540
  43.5 8.5 %collective-permute-start.4 = (f32[8,4,8,128]{3,2,1,0:T(8,128)S(1)}, f32[8,4,8,128]{3,2,1,0:T(8,128)S(1)}, u32[]{:S(2)}, u32[]{:S(2)}) collective-permute-start(f32[8,4,8,128]{3,2,1,0:T(8,128)S(1)} %get-tuple-element.33), channel_id=1, source_target_pairs={{0,3},{1,0},{2,1},{3,2},{4,7},{5,4},{6,5},{7,6},{8,11},{9,8},{10,9... | collective-permute-start | bytes 393224 | tf_op jit(solution)/shard_map/ppermute | solution.py:540
  45.4 10.5 %collective-permute-start.3 = (f32[8,4,8,128]{3,2,1,0:T(8,128)S(1)}, f32[8,4,8,128]{3,2,1,0:T(8,128)S(1)}, u32[]{:S(2)}, u32[]{:S(2)}) collective-permute-start(f32[8,4,8,128]{3,2,1,0:T(8,128)S(1)} %get-tuple-element.34), channel_id=1, source_target_pairs={{0,2},{1,3},{2,0},{3,1},{4,6},{5,7},{6,4},{7,5},{8,10},{9,11},{10,... | collective-permute-start | bytes 393224 | tf_op jit(solution)/shard_map/ppermute | solution.py:540
  56.0 4.5 %collective-permute-start.5 = (f32[8,8,128]{2,1,0:T(8,128)S(1)}, f32[8,8,128]{2,1,0:T(8,128)S(1)}, u32[]{:S(2)}, u32[]{:S(2)}) collective-permute-start(f32[8,8,128]{2,1,0:T(8,128)S(1)} %get-tuple-element.35), channel_id=1, source_target_pairs={{0,8},{4,12},{8,16},{12,20},{16,24},{20,28},{24,0},{28,4},{32,40},... | collective-permute-start | bytes 98312 | tf_op jit(solution)/shard_map/ppermute | solution.py:540
  56.1 4.4 %collective-permute-start.7 = (f32[8,8,128]{2,1,0:T(8,128)S(1)}, f32[8,8,128]{2,1,0:T(8,128)S(1)}, u32[]{:S(2)}, u32[]{:S(2)}) collective-permute-start(f32[8,8,128]{2,1,0:T(8,128)S(1)} %get-tuple-element.36), channel_id=1, source_target_pairs={{0,24},{4,28},{8,0},{12,4},{16,8},{20,12},{24,16},{28,20},{32,56},... | collective-permute-start | bytes 98312 | tf_op jit(solution)/shard_map/ppermute | solution.py:540
  58.7 5.4 %collective-permute-start.6 = (f32[8,8,128]{2,1,0:T(8,128)S(1)}, f32[8,8,128]{2,1,0:T(8,128)S(1)}, u32[]{:S(2)}, u32[]{:S(2)}) collective-permute-start(f32[8,8,128]{2,1,0:T(8,128)S(1)} %get-tuple-element.37), channel_id=1, source_target_pairs={{0,16},{4,20},{8,24},{12,28},{16,0},{20,4},{24,8},{28,12},{32,48},... | collective-permute-start | bytes 98312 | tf_op jit(solution)/shard_map/ppermute | solution.py:540
  91.6 1.4 copy-start.7
  92.9 43.3 %copy-start.8 = (f32[16,256,128]{2,1,0:T(8,128)S(1)}, f32[16,256,128]{2,1,0:T(8,128)}, u32[]{:S(2)}) copy-start(f32[16,256,128]{2,1,0:T(8,128)} %copy-done.7) | copy-start | bytes 6291460
  153.7 1.4 copy-start
  155.0 56.3 %all-to-all-start.4 = ((f32[128,32,128]{2,1,0:T(8,128)}), f32[128,32,128]{2,1,0:T(8,128)S(1)}, u32[]{:S(2)}, u32[]{:S(2)}) async-start(f32[128,32,128]{2,1,0:T(8,128)} %bitcast.68), calls=%async_computation.4 | async-start | bytes 4194304 | tf_op jit(solution)/shard_map/all_to_all | solution.py:471
  212.5 18.8 %collective-permute-start.8 = (f32[128,16,128]{2,1,0:T(8,128)}, f32[128,16,128]{2,1,0:T(8,128)S(1)}, u32[]{:S(2)}, u32[]{:S(2)}) collective-permute-start(f32[128,16,128]{2,1,0:T(8,128)} %constant_dynamic-slice_fusion.8), channel_id=1, source_target_pairs={{0,4},{4,0},{8,12},{12,8},{16,20},{20,16},{24,28},{28,24},{32,36},... | collective-permute-start | bytes 3145736 | tf_op jit(solution)/shard_map/ppermute | solution.py:527
  216.6 4.1 %collective-permute-start.9 = (f32[8,128]{1,0:T(8,128)S(1)}, f32[8,128]{1,0:T(8,128)S(1)}, u32[]{:S(2)}, u32[]{:S(2)}) collective-permute-start(f32[8,128]{1,0:T(8,128)S(1)} %get-tuple-element.38), channel_id=1, source_target_pairs={{0,32},{4,36},{8,40},{12,44},{16,48},{20,52},{24,56},{28,60},{32,6... | collective-permute-start | bytes 12296 | tf_op jit(solution)/shard_map/ppermute | solution.py:540
  217.7 7.0 %collective-permute-start.15 = (f32[8,128]{1,0:T(8,128)S(1)}, f32[8,128]{1,0:T(8,128)S(1)}, u32[]{:S(2)}, u32[]{:S(2)}) collective-permute-start(f32[8,128]{1,0:T(8,128)S(1)} %get-tuple-element.39), channel_id=1, source_target_pairs={{0,224},{4,228},{8,232},{12,236},{16,240},{20,244},{24,248},{28,25... | collective-permute-start | bytes 12296 | tf_op jit(solution)/shard_map/ppermute | solution.py:540
  219.4 6.2 %collective-permute-start.14 = (f32[8,128]{1,0:T(8,128)S(1)}, f32[8,128]{1,0:T(8,128)S(1)}, u32[]{:S(2)}, u32[]{:S(2)}) collective-permute-start(f32[8,128]{1,0:T(8,128)S(1)} %get-tuple-element.40), channel_id=1, source_target_pairs={{0,192},{4,196},{8,200},{12,204},{16,208},{20,212},{24,216},{28,22... | collective-permute-start | bytes 12296 | tf_op jit(solution)/shard_map/ppermute | solution.py:540
  219.4 6.9 %collective-permute-start.13 = (f32[8,128]{1,0:T(8,128)S(1)}, f32[8,128]{1,0:T(8,128)S(1)}, u32[]{:S(2)}, u32[]{:S(2)}) collective-permute-start(f32[8,128]{1,0:T(8,128)S(1)} %get-tuple-element.41), channel_id=1, source_target_pairs={{0,160},{4,164},{8,168},{12,172},{16,176},{20,180},{24,184},{28,18... | collective-permute-start | bytes 12296 | tf_op jit(solution)/shard_map/ppermute | solution.py:540
  220.7 6.4 %collective-permute-start.12 = (f32[8,128]{1,0:T(8,128)S(1)}, f32[8,128]{1,0:T(8,128)S(1)}, u32[]{:S(2)}, u32[]{:S(2)}) collective-permute-start(f32[8,128]{1,0:T(8,128)S(1)} %get-tuple-element.42), channel_id=1, source_target_pairs={{0,128},{4,132},{8,136},{12,140},{16,144},{20,148},{24,152},{28,15... | collective-permute-start | bytes 12296 | tf_op jit(solution)/shard_map/ppermute | solution.py:540
  224.8 5.5 %collective-permute-start.11 = (f32[8,128]{1,0:T(8,128)S(1)}, f32[8,128]{1,0:T(8,128)S(1)}, u32[]{:S(2)}, u32[]{:S(2)}) collective-permute-start(f32[8,128]{1,0:T(8,128)S(1)} %get-tuple-element.43), channel_id=1, source_target_pairs={{0,96},{4,100},{8,104},{12,108},{16,112},{20,116},{24,120},{28,124... | collective-permute-start | bytes 12296 | tf_op jit(solution)/shard_map/ppermute | solution.py:540
  225.6 5.0 %collective-permute-start.10 = (f32[8,128]{1,0:T(8,128)S(1)}, f32[8,128]{1,0:T(8,128)S(1)}, u32[]{:S(2)}, u32[]{:S(2)}) collective-permute-start(f32[8,128]{1,0:T(8,128)S(1)} %get-tuple-element.44), channel_id=1, source_target_pairs={{0,64},{4,68},{8,72},{12,76},{16,80},{20,84},{24,88},{28,92},{32,9... | collective-permute-start | bytes 12296 | tf_op jit(solution)/shard_map/ppermute | solution.py:540
  (3 other events, 2.9 us)

commit v2 on v1

--- a/solution.py
+++ b/solution.py
@@ -16,7 +16,7 @@
 SHIFT = 2
 STRIP = 16
 ROWS = 8
-BLOCK = 32
+BLOCK = 64
 
 magic_taps = (0.0028, -0.0236, 0.1026, 0.8364, 0.1026, -0.0236, 0.0028)
 kinetic_taps = (
@@ -83,23 +83,47 @@
 
 def hamiltonian_kernel(
     place_ref,
-    bounds_ref,
     occupation_ref,
-    orbital_ref,
-    potential_ref,
-    both_high_ref,
-    both_low_ref,
-    magic_high_ref,
-    magic_low_ref,
+    bounds_hbm,
+    orbital_hbm,
+    both_high_hbm,
+    both_low_hbm,
+    potential_hbm,
+    magic_high_hbm,
+    magic_low_hbm,
     keep_ref,
     give_ref,
     density_ref,
+    bounds_ref,
+    orbital_ref,
+    both_high_ref,
+    both_low_ref,
+    potential_ref,
+    magic_high_ref,
+    magic_low_ref,
     source,
     filtered,
     kinetic,
+    sems,
 ):
     margin = len(kinetic_taps) // 2
     position, core = place_ref[0], place_ref[1]
+    copies = [
+        pltpu.make_async_copy(far, near, sems.at[k])
+        for k, (far, near) in enumerate(
+            (
+                (bounds_hbm, bounds_ref),
+                (orbital_hbm, orbital_ref),
+                (both_high_hbm, both_high_ref),
+                (both_low_hbm, both_low_ref),
+                (potential_hbm, potential_ref),
+                (magic_high_hbm, magic_high_ref),
+                (magic_low_hbm, magic_low_ref),
+            )
+        )
+    ]
+    for copy in copies:
+        copy.start()
 
     zeros = jnp.zeros((margin, PAIRS + 2 * PAD, LANES), jnp.float32)
     source[:margin] = zeros
@@ -132,8 +156,11 @@
     def half(x):
         return filtered[pl.ds(margin + x, STRIP)]
 
-    planes = lax.broadcasted_iota(jnp.int32, (STRIP, PAIRS, LANES), 0)
-    begin, end = bounds_ref[position, 0], bounds_ref[position, 1]
+    copies[0].wait()
+    copies[1].wait()
+    planes = lax.broadcasted_iota(jnp.int32, (STRIP * PAIRS, LANES), 0) // PAIRS
+    bounds = bounds_ref[pl.ds(position, 1), :]
+    begin, end = bounds[:, 0:1], bounds[:, 1:2]
     blocks = STRIP * PAIRS // ROWS
     half_planes = G // 2
 
@@ -144,10 +171,14 @@
         for strip in range(0, half_planes, STRIP):
             x = half_planes * side + strip
             inside = (planes + x >= begin) & (planes + x < end)
-            masked = jnp.where(inside, orbital_ref[pl.ds(x, STRIP)], 0.0)
+            orbital = orbital_ref[pl.ds(x, STRIP)].reshape(STRIP * PAIRS, LANES)
+            masked = jnp.where(inside, orbital, 0.0).reshape(STRIP, PAIRS, LANES)
             source[pl.ds(margin + x, STRIP), PAD : PAD + PAIRS] = masked
             first = strip * PAIRS // ROWS
             out_ref[first : first + blocks, :ROWS, :] = tiled(masked)
+
+    copies[2].wait()
+    copies[3].wait()
 
     @pl.loop(0, G, step=STRIP)
     def _(x):
@@ -157,6 +188,7 @@
             own, x, kinetic_taps
         )
 
+    copies[4].wait()
     scale = occupation_ref[position] * (1.0 / occupation_ref.shape[0])
     lines = STRIP * G // 2
 
@@ -169,6 +201,9 @@
         ).reshape(STRIP, PAIRS, LANES)
         source[pl.ds(margin + x, STRIP), PAD : PAD + PAIRS] = realspace * potential
 
+    copies[5].wait()
+    copies[6].wait()
+
     @pl.loop(0, G, step=STRIP)
     def _(x):
         filtered[pl.ds(margin + x, STRIP)] = product(x, magic_high_ref, magic_low_ref).reshape(
@@ -191,37 +226,35 @@
     return pl.BlockSpec(memory_space=pltpu.SMEM)
 
 
+def anywhere():
+    return pl.BlockSpec(memory_space=pl.ANY)
+
+
 def apply_hamiltonian(place, region_bounds, occupation, orbital, potential):
     (both_high, both_low), (magic_high, magic_low) = filter_constants()
     margin = len(kinetic_taps) // 2
     side = jax.ShapeDtypeStruct((G * PAIRS // ROWS // 2, 2 * ROWS, LANES), jnp.float32)
     grid = jax.ShapeDtypeStruct((G, PAIRS, LANES), jnp.float32)
+    far = (region_bounds, orbital, both_high, both_low, potential, magic_high, magic_low)
+    far = [jnp.asarray(values) for values in far]
     return pl.pallas_call(
         hamiltonian_kernel,
         out_shape=(side, side, grid),
-        in_specs=[smem()] * 3 + [vmem()] * 6,
+        in_specs=[smem()] * 2 + [anywhere()] * len(far),
         out_specs=(vmem(),) * 3,
-        scratch_shapes=[
+        scratch_shapes=[pltpu.VMEM(values.shape, values.dtype) for values in far]
+        + [
             pltpu.VMEM((G + 2 * margin, PAIRS + 2 * PAD, LANES), jnp.float32),
             pltpu.VMEM((G + 2 * margin, PAIRS, LANES), jnp.float32),
             pltpu.VMEM((G, PAIRS, LANES), jnp.float32),
+            pltpu.SemaphoreType.DMA((len(far),)),
         ],
         compiler_params=pltpu.CompilerParams(vmem_limit_bytes=40 * 2**20),
         cost_estimate=pl.CostEstimate(
             flops=6 * 2048 * 640 * 384, bytes_accessed=5 * 2**20, transcendentals=0
         ),
         name="hamiltonian",
-    )(
-        place,
-        region_bounds,
-        occupation,
-        orbital,
-        potential,
-        jnp.asarray(both_high),
-        jnp.asarray(both_low),
-        jnp.asarray(magic_high),
-        jnp.asarray(magic_low),
-    )
+    )(place, occupation, *far)
 
 
 def transposed_dot(a, b):
@@ -234,28 +267,32 @@
 LINES = 4
 
 
-def natural_rows(flat_ref, natural_ref, core, gather):
+def natural_rows(flat_ref, natural_ref, core, gather, part=0, parts=1):
     planes, orbitals, _ = natural_ref.shape
-    groups = orbitals // (CORES * LINES)
+    groups = orbitals // (CORES * LINES * parts)
     stride = CORES * LINES * planes
     for slot in range(CORES):
         for line in range(LINES):
             for plane in range(planes):
-                inner = pl.ds((line * CORES + slot) * planes + plane, groups, stride=stride)
-                outer = pl.ds((slot ^ core) * LINES + line, groups, stride=CORES * LINES)
+                inner = (line * CORES + slot) * planes + plane + part * groups * stride
+                inner = pl.ds(inner, groups, stride=stride)
+                outer = (slot ^ core) * LINES + line + part * groups * CORES * LINES
+                outer = pl.ds(outer, groups, stride=CORES * LINES)
                 if gather:
                     natural_ref[plane, outer, :] = flat_ref[inner, :]
                 else:
                     flat_ref[inner, :] = natural_ref[plane, outer, :]
 
 
-def overlap_kernel(core_ref, flat_ref, natural_ref, packed_ref):
+def overlap_kernel(core_ref, flat_ref, natural_hbm, packed_ref, natural_ref, sem):
     for core in range(CORES):
 
         @pl.when(core_ref[0] == core)
         def _(core=core):
             natural_rows(flat_ref, natural_ref, core, True)
 
+    copy = pltpu.make_async_copy(natural_ref, natural_hbm, sem)
+    copy.start()
     planes, size, _ = natural_ref.shape
     half = planes // 2
     total = None
@@ -279,6 +316,7 @@
     packed_ref[:, size // LANES * ROWS :, :] = jnp.broadcast_to(
         diagonal, (size, LANES)
     ).reshape(chunks, ROWS, LANES)
+    copy.wait()
 
 
 def overlap(core, arrived):
@@ -292,7 +330,11 @@
             jax.ShapeDtypeStruct((size // ROWS, (size // LANES + 1) * ROWS, LANES), jnp.float32),
         ),
         in_specs=[smem(), vmem()],
-        out_specs=(vmem(), vmem()),
+        out_specs=(anywhere(), vmem()),
+        scratch_shapes=[
+            pltpu.VMEM((planes, size, lanes), jnp.float32),
+            pltpu.SemaphoreType.DMA,
+        ],
         compiler_params=pltpu.CompilerParams(vmem_limit_bytes=40 * 2**20),
         cost_estimate=pl.CostEstimate(
             flops=24 * 256 * 256 * 1024, bytes_accessed=4 * 2**20, transcendentals=0
@@ -334,12 +376,13 @@
             for j in range(ROWS):
                 pivot = row_of(spread[q][j], j)
                 root = lax.rsqrt(pivot)
-                root = root * (1.5 - 0.5 * pivot * root * root)
                 scales = jnp.where(sub == j, root, scales)
                 weight = {}
                 for g in range(q, groups):
-                    weight[g] = spread[g][j] * root
-                weight[q] = jnp.where(sub > j, weight[q], 0.0)
+                    below = spread[g][j]
+                    if g == q:
+                        below = jnp.where(sub > j, below, 0.0)
+                    weight[g] = below * root
                 for m in range(j + 1, ROWS):
                     top = row_of(spread[q][m], j) * root
                     for g in range(q, groups):
@@ -366,7 +409,22 @@
             work[stop:, low:last] = work[stop:, low:last] - update[stop - low :, :]
 
 
-def solve_kernel(cells, summed_ref, natural_ref, flat_ref, subspace_ref, work, mixed):
+def solve_kernel(
+    cells,
+    summed_ref,
+    natural_hbm,
+    flat_hbm,
+    subspace_ref,
+    work,
+    natural_ref,
+    mixed,
+    flat_ref,
+    in_sem,
+    out_sems,
+):
+    arrival = pltpu.make_async_copy(natural_hbm, natural_ref, in_sem)
+    arrival.start()
+
     def dot(a, b):
         return jnp.dot(a, b, precision=precise, preferred_element_type=jnp.float32)
 
@@ -390,6 +448,7 @@
     subspace_ref[...] = subspace
     planes = natural_ref.shape[0]
     half = planes // 2
+    arrival.wait()
     for plane in range(0, half, 2):
         both = [
             dot(
@@ -402,7 +461,17 @@
         for k, part in enumerate(both):
             mixed[plane + k] = part[:, :LANES]
             mixed[half + plane + k] = part[:, LANES:] - product[:, k * LANES : (k + 1) * LANES]
-    natural_rows(flat_ref, mixed, 0, False)
+    parts = 4
+    rows = flat_ref.shape[0] // parts
+    copies = []
+    for part in range(parts):
+        natural_rows(flat_ref, mixed, 0, False, part, parts)
+        here = pl.ds(part * rows, rows)
+        copy = pltpu.make_async_copy(flat_ref.at[here], flat_hbm.at[here], out_sems.at[part])
+        copy.start()
+        copies.append(copy)
+    for copy in copies:
+        copy.wait()
 
 
 def solve(summed, natural, cells):
@@ -413,11 +482,15 @@
             jax.ShapeDtypeStruct((planes * size, lanes), jnp.float32),
             jax.ShapeDtypeStruct((size, size), jnp.float32),
         ),
-        in_specs=[vmem()] * 2,
-        out_specs=(vmem(), vmem()),
+        in_specs=[vmem(), anywhere()],
+        out_specs=(anywhere(), vmem()),
         scratch_shapes=[
             pltpu.VMEM((size, 2 * size), jnp.float32),
             pltpu.VMEM(natural.shape, jnp.float32),
+            pltpu.VMEM(natural.shape, jnp.float32),
+            pltpu.VMEM((planes * size, lanes), jnp.float32),
+            pltpu.SemaphoreType.DMA,
+            pltpu.SemaphoreType.DMA((4,)),
         ],
         compiler_params=pltpu.CompilerParams(vmem_limit_bytes=48 * 2**20),
         cost_estimate=pl.CostEstimate(
@@ -451,12 +524,11 @@
 def assemble(core, arrived, received):
     blocks, _, lanes = received.shape
     out = jax.ShapeDtypeStruct((CORES * blocks, ROWS, lanes), jnp.float32)
-    anywhere = pl.BlockSpec(memory_space=pl.ANY)
     return pl.pallas_call(
         assemble_kernel,
         out_shape=(out, out),
         in_specs=[smem(), vmem(), vmem()],
-        out_specs=(anywhere, anywhere),
+        out_specs=(anywhere(), anywhere()),
         scratch_shapes=[
             pltpu.VMEM((4, blocks, ROWS, lanes), jnp.float32),
             pltpu.SemaphoreType.DMA((4,)),
@@ -531,7 +603,6 @@
     me = lax.axis_index("orb")
     core = me % layout.core
     x = me // layout.core % layout.x
-    z = me // (layout.core * layout.x)
     y = lax.axis_index("grp")
 
     def stage(values, dim, count, index, axis, pairs):
@@ -548,9 +619,9 @@
             total = total + term
         return total
 
-    def along(dz, dx, dc):
+    def along(dx, dc):
         return lambda k: [
-            (layout.orb(a, b, c), layout.orb(a + dz * k, b + dx * k, c + dc * k))
+            (layout.orb(a, b, c), layout.orb(a, b + dx * k, c + dc * k))
             for a, b, c in layout.places()
         ]
 
@@ -558,21 +629,19 @@
         return [(i, (i + k) % layout.y) for i in range(layout.y)]
 
     values = partial.reshape(layout.z, layout.x, layout.core, layout.y, -1, LANES)
-    values = stage(values, 2, layout.core, core, "orb", along(0, 0, 1))
+    values = stage(values, 2, layout.core, core, "orb", along(0, 1))
     values = stage(values, 2, layout.y, y, "grp", lines)
-    values = stage(values, 1, layout.x, x, "orb", along(0, 1, 0))
-    return values, lambda values: stage(values, 0, layout.z, z, "orb", along(1, 0, 0))
-
-
-def sum_everywhere(chunks, layout):
+    return stage(values, 1, layout.x, x, "orb", along(1, 0))
+
+
+def sum_everywhere(chunks, slabs, layout):
     count, rows, lanes = chunks.shape
-
-    def spread(values, copies):
-        return jnp.broadcast_to(jnp.sum(values, axis=0, keepdims=True), (copies, rows, lanes))
-
-    part = spread(exchange(chunks, layout.planes()), layout.z)
-    part = spread(exchange(part, layout.columns(), "orb"), count)
-    return exchange(part, layout.planes())
+    part = jnp.sum(exchange(chunks, layout.planes()), axis=0, keepdims=True)
+    part = jnp.broadcast_to(part, (layout.z, rows, lanes))
+    part = exchange(jnp.concatenate([part, slabs], axis=1), layout.columns(), "orb")
+    total = jnp.sum(part, axis=0)
+    everywhere = jnp.broadcast_to(total[None, :rows], (count, rows, lanes))
+    return exchange(everywhere, layout.planes()), total[rows:]
 
 
 def on_device(layout, orbitals, potential, occupation, region_bounds):
@@ -586,14 +655,12 @@
         place, region_bounds, occupation, orbitals.reshape(G, PAIRS, LANES), potential
     )
     sent = jnp.concatenate([keep, layout.swap_cores(give)], axis=1)
-    plane_density, along_z = reduce_slab(density_part, layout)
+    slabs = reduce_slab(density_part, layout)
     arrived = exchange(sent, layout.chips())
-    arrived, plane_density = lax.optimization_barrier((arrived, plane_density))
+    arrived, slabs = lax.optimization_barrier((arrived, slabs))
     natural, packed = overlap(core, arrived.reshape(-1, LANES))
-    summed = sum_everywhere(packed, layout)
+    summed, density = sum_everywhere(packed, slabs, layout)
     mixed, subspace = solve(summed, natural, cell_total)
-    mixed, plane_density = lax.optimization_barrier((mixed, plane_density))
-    density = along_z(plane_density)
     back = exchange(mixed.reshape(-1, 4 * ROWS, LANES), layout.chips())
     other = lax.dynamic_slice_in_dim(back, (1 - core[0]) * 2 * ROWS, 2 * ROWS, 1)
     orthonormal, gradient = assemble(core, back, layout.swap_cores(other))

time: 234 us -> 219 us (0.936)
  starting transfers between devices: 45.5 us -> 37.2 us
  waiting for transfers between devices: 96.2 us -> 92.2 us
  Pallas kernels: 31.7 us -> 29.1 us
    ppermute x14 -> x7, starting transfers between devices: 17.8 us -> 9.65 us  [stage(): lax.ppermute(lax.dynamic_index_in_dim(values, (index + k) % count, dim, k...]
    ppermute x14 -> x7, waiting for transfers between devices: 19.8 us -> 14 us  [stage(): lax.ppermute(lax.dynamic_index_in_dim(values, (index + k) % count, dim, k...]
  transfers between devices with their start and end apart: 18 -> 11, of which waited for: 12 -> 8; matrix products, arithmetic and copies ran while one was open for 1% -> 1% of each run, Pallas kernels for 0% -> 0%
where the time goes in v2:
time: 219 us; the launch traced here: 218 us
  waiting for transfers between devices  92.2 us (42%)
  blocking collectives  43.4 us (20%)
  starting transfers between devices  37.2 us (17%)
  Pallas kernels  29.1 us (13%)
  local copies, waits for them, and re-layouts  12.2 us (6%)
  other arithmetic  2.95 us (1%)
    all_to_all x2, waiting for transfers between devices, exchange(): lax.all_to_all(blocks, axes, split_axis=0, concat_axis=0, tiled=True, axi...  74 us
    all_to_all x3, blocking collectives, exchange(): lax.all_to_all(blocks, axes, split_axis=0, concat_axis=0, tiled=True, axi...  43.4 us
    all_to_all x2, starting transfers between devices, exchange(): lax.all_to_all(blocks, axes, split_axis=0, concat_axis=0, tiled=True, axi...  20 us
    pallas_call x1, Pallas kernels, solve(): pl.pallas_call(functools.partial(solve_kernel, cells), out_shape=(jax.Sha...  15.6 us
    ppermute x7, waiting for transfers between devices, stage(): lax.ppermute(lax.dynamic_index_in_dim(values, (index + k) % count, dim, k...  14 us
    ppermute x7, starting transfers between devices, stage(): lax.ppermute(lax.dynamic_index_in_dim(values, (index + k) % count, dim, k...  9.65 us
    unnamed x20, local copies, waits for them, and re-layouts  9.42 us
    pallas_call x1, Pallas kernels, apply_hamiltonian(): pl.pallas_call(hamiltonian_kernel, out_shape=(side, side, grid), in_specs...  8.65 us
  transfers between devices with their start and end apart: 11, of which 8 were waited for; matrix products, arithmetic and copies ran while one was open for 1% of the time, Pallas kernels for 0%

profile of v2, /device:TPU:1, one launch (start us, length us, event | category | flops | bytes accessed | tf_op | source)
XLA Modules:
  0.0 218.0 jit_solution(2370170831217692363)
XLA Ops:
  1.5 1.8 copy.15.potential_hbm
  7.5 8.7 %hamiltonian.1 = (f32[128,16,128]{2,1,0:T(8,128)S(1)}, f32[128,16,128]{2,1,0:T(8,128)S(1)}, f32[64,32,128]{2,1,0:T(8,128)S(1)}) custom-call(s32[2]{0:T(128)S(1)} %pad_add_fusion.place_ref, f32[256]{0:T(256)S(1)} %copy-done.2, s32[256,2]{1,0:T(8,128)S(1)} %copy.14.bounds_hbm, f32[64,32,128]{2,1,0:T(8,128)S(1)} %bitcast.43, bf16[640,256]{1,0:T(8,128)(2,1)S(1)} %copy-done.4, ...), custom_call_target="tpu_custom_call" | custom-call | flops 3019898880 | bytes 5242880 | tf_op jit(solution)/shard_map/hamiltonian/pallas_call | solution.py:240
  16.2 3.3 %collective-permute-start = (f32[128,16,128]{2,1,0:T(8,128)S(1)}, f32[128,16,128]{2,1,0:T(8,128)S(1)}, u32[]{:S(2)}, u32[]{:S(2)}) collective-permute-start(f32[128,16,128]{2,1,0:T(8,128)S(1)} %get-tuple-element.16), channel_id=1, source_target_pairs={{0,4},{4,0},{8,12},{12,8},{16,20},{20,16},{24,28},{28,24},{32,36},... | collective-permute-start | bytes 3145736 | tf_op jit(solution)/shard_map/ppermute | solution.py:599
  19.5 2.3 %collective-permute-done = f32[128,16,128]{2,1,0:T(8,128)S(1)} collective-permute-done((f32[128,16,128]{2,1,0:T(8,128)S(1)}, f32[128,16,128]{2,1,0:T(8,128)S(1)}, u32[]{:S(2)}, u32[]{:S(2)}) %collective-permute-start) | collective-permute-done | bytes 1048608 | tf_op jit(solution)/shard_map/ppermute | solution.py:599
  21.8 1.6 pad_maximum_fusion
  23.5 13.8 %all-to-all-start = ((f32[128,32,128]{2,1,0:T(8,128)}), f32[128,32,128]{2,1,0:T(8,128)S(1)}, u32[]{:S(2)}, u32[]{:S(2)}) async-start(f32[128,32,128]{2,1,0:T(8,128)} %pad_maximum_fusion), calls=%async_computation | async-start | bytes 4194304 | tf_op jit(solution)/shard_map/all_to_all | solution.py:543
  38.8 1.9 collective-permute-done.1
  42.8 2.4 %collective-permute-start.3 = (f32[8,4,8,128]{3,2,0,1:T(8,128)S(1)}, f32[8,4,8,128]{3,2,0,1:T(8,128)S(1)}, u32[]{:S(2)}, u32[]{:S(2)}) collective-permute-start(f32[8,4,8,128]{3,2,0,1:T(8,128)S(1)} %bitcast.45), channel_id=1, source_target_pairs={{0,2},{1,3},{2,0},{3,1},{4,6},{5,7},{6,4},{7,5},{8,10},{9,11},{10,... | collective-permute-start | bytes 393224 | tf_op jit(solution)/shard_map/ppermute | solution.py:611
  46.4 3.1 %collective-permute-done.2 = f32[8,4,8,128]{3,2,0,1:T(8,128)S(1)} collective-permute-done((f32[8,4,8,128]{3,2,0,1:T(8,128)S(1)}, f32[8,4,8,128]{3,2,0,1:T(8,128)S(1)}, u32[]{:S(2)}, u32[]{:S(2)}) %collective-permute-start.2) | collective-permute-done | bytes 131104 | tf_op jit(solution)/shard_map/ppermute | solution.py:611
  49.5 5.8 %collective-permute-done.3 = f32[8,4,8,128]{3,2,0,1:T(8,128)S(1)} collective-permute-done((f32[8,4,8,128]{3,2,0,1:T(8,128)S(1)}, f32[8,4,8,128]{3,2,0,1:T(8,128)S(1)}, u32[]{:S(2)}, u32[]{:S(2)}) %collective-permute-start.3) | collective-permute-done | bytes 131104 | tf_op jit(solution)/shard_map/ppermute | solution.py:611
  56.0 2.1 collective-permute-start.7
  58.1 1.7 collective-permute-start.6
  59.9 3.2 %collective-permute-done.6 = f32[8,8,128]{2,1,0:T(8,128)S(1)} collective-permute-done((f32[8,8,128]{2,1,0:T(8,128)S(1)}, f32[8,8,128]{2,1,0:T(8,128)S(1)}, u32[]{:S(2)}, u32[]{:S(2)}) %collective-permute-start.6) | collective-permute-done | bytes 32800 | tf_op jit(solution)/shard_map/ppermute | solution.py:611
  63.1 24.2 %all-to-all-done = f32[128,32,128]{2,1,0:T(8,128)S(1)} async-done(((f32[128,32,128]{2,1,0:T(8,128)}), f32[128,32,128]{2,1,0:T(8,128)S(1)}, u32[]{:S(2)}, u32[]{:S(2)}) %all-to-all-start) | async-done | bytes 2097184 | tf_op jit(solution)/shard_map/all_to_all | solution.py:543
  87.4 3.4 %overlap.1 = (f32[16,256,128]{2,1,0:T(8,128)S(1)}, f32[32,24,128]{2,1,0:T(8,128)S(1)}) custom-call(s32[1]{0:T(128)} %bitcast.core_ref, f32[4096,128]{1,0:T(8,128)S(1)} %bitcast.39), custom_call_target="tpu_custom_call" | custom-call | flops 1610612736 | bytes 4194304 | tf_op jit(solution)/shard_map/overlap/pallas_call | solution.py:326
  92.1 17.4 %all_to_all.25 = f32[32,24,128]{2,1,0:T(8,128)S(1)} all-to-all(f32[32,24,128]{2,1,0:T(8,128)S(1)} %get-tuple-element.19), channel_id=1, replica_groups={{0,1,2,3,4,5,6,7,8,9,10,11,12,13,14,15,16,17,18,19,20,21,22,23,24,25,26..., dimensions={0} | all-to-all | bytes 786432 | tf_op jit(solution)/shard_map/all_to_all | solution.py:543
  109.6 10.4 %all_to_all.26 = f32[8,32,128]{2,1,0:T(8,128)S(1)} all-to-all(f32[8,32,128]{2,1,0:T(8,128)S(1)} %pad_maximum_fusion.1), channel_id=1, replica_groups={{0,32,64,96,128,160,192,224},{4,36,68,100,132,164,196,228},{8,40,72,104..., dimensions={0} | all-to-all | bytes 262144 | tf_op jit(solution)/shard_map/all_to_all | solution.py:543
  120.0 15.6 %all_to_all.27.summed_ref = f32[32,24,128]{2,1,0:T(8,128)S(1)} all-to-all(f32[32,24,128]{2,1,0:T(8,128)S(1)} %broadcast_in_dim.5), channel_id=1, replica_groups={{0,1,2,3,4,5,6,7,8,9,10,11,12,13,14,15,16,17,18,19,20,21,22,23,24,25,26..., dimensions={0} | all-to-all | bytes 786432 | tf_op jit(solution)/shard_map/all_to_all | solution.py:543
  135.6 15.6 %solve.1 = (f32[4096,128]{1,0:T(8,128)S(1)}, f32[256,256]{1,0:T(8,128)}) custom-call(f32[32,24,128]{2,1,0:T(8,128)S(1)} %all_to_all.27.summed_ref, f32[16,256,128]{2,1,0:T(8,128)S(1)} %copy-done.8), custom_call_target="tpu_custom_call" | custom-call | flops 20000000000 | bytes 6291456 | tf_op jit(solution)/shard_map/solve/pallas_call | solution.py:479
  152.6 6.2 %all-to-all-start.4 = ((f32[128,32,128]{2,1,0:T(8,128)}), f32[128,32,128]{2,1,0:T(8,128)S(1)}, u32[]{:S(2)}, u32[]{:S(2)}) async-start(f32[128,32,128]{2,1,0:T(8,128)} %bitcast.40), calls=%async_computation.4 | async-start | bytes 4194304 | tf_op jit(solution)/shard_map/all_to_all | solution.py:543
  158.8 49.8 %all-to-all-done.4.arrived_ref = f32[128,32,128]{2,1,0:T(8,128)S(1)} async-done(((f32[128,32,128]{2,1,0:T(8,128)}), f32[128,32,128]{2,1,0:T(8,128)S(1)}, u32[]{:S(2)}, u32[]{:S(2)}) %all-to-all-start.4) | async-done | bytes 2097184 | tf_op jit(solution)/shard_map/all_to_all | solution.py:543
  209.7 4.3 %collective-permute-start.8 = (f32[128,16,128]{2,1,0:T(8,128)}, f32[128,16,128]{2,1,0:T(8,128)S(1)}, u32[]{:S(2)}, u32[]{:S(2)}) collective-permute-start(f32[128,16,128]{2,1,0:T(8,128)} %constant_dynamic-slice_fusion), channel_id=1, source_target_pairs={{0,4},{4,0},{8,12},{12,8},{16,20},{20,16},{24,28},{28,24},{32,36},... | collective-permute-start | bytes 3145736 | tf_op jit(solution)/shard_map/ppermute | solution.py:599
  214.6 1.8 collective-permute-done.8.received_ref
  216.4 1.4 assemble.1
  (45 shorter events, 15.1 us)
Async XLA Ops:
  0.6 2.8 %copy-start.5 = (bf16[640,128]{1,0:T(8,128)(2,1)S(1)}, bf16[640,128]{1,0:T(8,128)(2,1)}, u32[]{:S(2)}) copy-start(bf16[640,128]{1,0:T(8,128)(2,1)} %constant.120.clone.magic_low_hbm) | copy-start | bytes 491524
  0.6 2.8 %copy-start.2 = (f32[256]{0:T(256)S(1)}, f32[256]{0:T(256)}, u32[]{:S(2)}) copy-start(f32[256]{0:T(256)} %occupation_ref.1) | copy-start | bytes 3076
  3.4 1.2 copy-start.1
  4.7 1.0 copy-start.3
  5.6 1.0 copy-start.4
  6.6 0.9 copy-start.6
  16.2 5.6 %collective-permute-start = (f32[128,16,128]{2,1,0:T(8,128)S(1)}, f32[128,16,128]{2,1,0:T(8,128)S(1)}, u32[]{:S(2)}, u32[]{:S(2)}) collective-permute-start(f32[128,16,128]{2,1,0:T(8,128)S(1)} %get-tuple-element.16), channel_id=1, source_target_pairs={{0,4},{4,0},{8,12},{12,8},{16,20},{20,16},{24,28},{28,24},{32,36},... | collective-permute-start | bytes 3145736 | tf_op jit(solution)/shard_map/ppermute | solution.py:599
  23.5 63.9 %all-to-all-start = ((f32[128,32,128]{2,1,0:T(8,128)}), f32[128,32,128]{2,1,0:T(8,128)S(1)}, u32[]{:S(2)}, u32[]{:S(2)}) async-start(f32[128,32,128]{2,1,0:T(8,128)} %pad_maximum_fusion), calls=%async_computation | async-start | bytes 4194304 | tf_op jit(solution)/shard_map/all_to_all | solution.py:543
  38.1 2.5 %collective-permute-start.1 = (f32[8,4,4,8,128]{4,3,2,1,0:T(8,128)}, f32[8,4,4,8,128]{4,3,2,1,0:T(8,128)}, u32[]{:S(2)}, u32[]{:S(2)}) collective-permute-start(f32[8,4,4,8,128]{4,3,2,1,0:T(8,128)} %dynamic-slice_bitcast_fusion), channel_id=1, source_target_pairs={{0,4},{4,0},{8,12},{12,8},{16,20},{20,16},{24,28},{28,24},{32,36},... | collective-permute-start | bytes 1572872 | tf_op jit(solution)/shard_map/ppermute | solution.py:611
  41.9 7.6 %collective-permute-start.2 = (f32[8,4,8,128]{3,2,0,1:T(8,128)S(1)}, f32[8,4,8,128]{3,2,0,1:T(8,128)S(1)}, u32[]{:S(2)}, u32[]{:S(2)}) collective-permute-start(f32[8,4,8,128]{3,2,0,1:T(8,128)S(1)} %bitcast.46), channel_id=1, source_target_pairs={{0,1},{1,2},{2,3},{3,0},{4,5},{5,6},{6,7},{7,4},{8,9},{9,10},{10,1... | collective-permute-start | bytes 393224 | tf_op jit(solution)/shard_map/ppermute | solution.py:611
  42.8 12.5 %collective-permute-start.3 = (f32[8,4,8,128]{3,2,0,1:T(8,128)S(1)}, f32[8,4,8,128]{3,2,0,1:T(8,128)S(1)}, u32[]{:S(2)}, u32[]{:S(2)}) collective-permute-start(f32[8,4,8,128]{3,2,0,1:T(8,128)S(1)} %bitcast.45), channel_id=1, source_target_pairs={{0,2},{1,3},{2,0},{3,1},{4,6},{5,7},{6,4},{7,5},{8,10},{9,11},{10,... | collective-permute-start | bytes 393224 | tf_op jit(solution)/shard_map/ppermute | solution.py:611
  45.2 10.1 %collective-permute-start.4 = (f32[8,4,8,128]{3,2,0,1:T(8,128)S(1)}, f32[8,4,8,128]{3,2,0,1:T(8,128)S(1)}, u32[]{:S(2)}, u32[]{:S(2)}) collective-permute-start(f32[8,4,8,128]{3,2,0,1:T(8,128)S(1)} %bitcast.44), channel_id=1, source_target_pairs={{0,3},{1,0},{2,1},{3,2},{4,7},{5,4},{6,5},{7,6},{8,11},{9,8},{10,9... | collective-permute-start | bytes 393224 | tf_op jit(solution)/shard_map/ppermute | solution.py:611
  55.4 4.5 %collective-permute-start.5 = (f32[8,8,128]{2,1,0:T(8,128)S(1)}, f32[8,8,128]{2,1,0:T(8,128)S(1)}, u32[]{:S(2)}, u32[]{:S(2)}) collective-permute-start(f32[8,8,128]{2,1,0:T(8,128)S(1)} %get-tuple-element.30), channel_id=1, source_target_pairs={{0,8},{4,12},{8,16},{12,20},{16,24},{20,28},{24,0},{28,4},{32,40},... | collective-permute-start | bytes 98312 | tf_op jit(solution)/shard_map/ppermute | solution.py:611
  56.0 3.8 %collective-permute-start.7 = (f32[8,8,128]{2,1,0:T(8,128)S(1)}, f32[8,8,128]{2,1,0:T(8,128)S(1)}, u32[]{:S(2)}, u32[]{:S(2)}) collective-permute-start(f32[8,8,128]{2,1,0:T(8,128)S(1)} %get-tuple-element.31), channel_id=1, source_target_pairs={{0,24},{4,28},{8,0},{12,4},{16,8},{20,12},{24,16},{28,20},{32,56},... | collective-permute-start | bytes 98312 | tf_op jit(solution)/shard_map/ppermute | solution.py:611
  58.1 5.0 %collective-permute-start.6 = (f32[8,8,128]{2,1,0:T(8,128)S(1)}, f32[8,8,128]{2,1,0:T(8,128)S(1)}, u32[]{:S(2)}, u32[]{:S(2)}) collective-permute-start(f32[8,8,128]{2,1,0:T(8,128)S(1)} %get-tuple-element.32), channel_id=1, source_target_pairs={{0,16},{4,20},{8,24},{12,28},{16,0},{20,4},{24,8},{28,12},{32,48},... | collective-permute-start | bytes 98312 | tf_op jit(solution)/shard_map/ppermute | solution.py:611
  90.8 1.3 copy-start.7
  92.1 43.5 %copy-start.8 = (f32[16,256,128]{2,1,0:T(8,128)S(1)}, f32[16,256,128]{2,1,0:T(8,128)}, u32[]{:S(2)}) copy-start(f32[16,256,128]{2,1,0:T(8,128)} %copy-done.7) | copy-start | bytes 6291460
  151.2 1.3 copy-start
  152.6 56.0 %all-to-all-start.4 = ((f32[128,32,128]{2,1,0:T(8,128)}), f32[128,32,128]{2,1,0:T(8,128)S(1)}, u32[]{:S(2)}, u32[]{:S(2)}) async-start(f32[128,32,128]{2,1,0:T(8,128)} %bitcast.40), calls=%async_computation.4 | async-start | bytes 4194304 | tf_op jit(solution)/shard_map/all_to_all | solution.py:543
  209.7 6.8 %collective-permute-start.8 = (f32[128,16,128]{2,1,0:T(8,128)}, f32[128,16,128]{2,1,0:T(8,128)S(1)}, u32[]{:S(2)}, u32[]{:S(2)}) collective-permute-start(f32[128,16,128]{2,1,0:T(8,128)} %constant_dynamic-slice_fusion), channel_id=1, source_target_pairs={{0,4},{4,0},{8,12},{12,8},{16,20},{20,16},{24,28},{28,24},{32,36},... | collective-permute-start | bytes 3145736 | tf_op jit(solution)/shard_map/ppermute | solution.py:599

commit v3 on v2

--- a/solution.py
+++ b/solution.py
@@ -226,8 +226,8 @@
     return pl.BlockSpec(memory_space=pltpu.SMEM)
 
 
-def anywhere():
-    return pl.BlockSpec(memory_space=pl.ANY)
+def far_away():
+    return pl.BlockSpec(memory_space=pltpu.HBM)
 
 
 def apply_hamiltonian(place, region_bounds, occupation, orbital, potential):
@@ -240,7 +240,7 @@
     return pl.pallas_call(
         hamiltonian_kernel,
         out_shape=(side, side, grid),
-        in_specs=[smem()] * 2 + [anywhere()] * len(far),
+        in_specs=[smem()] * 2 + [far_away()] * len(far),
         out_specs=(vmem(),) * 3,
         scratch_shapes=[pltpu.VMEM(values.shape, values.dtype) for values in far]
         + [
@@ -330,7 +330,7 @@
             jax.ShapeDtypeStruct((size // ROWS, (size // LANES + 1) * ROWS, LANES), jnp.float32),
         ),
         in_specs=[smem(), vmem()],
-        out_specs=(anywhere(), vmem()),
+        out_specs=(far_away(), vmem()),
         scratch_shapes=[
             pltpu.VMEM((planes, size, lanes), jnp.float32),
             pltpu.SemaphoreType.DMA,
@@ -372,27 +372,35 @@
                 else None
                 for g in range(groups)
             ]
-            scales = jnp.ones((ROWS, LANES), jnp.float32)
-            for j in range(ROWS):
-                pivot = row_of(spread[q][j], j)
+            for j in range(0, ROWS, 2):
+                first, second = spread[q][j], spread[q][j + 1]
+                pivot, side, corner = row_of(first, j), row_of(first, j + 1), row_of(second, j + 1)
                 root = lax.rsqrt(pivot)
-                scales = jnp.where(sub == j, root, scales)
-                weight = {}
+                lower = side * root
+                root2 = lax.rsqrt(pivot * corner - side * side) * (pivot * root)
+                weight, weight2 = {}, {}
                 for g in range(q, groups):
-                    below = spread[g][j]
+                    below, below2 = spread[g][j], spread[g][j + 1]
                     if g == q:
-                        below = jnp.where(sub > j, below, 0.0)
+                        below = jnp.where(sub > j + 1, below, 0.0)
+                        below2 = jnp.where(sub > j + 1, below2, 0.0)
                     weight[g] = below * root
-                for m in range(j + 1, ROWS):
-                    top = row_of(spread[q][m], j) * root
+                    weight2[g] = (below2 - weight[g] * lower) * root2
+
+                def tops(tile):
+                    top = row_of(tile, j) * root
+                    return top, (row_of(tile, j + 1) - lower * top) * root2
+
+                for m in range(j + 2, ROWS):
+                    top, top2 = tops(spread[q][m])
                     for g in range(q, groups):
-                        spread[g][m] = spread[g][m] - weight[g] * top
+                        spread[g][m] = spread[g][m] - weight[g] * top - weight2[g] * top2
                 for c in lanes:
-                    top = row_of(tiles[q][c], j) * root
+                    top, top2 = tops(tiles[q][c])
                     for g in range(q, groups):
-                        tiles[g][c] = tiles[g][c] - weight[g] * top
-            for c in lanes:
-                tiles[q][c] = tiles[q][c] * scales
+                        tiles[g][c] = tiles[g][c] - weight[g] * top - weight2[g] * top2
+                    here = jnp.where(sub == j + 1, top2, tiles[q][c])
+                    tiles[q][c] = jnp.where(sub == j, top, here)
         for g in range(groups):
             for c in lanes:
                 work[start + g * ROWS : start + (g + 1) * ROWS, c : c + LANES] = tiles[g][c]
@@ -439,8 +447,11 @@
     row = lax.broadcasted_iota(jnp.int32, (size, size), 0)
     column = lax.broadcasted_iota(jnp.int32, (size, size), 1)
     turned = packed.T
-    work[:, :size] = jnp.where(row <= column, packed, turned)
-    work[:, size:] = jnp.where(row == column, 1.0, 0.0)
+    on_diagonal = jnp.where(row == column, packed, 0.0)
+    scale = lax.rsqrt(jnp.sum(on_diagonal, axis=0, keepdims=True))
+    scale_down = lax.rsqrt(jnp.sum(on_diagonal, axis=1, keepdims=True))
+    work[:, :size] = jnp.where(row <= column, packed, turned) * scale_down * scale
+    work[:, size:] = jnp.where(row == column, scale, 0.0)
     hamilton = jnp.where(row > column, packed, jnp.where(row == column, diagonal, turned))
     eliminate(work)
     inverse = jnp.where(row >= column, work[:, size:], 0.0)
@@ -482,8 +493,8 @@
             jax.ShapeDtypeStruct((planes * size, lanes), jnp.float32),
             jax.ShapeDtypeStruct((size, size), jnp.float32),
         ),
-        in_specs=[vmem(), anywhere()],
-        out_specs=(anywhere(), vmem()),
+        in_specs=[vmem(), far_away()],
+        out_specs=(far_away(), vmem()),
         scratch_shapes=[
             pltpu.VMEM((size, 2 * size), jnp.float32),
             pltpu.VMEM(natural.shape, jnp.float32),
@@ -528,7 +539,7 @@
         assemble_kernel,
         out_shape=(out, out),
         in_specs=[smem(), vmem(), vmem()],
-        out_specs=(anywhere(), anywhere()),
+        out_specs=(far_away(), far_away()),
         scratch_shapes=[
             pltpu.VMEM((4, blocks, ROWS, lanes), jnp.float32),
             pltpu.SemaphoreType.DMA((4,)),

time: 219 us -> 219 us (level)
  no operation moved by 1% of the time
where the time goes in v3:
time: 219 us; the launch traced here: 218 us
  waiting for transfers between devices  92.2 us (42%)
  blocking collectives  43.4 us (20%)
  starting transfers between devices  37.2 us (17%)
  Pallas kernels  29.3 us (13%)
  local copies, waits for them, and re-layouts  12.2 us (6%)
  other arithmetic  2.95 us (1%)
    all_to_all x2, waiting for transfers between devices, exchange(): lax.all_to_all(blocks, axes, split_axis=0, concat_axis=0, tiled=True, axi...  74 us
    all_to_all x3, blocking collectives, exchange(): lax.all_to_all(blocks, axes, split_axis=0, concat_axis=0, tiled=True, axi...  43.4 us
    all_to_all x2, starting transfers between devices, exchange(): lax.all_to_all(blocks, axes, split_axis=0, concat_axis=0, tiled=True, axi...  20 us
    pallas_call x1, Pallas kernels, solve(): pl.pallas_call(functools.partial(solve_kernel, cells), out_shape=(jax.Sha...  15.8 us
    ppermute x7, waiting for transfers between devices, stage(): lax.ppermute(lax.dynamic_index_in_dim(values, (index + k) % count, dim, k...  14 us
    ppermute x7, starting transfers between devices, stage(): lax.ppermute(lax.dynamic_index_in_dim(values, (index + k) % count, dim, k...  9.65 us
    unnamed x20, local copies, waits for them, and re-layouts  9.42 us
    pallas_call x1, Pallas kernels, apply_hamiltonian(): pl.pallas_call(hamiltonian_kernel, out_shape=(side, side, grid), in_specs...  8.65 us
  transfers between devices with their start and end apart: 11, of which 8 were waited for; matrix products, arithmetic and copies ran while one was open for 1% of the time, Pallas kernels for 0%

profile of v3, /device:TPU:1, one launch (start us, length us, event | category | flops | bytes accessed | tf_op | source)
XLA Modules:
  0.0 218.2 jit_solution(7656738409045779152)
XLA Ops:
  1.5 1.8 copy.15.potential_hbm
  7.5 8.7 %hamiltonian.1 = (f32[128,16,128]{2,1,0:T(8,128)S(1)}, f32[128,16,128]{2,1,0:T(8,128)S(1)}, f32[64,32,128]{2,1,0:T(8,128)S(1)}) custom-call(s32[2]{0:T(128)S(1)} %pad_add_fusion.place_ref, f32[256]{0:T(256)S(1)} %copy-done.2, s32[256,2]{1,0:T(8,128)S(1)} %copy.14.bounds_hbm, f32[64,32,128]{2,1,0:T(8,128)S(1)} %bitcast.43, bf16[640,256]{1,0:T(8,128)(2,1)S(1)} %copy-done.4, ...), custom_call_target="tpu_custom_call" | custom-call | flops 3019898880 | bytes 5242880 | tf_op jit(solution)/shard_map/hamiltonian/pallas_call | solution.py:240
  16.2 3.3 %collective-permute-start = (f32[128,16,128]{2,1,0:T(8,128)S(1)}, f32[128,16,128]{2,1,0:T(8,128)S(1)}, u32[]{:S(2)}, u32[]{:S(2)}) collective-permute-start(f32[128,16,128]{2,1,0:T(8,128)S(1)} %get-tuple-element.16), channel_id=1, source_target_pairs={{0,4},{4,0},{8,12},{12,8},{16,20},{20,16},{24,28},{28,24},{32,36},... | collective-permute-start | bytes 3145736 | tf_op jit(solution)/shard_map/ppermute | solution.py:610
  19.5 2.3 %collective-permute-done = f32[128,16,128]{2,1,0:T(8,128)S(1)} collective-permute-done((f32[128,16,128]{2,1,0:T(8,128)S(1)}, f32[128,16,128]{2,1,0:T(8,128)S(1)}, u32[]{:S(2)}, u32[]{:S(2)}) %collective-permute-start) | collective-permute-done | bytes 1048608 | tf_op jit(solution)/shard_map/ppermute | solution.py:610
  21.8 1.6 pad_maximum_fusion
  23.5 13.8 %all-to-all-start = ((f32[128,32,128]{2,1,0:T(8,128)}), f32[128,32,128]{2,1,0:T(8,128)S(1)}, u32[]{:S(2)}, u32[]{:S(2)}) async-start(f32[128,32,128]{2,1,0:T(8,128)} %pad_maximum_fusion), calls=%async_computation | async-start | bytes 4194304 | tf_op jit(solution)/shard_map/all_to_all | solution.py:554
  38.8 1.9 collective-permute-done.1
  42.8 2.4 %collective-permute-start.3 = (f32[8,4,8,128]{3,2,0,1:T(8,128)S(1)}, f32[8,4,8,128]{3,2,0,1:T(8,128)S(1)}, u32[]{:S(2)}, u32[]{:S(2)}) collective-permute-start(f32[8,4,8,128]{3,2,0,1:T(8,128)S(1)} %bitcast.45), channel_id=1, source_target_pairs={{0,2},{1,3},{2,0},{3,1},{4,6},{5,7},{6,4},{7,5},{8,10},{9,11},{10,... | collective-permute-start | bytes 393224 | tf_op jit(solution)/shard_map/ppermute | solution.py:622
  46.4 3.1 %collective-permute-done.2 = f32[8,4,8,128]{3,2,0,1:T(8,128)S(1)} collective-permute-done((f32[8,4,8,128]{3,2,0,1:T(8,128)S(1)}, f32[8,4,8,128]{3,2,0,1:T(8,128)S(1)}, u32[]{:S(2)}, u32[]{:S(2)}) %collective-permute-start.2) | collective-permute-done | bytes 131104 | tf_op jit(solution)/shard_map/ppermute | solution.py:622
  49.5 5.8 %collective-permute-done.3 = f32[8,4,8,128]{3,2,0,1:T(8,128)S(1)} collective-permute-done((f32[8,4,8,128]{3,2,0,1:T(8,128)S(1)}, f32[8,4,8,128]{3,2,0,1:T(8,128)S(1)}, u32[]{:S(2)}, u32[]{:S(2)}) %collective-permute-start.3) | collective-permute-done | bytes 131104 | tf_op jit(solution)/shard_map/ppermute | solution.py:622
  56.0 2.1 collective-permute-start.7
  58.1 1.7 collective-permute-start.6
  59.9 3.2 %collective-permute-done.6 = f32[8,8,128]{2,1,0:T(8,128)S(1)} collective-permute-done((f32[8,8,128]{2,1,0:T(8,128)S(1)}, f32[8,8,128]{2,1,0:T(8,128)S(1)}, u32[]{:S(2)}, u32[]{:S(2)}) %collective-permute-start.6) | collective-permute-done | bytes 32800 | tf_op jit(solution)/shard_map/ppermute | solution.py:622
  63.1 24.2 %all-to-all-done = f32[128,32,128]{2,1,0:T(8,128)S(1)} async-done(((f32[128,32,128]{2,1,0:T(8,128)}), f32[128,32,128]{2,1,0:T(8,128)S(1)}, u32[]{:S(2)}, u32[]{:S(2)}) %all-to-all-start) | async-done | bytes 2097184 | tf_op jit(solution)/shard_map/all_to_all | solution.py:554
  87.4 3.4 %overlap.1 = (f32[16,256,128]{2,1,0:T(8,128)S(1)}, f32[32,24,128]{2,1,0:T(8,128)S(1)}) custom-call(s32[1]{0:T(128)} %bitcast.core_ref, f32[4096,128]{1,0:T(8,128)S(1)} %bitcast.39), custom_call_target="tpu_custom_call" | custom-call | flops 1610612736 | bytes 4194304 | tf_op jit(solution)/shard_map/overlap/pallas_call | solution.py:326
  92.1 17.4 %all_to_all.25 = f32[32,24,128]{2,1,0:T(8,128)S(1)} all-to-all(f32[32,24,128]{2,1,0:T(8,128)S(1)} %get-tuple-element.19), channel_id=1, replica_groups={{0,1,2,3,4,5,6,7,8,9,10,11,12,13,14,15,16,17,18,19,20,21,22,23,24,25,26..., dimensions={0} | all-to-all | bytes 786432 | tf_op jit(solution)/shard_map/all_to_all | solution.py:554
  109.6 10.4 %all_to_all.26 = f32[8,32,128]{2,1,0:T(8,128)S(1)} all-to-all(f32[8,32,128]{2,1,0:T(8,128)S(1)} %pad_maximum_fusion.1), channel_id=1, replica_groups={{0,32,64,96,128,160,192,224},{4,36,68,100,132,164,196,228},{8,40,72,104..., dimensions={0} | all-to-all | bytes 262144 | tf_op jit(solution)/shard_map/all_to_all | solution.py:554
  120.0 15.6 %all_to_all.27.summed_ref = f32[32,24,128]{2,1,0:T(8,128)S(1)} all-to-all(f32[32,24,128]{2,1,0:T(8,128)S(1)} %broadcast_in_dim.5), channel_id=1, replica_groups={{0,1,2,3,4,5,6,7,8,9,10,11,12,13,14,15,16,17,18,19,20,21,22,23,24,25,26..., dimensions={0} | all-to-all | bytes 786432 | tf_op jit(solution)/shard_map/all_to_all | solution.py:554
  135.6 15.8 %solve.1 = (f32[4096,128]{1,0:T(8,128)S(1)}, f32[256,256]{1,0:T(8,128)}) custom-call(f32[32,24,128]{2,1,0:T(8,128)S(1)} %all_to_all.27.summed_ref, f32[16,256,128]{2,1,0:T(8,128)S(1)} %copy-done.8), custom_call_target="tpu_custom_call" | custom-call | flops 20000000000 | bytes 6291456 | tf_op jit(solution)/shard_map/solve/pallas_call | solution.py:490
  152.8 6.2 %all-to-all-start.4 = ((f32[128,32,128]{2,1,0:T(8,128)}), f32[128,32,128]{2,1,0:T(8,128)S(1)}, u32[]{:S(2)}, u32[]{:S(2)}) async-start(f32[128,32,128]{2,1,0:T(8,128)} %bitcast.40), calls=%async_computation.4 | async-start | bytes 4194304 | tf_op jit(solution)/shard_map/all_to_all | solution.py:554
  159.0 49.8 %all-to-all-done.4.arrived_ref = f32[128,32,128]{2,1,0:T(8,128)S(1)} async-done(((f32[128,32,128]{2,1,0:T(8,128)}), f32[128,32,128]{2,1,0:T(8,128)S(1)}, u32[]{:S(2)}, u32[]{:S(2)}) %all-to-all-start.4) | async-done | bytes 2097184 | tf_op jit(solution)/shard_map/all_to_all | solution.py:554
  209.9 4.2 %collective-permute-start.8 = (f32[128,16,128]{2,1,0:T(8,128)}, f32[128,16,128]{2,1,0:T(8,128)S(1)}, u32[]{:S(2)}, u32[]{:S(2)}) collective-permute-start(f32[128,16,128]{2,1,0:T(8,128)} %constant_dynamic-slice_fusion), channel_id=1, source_target_pairs={{0,4},{4,0},{8,12},{12,8},{16,20},{20,16},{24,28},{28,24},{32,36},... | collective-permute-start | bytes 3145736 | tf_op jit(solution)/shard_map/ppermute | solution.py:610
  214.8 1.8 collective-permute-done.8.received_ref
  216.6 1.4 assemble.1
  (45 shorter events, 15.1 us)
Async XLA Ops:
  0.6 2.8 %copy-start.5 = (bf16[640,128]{1,0:T(8,128)(2,1)S(1)}, bf16[640,128]{1,0:T(8,128)(2,1)}, u32[]{:S(2)}) copy-start(bf16[640,128]{1,0:T(8,128)(2,1)} %constant.120.clone.magic_low_hbm) | copy-start | bytes 491524
  0.6 2.8 %copy-start.2 = (f32[256]{0:T(256)S(1)}, f32[256]{0:T(256)}, u32[]{:S(2)}) copy-start(f32[256]{0:T(256)} %occupation_ref.1) | copy-start | bytes 3076
  3.4 1.2 copy-start.1
  4.7 1.0 copy-start.3
  5.6 1.0 copy-start.4
  6.6 0.9 copy-start.6
  16.2 5.6 %collective-permute-start = (f32[128,16,128]{2,1,0:T(8,128)S(1)}, f32[128,16,128]{2,1,0:T(8,128)S(1)}, u32[]{:S(2)}, u32[]{:S(2)}) collective-permute-start(f32[128,16,128]{2,1,0:T(8,128)S(1)} %get-tuple-element.16), channel_id=1, source_target_pairs={{0,4},{4,0},{8,12},{12,8},{16,20},{20,16},{24,28},{28,24},{32,36},... | collective-permute-start | bytes 3145736 | tf_op jit(solution)/shard_map/ppermute | solution.py:610
  23.5 63.9 %all-to-all-start = ((f32[128,32,128]{2,1,0:T(8,128)}), f32[128,32,128]{2,1,0:T(8,128)S(1)}, u32[]{:S(2)}, u32[]{:S(2)}) async-start(f32[128,32,128]{2,1,0:T(8,128)} %pad_maximum_fusion), calls=%async_computation | async-start | bytes 4194304 | tf_op jit(solution)/shard_map/all_to_all | solution.py:554
  38.1 2.5 %collective-permute-start.1 = (f32[8,4,4,8,128]{4,3,2,1,0:T(8,128)}, f32[8,4,4,8,128]{4,3,2,1,0:T(8,128)}, u32[]{:S(2)}, u32[]{:S(2)}) collective-permute-start(f32[8,4,4,8,128]{4,3,2,1,0:T(8,128)} %dynamic-slice_bitcast_fusion), channel_id=1, source_target_pairs={{0,4},{4,0},{8,12},{12,8},{16,20},{20,16},{24,28},{28,24},{32,36},... | collective-permute-start | bytes 1572872 | tf_op jit(solution)/shard_map/ppermute | solution.py:622
  41.9 7.6 %collective-permute-start.2 = (f32[8,4,8,128]{3,2,0,1:T(8,128)S(1)}, f32[8,4,8,128]{3,2,0,1:T(8,128)S(1)}, u32[]{:S(2)}, u32[]{:S(2)}) collective-permute-start(f32[8,4,8,128]{3,2,0,1:T(8,128)S(1)} %bitcast.46), channel_id=1, source_target_pairs={{0,1},{1,2},{2,3},{3,0},{4,5},{5,6},{6,7},{7,4},{8,9},{9,10},{10,1... | collective-permute-start | bytes 393224 | tf_op jit(solution)/shard_map/ppermute | solution.py:622
  42.8 12.5 %collective-permute-start.3 = (f32[8,4,8,128]{3,2,0,1:T(8,128)S(1)}, f32[8,4,8,128]{3,2,0,1:T(8,128)S(1)}, u32[]{:S(2)}, u32[]{:S(2)}) collective-permute-start(f32[8,4,8,128]{3,2,0,1:T(8,128)S(1)} %bitcast.45), channel_id=1, source_target_pairs={{0,2},{1,3},{2,0},{3,1},{4,6},{5,7},{6,4},{7,5},{8,10},{9,11},{10,... | collective-permute-start | bytes 393224 | tf_op jit(solution)/shard_map/ppermute | solution.py:622
  45.2 10.1 %collective-permute-start.4 = (f32[8,4,8,128]{3,2,0,1:T(8,128)S(1)}, f32[8,4,8,128]{3,2,0,1:T(8,128)S(1)}, u32[]{:S(2)}, u32[]{:S(2)}) collective-permute-start(f32[8,4,8,128]{3,2,0,1:T(8,128)S(1)} %bitcast.44), channel_id=1, source_target_pairs={{0,3},{1,0},{2,1},{3,2},{4,7},{5,4},{6,5},{7,6},{8,11},{9,8},{10,9... | collective-permute-start | bytes 393224 | tf_op jit(solution)/shard_map/ppermute | solution.py:622
  55.4 4.5 %collective-permute-start.5 = (f32[8,8,128]{2,1,0:T(8,128)S(1)}, f32[8,8,128]{2,1,0:T(8,128)S(1)}, u32[]{:S(2)}, u32[]{:S(2)}) collective-permute-start(f32[8,8,128]{2,1,0:T(8,128)S(1)} %get-tuple-element.30), channel_id=1, source_target_pairs={{0,8},{4,12},{8,16},{12,20},{16,24},{20,28},{24,0},{28,4},{32,40},... | collective-permute-start | bytes 98312 | tf_op jit(solution)/shard_map/ppermute | solution.py:622
  56.0 3.8 %collective-permute-start.7 = (f32[8,8,128]{2,1,0:T(8,128)S(1)}, f32[8,8,128]{2,1,0:T(8,128)S(1)}, u32[]{:S(2)}, u32[]{:S(2)}) collective-permute-start(f32[8,8,128]{2,1,0:T(8,128)S(1)} %get-tuple-element.31), channel_id=1, source_target_pairs={{0,24},{4,28},{8,0},{12,4},{16,8},{20,12},{24,16},{28,20},{32,56},... | collective-permute-start | bytes 98312 | tf_op jit(solution)/shard_map/ppermute | solution.py:622
  58.1 5.0 %collective-permute-start.6 = (f32[8,8,128]{2,1,0:T(8,128)S(1)}, f32[8,8,128]{2,1,0:T(8,128)S(1)}, u32[]{:S(2)}, u32[]{:S(2)}) collective-permute-start(f32[8,8,128]{2,1,0:T(8,128)S(1)} %get-tuple-element.32), channel_id=1, source_target_pairs={{0,16},{4,20},{8,24},{12,28},{16,0},{20,4},{24,8},{28,12},{32,48},... | collective-permute-start | bytes 98312 | tf_op jit(solution)/shard_map/ppermute | solution.py:622
  90.8 1.3 copy-start.7
  92.1 43.5 %copy-start.8 = (f32[16,256,128]{2,1,0:T(8,128)S(1)}, f32[16,256,128]{2,1,0:T(8,128)}, u32[]{:S(2)}) copy-start(f32[16,256,128]{2,1,0:T(8,128)} %copy-done.7) | copy-start | bytes 6291460
  151.4 1.3 copy-start
  152.8 56.0 %all-to-all-start.4 = ((f32[128,32,128]{2,1,0:T(8,128)}), f32[128,32,128]{2,1,0:T(8,128)S(1)}, u32[]{:S(2)}, u32[]{:S(2)}) async-start(f32[128,32,128]{2,1,0:T(8,128)} %bitcast.40), calls=%async_computation.4 | async-start | bytes 4194304 | tf_op jit(solution)/shard_map/all_to_all | solution.py:554
  209.9 6.7 %collective-permute-start.8 = (f32[128,16,128]{2,1,0:T(8,128)}, f32[128,16,128]{2,1,0:T(8,128)S(1)}, u32[]{:S(2)}, u32[]{:S(2)}) collective-permute-start(f32[128,16,128]{2,1,0:T(8,128)} %constant_dynamic-slice_fusion), channel_id=1, source_target_pairs={{0,4},{4,0},{8,12},{12,8},{16,20},{20,16},{24,28},{28,24},{32,36},... | collective-permute-start | bytes 3145736 | tf_op jit(solution)/shard_map/ppermute | solution.py:610

commit v4 on v3

--- a/solution.py
+++ b/solution.py
@@ -17,6 +17,7 @@
 STRIP = 16
 ROWS = 8
 BLOCK = 64
+MOST_VMEM = 60 * 2**20
 
 magic_taps = (0.0028, -0.0236, 0.1026, 0.8364, 0.1026, -0.0236, 0.0028)
 kinetic_taps = (
@@ -91,9 +92,9 @@
     potential_hbm,
     magic_high_hbm,
     magic_low_hbm,
-    keep_ref,
-    give_ref,
-    density_ref,
+    keep_hbm,
+    give_hbm,
+    density_hbm,
     bounds_ref,
     orbital_ref,
     both_high_ref,
@@ -104,7 +105,12 @@
     source,
     filtered,
     kinetic,
+    lines_ref,
+    keep_ref,
+    give_ref,
+    density_ref,
     sems,
+    out_sems,
 ):
     margin = len(kinetic_taps) // 2
     position, core = place_ref[0], place_ref[1]
@@ -159,8 +165,10 @@
     copies[0].wait()
     copies[1].wait()
     planes = lax.broadcasted_iota(jnp.int32, (STRIP * PAIRS, LANES), 0) // PAIRS
-    bounds = bounds_ref[pl.ds(position, 1), :]
-    begin, end = bounds[:, 0:1], bounds[:, 1:2]
+    bounds = bounds_ref[...]
+    own_place = lax.broadcasted_iota(jnp.int32, bounds.shape, 1) == position
+    bounds = jnp.sum(jnp.where(own_place, bounds, 0), axis=1, keepdims=True)
+    begin, end = bounds[0:1], bounds[1:2]
     blocks = STRIP * PAIRS // ROWS
     half_planes = G // 2
 
@@ -177,18 +185,19 @@
             first = strip * PAIRS // ROWS
             out_ref[first : first + blocks, :ROWS, :] = tiled(masked)
 
-    copies[2].wait()
-    copies[3].wait()
+    for copy in copies[2:5]:
+        copy.wait()
 
     @pl.loop(0, G, step=STRIP)
     def _(x):
+        cells = pl.ds(pl.multiple_of(x * G, STRIP * G), STRIP * G)
+        lines_ref[cells, :] = potential_ref[:, cells].T
         both = product(x, both_high_ref, both_low_ref)
         filtered[pl.ds(margin + x, STRIP)] = both[:, :LANES].reshape(STRIP, PAIRS, LANES)
         kinetic[pl.ds(x, STRIP)] = both[:, LANES:].reshape(STRIP, PAIRS, LANES) + plane_filter(
             own, x, kinetic_taps
         )
 
-    copies[4].wait()
     scale = occupation_ref[position] * (1.0 / occupation_ref.shape[0])
     lines = STRIP * G // 2
 
@@ -197,10 +206,12 @@
         realspace = plane_filter(half, x, magic_taps)
         density_ref[pl.ds(x, STRIP)] = scale * realspace * realspace
         potential = jnp.concatenate(
-            [potential_ref[pl.ds(x * G + odd, lines, stride=2), :] for odd in range(2)], axis=1
+            [lines_ref[pl.ds(x * G + odd, lines, stride=2), :] for odd in range(2)], axis=1
         ).reshape(STRIP, PAIRS, LANES)
         source[pl.ds(margin + x, STRIP), PAD : PAD + PAIRS] = realspace * potential
 
+    density_out = pltpu.make_async_copy(density_ref, density_hbm, out_sems.at[4])
+    density_out.start()
     copies[5].wait()
     copies[6].wait()
 
@@ -210,12 +221,21 @@
             STRIP, PAIRS, LANES
         )
 
-    for side, out_ref in ((core, keep_ref), (1 - core, give_ref)):
+    done = [density_out]
+    for side, out_ref, out_hbm in ((core, keep_ref, keep_hbm), (1 - core, give_ref, give_hbm)):
         for strip in range(0, half_planes, STRIP):
             x = half_planes * side + strip
             images = plane_filter(half, x, magic_taps) - 0.5 * kinetic[pl.ds(x, STRIP)]
             first = strip * PAIRS // ROWS
             out_ref[first : first + blocks, ROWS:, :] = tiled(images)
+            here = pl.ds(first, blocks)
+            copy = pltpu.make_async_copy(
+                out_ref.at[here], out_hbm.at[here], out_sems.at[len(done) - 1]
+            )
+            copy.start()
+            done.append(copy)
+    for copy in done:
+        copy.wait()
 
 
 def vmem():
@@ -235,21 +255,26 @@
     margin = len(kinetic_taps) // 2
     side = jax.ShapeDtypeStruct((G * PAIRS // ROWS // 2, 2 * ROWS, LANES), jnp.float32)
     grid = jax.ShapeDtypeStruct((G, PAIRS, LANES), jnp.float32)
-    far = (region_bounds, orbital, both_high, both_low, potential, magic_high, magic_low)
+    far = (region_bounds.T, orbital, both_high, both_low, potential.T, magic_high, magic_low)
     far = [jnp.asarray(values) for values in far]
     return pl.pallas_call(
         hamiltonian_kernel,
         out_shape=(side, side, grid),
         in_specs=[smem()] * 2 + [far_away()] * len(far),
-        out_specs=(vmem(),) * 3,
+        out_specs=(far_away(),) * 3,
         scratch_shapes=[pltpu.VMEM(values.shape, values.dtype) for values in far]
         + [
             pltpu.VMEM((G + 2 * margin, PAIRS + 2 * PAD, LANES), jnp.float32),
             pltpu.VMEM((G + 2 * margin, PAIRS, LANES), jnp.float32),
             pltpu.VMEM((G, PAIRS, LANES), jnp.float32),
+            pltpu.VMEM((G * G, G), jnp.float32),
+            pltpu.VMEM(side.shape, side.dtype),
+            pltpu.VMEM(side.shape, side.dtype),
+            pltpu.VMEM(grid.shape, grid.dtype),
             pltpu.SemaphoreType.DMA((len(far),)),
+            pltpu.SemaphoreType.DMA((5,)),
         ],
-        compiler_params=pltpu.CompilerParams(vmem_limit_bytes=40 * 2**20),
+        compiler_params=pltpu.CompilerParams(vmem_limit_bytes=MOST_VMEM),
         cost_estimate=pl.CostEstimate(
             flops=6 * 2048 * 640 * 384, bytes_accessed=5 * 2**20, transcendentals=0
         ),
@@ -264,6 +289,7 @@
 
 
 CORES = 2
+PARTS = 4
 LINES = 4
 
 
@@ -284,14 +310,25 @@
                     flat_ref[inner, :] = natural_ref[plane, outer, :]
 
 
-def overlap_kernel(core_ref, flat_ref, natural_hbm, packed_ref, natural_ref, sem):
-    for core in range(CORES):
-
-        @pl.when(core_ref[0] == core)
-        def _(core=core):
-            natural_rows(flat_ref, natural_ref, core, True)
-
-    copy = pltpu.make_async_copy(natural_ref, natural_hbm, sem)
+def overlap_kernel(
+    core_ref, flat_hbm, natural_hbm, packed_ref, flat_ref, natural_ref, in_sems, out_sem
+):
+    rows = flat_ref.shape[0] // PARTS
+    arrivals = []
+    for part in range(PARTS):
+        here = pl.ds(part * rows, rows)
+        copy = pltpu.make_async_copy(flat_hbm.at[here], flat_ref.at[here], in_sems.at[part])
+        copy.start()
+        arrivals.append(copy)
+    for part in range(PARTS):
+        arrivals[part].wait()
+        for core in range(CORES):
+
+            @pl.when(core_ref[0] == core)
+            def _(core=core, part=part):
+                natural_rows(flat_ref, natural_ref, core, True, part, PARTS)
+
+    copy = pltpu.make_async_copy(natural_ref, natural_hbm, out_sem)
     copy.start()
     planes, size, _ = natural_ref.shape
     half = planes // 2
@@ -329,13 +366,15 @@
             jax.ShapeDtypeStruct((planes, size, lanes), jnp.float32),
             jax.ShapeDtypeStruct((size // ROWS, (size // LANES + 1) * ROWS, LANES), jnp.float32),
         ),
-        in_specs=[smem(), vmem()],
+        in_specs=[smem(), far_away()],
         out_specs=(far_away(), vmem()),
         scratch_shapes=[
+            pltpu.VMEM((rows, lanes), jnp.float32),
             pltpu.VMEM((planes, size, lanes), jnp.float32),
+            pltpu.SemaphoreType.DMA((PARTS,)),
             pltpu.SemaphoreType.DMA,
         ],
-        compiler_params=pltpu.CompilerParams(vmem_limit_bytes=40 * 2**20),
+        compiler_params=pltpu.CompilerParams(vmem_limit_bytes=MOST_VMEM),
         cost_estimate=pl.CostEstimate(
             flops=24 * 256 * 256 * 1024, bytes_accessed=4 * 2**20, transcendentals=0
         ),
@@ -472,11 +511,10 @@
         for k, part in enumerate(both):
             mixed[plane + k] = part[:, :LANES]
             mixed[half + plane + k] = part[:, LANES:] - product[:, k * LANES : (k + 1) * LANES]
-    parts = 4
-    rows = flat_ref.shape[0] // parts
+    rows = flat_ref.shape[0] // PARTS
     copies = []
-    for part in range(parts):
-        natural_rows(flat_ref, mixed, 0, False, part, parts)
+    for part in range(PARTS):
+        natural_rows(flat_ref, mixed, 0, False, part, PARTS)
         here = pl.ds(part * rows, rows)
         copy = pltpu.make_async_copy(flat_ref.at[here], flat_hbm.at[here], out_sems.at[part])
         copy.start()
@@ -501,9 +539,9 @@
             pltpu.VMEM(natural.shape, jnp.float32),
             pltpu.VMEM((planes * size, lanes), jnp.float32),
             pltpu.SemaphoreType.DMA,
-            pltpu.SemaphoreType.DMA((4,)),
+            pltpu.SemaphoreType.DMA((PARTS,)),
         ],
-        compiler_params=pltpu.CompilerParams(vmem_limit_bytes=48 * 2**20),
+        compiler_params=pltpu.CompilerParams(vmem_limit_bytes=MOST_VMEM),
         cost_estimate=pl.CostEstimate(
             flops=20_000_000_000, bytes_accessed=6 * 2**20, transcendentals=256
         ),
@@ -673,13 +711,14 @@
     summed, density = sum_everywhere(packed, slabs, layout)
     mixed, subspace = solve(summed, natural, cell_total)
     back = exchange(mixed.reshape(-1, 4 * ROWS, LANES), layout.chips())
+    back, density = lax.optimization_barrier((back, density.reshape(-1, G)))
     other = lax.dynamic_slice_in_dim(back, (1 - core[0]) * 2 * ROWS, 2 * ROWS, 1)
     orthonormal, gradient = assemble(core, back, layout.swap_cores(other))
     return (
         orthonormal.reshape(1, cell_total),
         gradient.reshape(1, cell_total),
         subspace,
-        density.reshape(-1, G),
+        density,
     )
 
 

time: 219 us -> 217 us (level)
  local copies, waits for them, and re-layouts: 12.2 us -> 3.1 us
  Pallas kernels: 29.3 us -> 34.8 us
    unnamed x20 -> x4, local copies, waits for them, and re-layouts: 9.42 us -> 1.32 us
where the time goes in v4:
time: 217 us
  waiting for transfers between devices  92.2 us (42%)
  blocking collectives  43.6 us (20%)
  starting transfers between devices  37.4 us (17%)
  Pallas kernels  34.8 us (16%)
  other arithmetic  4.69 us (2%)
  local copies, waits for them, and re-layouts  3.1 us (1%)
    all_to_all x2, waiting for transfers between devices, exchange(): lax.all_to_all(blocks, axes, split_axis=0, concat_axis=0, tiled=True, axi...  73.3 us
    all_to_all x3, blocking collectives, exchange(): lax.all_to_all(blocks, axes, split_axis=0, concat_axis=0, tiled=True, axi...  43.6 us
    all_to_all x2, starting transfers between devices, exchange(): lax.all_to_all(blocks, axes, split_axis=0, concat_axis=0, tiled=True, axi...  20.1 us
    pallas_call x1, Pallas kernels, solve(): pl.pallas_call(functools.partial(solve_kernel, cells), out_shape=(jax.Sha...  17.9 us
    ppermute x7, waiting for transfers between devices, stage(): lax.ppermute(lax.dynamic_index_in_dim(values, (index + k) % count, dim, k...  14 us
    pallas_call x1, Pallas kernels, apply_hamiltonian(): pl.pallas_call(hamiltonian_kernel, out_shape=(side, side, grid), in_specs...  10.3 us
    ppermute x7, starting transfers between devices, stage(): lax.ppermute(lax.dynamic_index_in_dim(values, (index + k) % count, dim, k...  9.65 us
    ppermute x2, starting transfers between devices, swap_cores(): return lax.ppermute(values, 'orb', pairs)  7.68 us
  transfers between devices with their start and end apart: 11, of which 8 were waited for; matrix products, arithmetic and copies ran while one was open for 1% of the time, Pallas kernels for 0%

profile of v4, /device:TPU:1, one launch (start us, length us, event | category | flops | bytes accessed | tf_op | source)
XLA Modules:
  0.0 216.8 jit_solution(1953971497370990446)
XLA Ops:
  1.2 10.3 %hamiltonian.1 = (f32[128,16,128]{2,1,0:T(8,128)}, f32[128,16,128]{2,1,0:T(8,128)}, f32[64,32,128]{2,1,0:T(8,128)}) custom-call(s32[2]{0:T(128)} %pad_add_fusion.place_ref, f32[256]{0:T(256)} %occupation_ref.1, s32[2,256]{1,0:T(2,128)} %bitcast.52, f32[64,32,128]{2,1,0:T(8,128)} %bitcast.48, bf16[640,256]{1,0:T(8,128)(2,1)} %constant.117.clone.both_high_hbm, ...), custom_call_target="tpu_custom_call" | custom-call | flops 3019898880 | bytes 5242880 | tf_op jit(solution)/shard_map/hamiltonian/pallas_call | solution.py:260
  11.5 3.3 %collective-permute-start = (f32[128,16,128]{2,1,0:T(8,128)}, f32[128,16,128]{2,1,0:T(8,128)S(1)}, u32[]{:S(2)}, u32[]{:S(2)}) collective-permute-start(f32[128,16,128]{2,1,0:T(8,128)} %get-tuple-element.18), channel_id=1, source_target_pairs={{0,4},{4,0},{8,12},{12,8},{16,20},{20,16},{24,28},{28,24},{32,36},... | collective-permute-start | bytes 3145736 | tf_op jit(solution)/shard_map/ppermute | solution.py:648
  14.9 2.5 %collective-permute-done = f32[128,16,128]{2,1,0:T(8,128)S(1)} collective-permute-done((f32[128,16,128]{2,1,0:T(8,128)}, f32[128,16,128]{2,1,0:T(8,128)S(1)}, u32[]{:S(2)}, u32[]{:S(2)}) %collective-permute-start) | collective-permute-done | bytes 1048608 | tf_op jit(solution)/shard_map/ppermute | solution.py:648
  17.4 2.9 %pad_maximum_fusion = f32[128,32,128]{2,1,0:T(8,128)} fusion(f32[128,16,128]{2,1,0:T(8,128)S(1)} %collective-permute-done, f32[128,16,128]{2,1,0:T(8,128)} %get-tuple-element.17), kind=kLoop, calls=%fused_computation | loop fusion | flops 524288 | bytes 4194304 | tf_op jit(solution)/shard_map/concatenate | solution.py:706
  20.2 13.9 %all-to-all-start = ((f32[128,32,128]{2,1,0:T(8,128)}), f32[128,32,128]{2,1,0:T(8,128)S(1)}, u32[]{:S(2)}, u32[]{:S(2)}) async-start(f32[128,32,128]{2,1,0:T(8,128)} %pad_maximum_fusion), calls=%async_computation | async-start | bytes 4194304 | tf_op jit(solution)/shard_map/all_to_all | solution.py:592
  35.7 1.9 collective-permute-done.1
  39.8 2.4 %collective-permute-start.3 = (f32[8,4,8,128]{3,2,0,1:T(8,128)S(1)}, f32[8,4,8,128]{3,2,0,1:T(8,128)S(1)}, u32[]{:S(2)}, u32[]{:S(2)}) collective-permute-start(f32[8,4,8,128]{3,2,0,1:T(8,128)S(1)} %bitcast.46), channel_id=1, source_target_pairs={{0,2},{1,3},{2,0},{3,1},{4,6},{5,7},{6,4},{7,5},{8,10},{9,11},{10,... | collective-permute-start | bytes 393224 | tf_op jit(solution)/shard_map/ppermute | solution.py:660
  43.3 3.1 %collective-permute-done.2 = f32[8,4,8,128]{3,2,0,1:T(8,128)S(1)} collective-permute-done((f32[8,4,8,128]{3,2,0,1:T(8,128)S(1)}, f32[8,4,8,128]{3,2,0,1:T(8,128)S(1)}, u32[]{:S(2)}, u32[]{:S(2)}) %collective-permute-start.2) | collective-permute-done | bytes 131104 | tf_op jit(solution)/shard_map/ppermute | solution.py:660
  46.4 5.8 %collective-permute-done.3 = f32[8,4,8,128]{3,2,0,1:T(8,128)S(1)} collective-permute-done((f32[8,4,8,128]{3,2,0,1:T(8,128)S(1)}, f32[8,4,8,128]{3,2,0,1:T(8,128)S(1)}, u32[]{:S(2)}, u32[]{:S(2)}) %collective-permute-start.3) | collective-permute-done | bytes 131104 | tf_op jit(solution)/shard_map/ppermute | solution.py:660
  53.0 2.1 collective-permute-start.7
  55.1 1.7 collective-permute-start.6
  56.8 3.2 %collective-permute-done.6 = f32[8,8,128]{2,1,0:T(8,128)S(1)} collective-permute-done((f32[8,8,128]{2,1,0:T(8,128)S(1)}, f32[8,8,128]{2,1,0:T(8,128)S(1)}, u32[]{:S(2)}, u32[]{:S(2)}) %collective-permute-start.6) | collective-permute-done | bytes 32800 | tf_op jit(solution)/shard_map/ppermute | solution.py:660
  60.1 24.2 %all-to-all-done = f32[128,32,128]{2,1,0:T(8,128)S(1)} async-done(((f32[128,32,128]{2,1,0:T(8,128)}), f32[128,32,128]{2,1,0:T(8,128)S(1)}, u32[]{:S(2)}, u32[]{:S(2)}) %all-to-all-start) | async-done | bytes 2097184 | tf_op jit(solution)/shard_map/all_to_all | solution.py:592
  84.3 1.3 copy-done
  85.6 5.3 %overlap.1 = (f32[16,256,128]{2,1,0:T(8,128)}, f32[32,24,128]{2,1,0:T(8,128)}) custom-call(s32[1]{0:T(128)} %bitcast.core_ref, f32[4096,128]{1,0:T(8,128)} %bitcast.41), custom_call_target="tpu_custom_call" | custom-call | flops 1610612736 | bytes 4194304 | tf_op jit(solution)/shard_map/overlap/pallas_call | solution.py:363
  90.9 17.5 %all_to_all.25 = f32[32,24,128]{2,1,0:T(8,128)S(1)} all-to-all(f32[32,24,128]{2,1,0:T(8,128)} %get-tuple-element.21), channel_id=1, replica_groups={{0,1,2,3,4,5,6,7,8,9,10,11,12,13,14,15,16,17,18,19,20,21,22,23,24,25,26..., dimensions={0} | all-to-all | bytes 786432 | tf_op jit(solution)/shard_map/all_to_all | solution.py:592
  108.5 10.3 %all_to_all.26 = f32[8,32,128]{2,1,0:T(8,128)S(1)} all-to-all(f32[8,32,128]{2,1,0:T(8,128)S(1)} %pad_maximum_fusion.1), channel_id=1, replica_groups={{0,32,64,96,128,160,192,224},{4,36,68,100,132,164,196,228},{8,40,72,104..., dimensions={0} | all-to-all | bytes 262144 | tf_op jit(solution)/shard_map/all_to_all | solution.py:592
  118.9 15.8 %all_to_all.27.summed_ref = f32[32,24,128]{2,1,0:T(8,128)} all-to-all(f32[32,24,128]{2,1,0:T(8,128)S(1)} %broadcast_in_dim.5), channel_id=1, replica_groups={{0,1,2,3,4,5,6,7,8,9,10,11,12,13,14,15,16,17,18,19,20,21,22,23,24,25,26..., dimensions={0} | all-to-all | bytes 786432 | tf_op jit(solution)/shard_map/all_to_all | solution.py:592
  134.6 17.9 %solve.1 = (f32[4096,128]{1,0:T(8,128)}, f32[256,256]{1,0:T(8,128)}) custom-call(f32[32,24,128]{2,1,0:T(8,128)} %all_to_all.27.summed_ref, f32[16,256,128]{2,1,0:T(8,128)} %get-tuple-element.23.natural_hbm), custom_call_target="tpu_custom_call" | custom-call | flops 20000000000 | bytes 6291456 | tf_op jit(solution)/shard_map/solve/pallas_call | solution.py:528
  152.5 6.2 %all-to-all-start.4 = ((f32[128,32,128]{2,1,0:T(8,128)}), f32[128,32,128]{2,1,0:T(8,128)S(1)}, u32[]{:S(2)}, u32[]{:S(2)}) async-start(f32[128,32,128]{2,1,0:T(8,128)} %bitcast.42), calls=%async_computation.4 | async-start | bytes 4194304 | tf_op jit(solution)/shard_map/all_to_all | solution.py:592
  159.4 49.1 %all-to-all-done.4.arrived_ref = f32[128,32,128]{2,1,0:T(8,128)S(1)} async-done(((f32[128,32,128]{2,1,0:T(8,128)}), f32[128,32,128]{2,1,0:T(8,128)S(1)}, u32[]{:S(2)}, u32[]{:S(2)}) %all-to-all-start.4) | async-done | bytes 2097184 | tf_op jit(solution)/shard_map/all_to_all | solution.py:592
  208.6 4.4 %collective-permute-start.8 = (f32[128,16,128]{2,1,0:T(8,128)S(1)}, f32[128,16,128]{2,1,0:T(8,128)S(1)}, u32[]{:S(2)}, u32[]{:S(2)}) collective-permute-start(f32[128,16,128]{2,1,0:T(8,128)S(1)} %constant_dynamic-slice_fusion), channel_id=1, source_target_pairs={{0,4},{4,0},{8,12},{12,8},{16,20},{20,16},{24,28},{28,24},{32,36},... | collective-permute-start | bytes 3145736 | tf_op jit(solution)/shard_map/ppermute | solution.py:648
  213.0 2.3 %collective-permute-done.8.received_ref = f32[128,16,128]{2,1,0:T(8,128)S(1)} collective-permute-done((f32[128,16,128]{2,1,0:T(8,128)S(1)}, f32[128,16,128]{2,1,0:T(8,128)S(1)}, u32[]{:S(2)}, u32[]{:S(2)}) %collective-permute-start.8) | collective-permute-done | bytes 1048608 | tf_op jit(solution)/shard_map/ppermute | solution.py:648
  215.3 1.4 assemble.1
  (29 shorter events, 7.0 us)
Async XLA Ops:
  11.5 5.8 %collective-permute-start = (f32[128,16,128]{2,1,0:T(8,128)}, f32[128,16,128]{2,1,0:T(8,128)S(1)}, u32[]{:S(2)}, u32[]{:S(2)}) collective-permute-start(f32[128,16,128]{2,1,0:T(8,128)} %get-tuple-element.18), channel_id=1, source_target_pairs={{0,4},{4,0},{8,12},{12,8},{16,20},{20,16},{24,28},{28,24},{32,36},... | collective-permute-start | bytes 3145736 | tf_op jit(solution)/shard_map/ppermute | solution.py:648
  20.2 13.9 %copy-start.1 = (f32[64,32,128]{2,1,0:T(8,128)S(1)}, f32[64,32,128]{2,1,0:T(8,128)}, u32[]{:S(2)}) copy-start(f32[64,32,128]{2,1,0:T(8,128)} %get-tuple-element.19) | copy-start | bytes 3145732
  20.2 64.0 %all-to-all-start = ((f32[128,32,128]{2,1,0:T(8,128)}), f32[128,32,128]{2,1,0:T(8,128)S(1)}, u32[]{:S(2)}, u32[]{:S(2)}) async-start(f32[128,32,128]{2,1,0:T(8,128)} %pad_maximum_fusion), calls=%async_computation | async-start | bytes 4194304 | tf_op jit(solution)/shard_map/all_to_all | solution.py:592
  35.0 2.5 %collective-permute-start.1 = (f32[8,4,4,8,128]{4,3,2,1,0:T(8,128)}, f32[8,4,4,8,128]{4,3,2,1,0:T(8,128)}, u32[]{:S(2)}, u32[]{:S(2)}) collective-permute-start(f32[8,4,4,8,128]{4,3,2,1,0:T(8,128)} %dynamic-slice_bitcast_fusion), channel_id=1, source_target_pairs={{0,4},{4,0},{8,12},{12,8},{16,20},{20,16},{24,28},{28,24},{32,36},... | collective-permute-start | bytes 1572872 | tf_op jit(solution)/shard_map/ppermute | solution.py:660
  38.8 7.6 %collective-permute-start.2 = (f32[8,4,8,128]{3,2,0,1:T(8,128)S(1)}, f32[8,4,8,128]{3,2,0,1:T(8,128)S(1)}, u32[]{:S(2)}, u32[]{:S(2)}) collective-permute-start(f32[8,4,8,128]{3,2,0,1:T(8,128)S(1)} %bitcast.47), channel_id=1, source_target_pairs={{0,1},{1,2},{2,3},{3,0},{4,5},{5,6},{6,7},{7,4},{8,9},{9,10},{10,1... | collective-permute-start | bytes 393224 | tf_op jit(solution)/shard_map/ppermute | solution.py:660
  39.8 12.5 %collective-permute-start.3 = (f32[8,4,8,128]{3,2,0,1:T(8,128)S(1)}, f32[8,4,8,128]{3,2,0,1:T(8,128)S(1)}, u32[]{:S(2)}, u32[]{:S(2)}) collective-permute-start(f32[8,4,8,128]{3,2,0,1:T(8,128)S(1)} %bitcast.46), channel_id=1, source_target_pairs={{0,2},{1,3},{2,0},{3,1},{4,6},{5,7},{6,4},{7,5},{8,10},{9,11},{10,... | collective-permute-start | bytes 393224 | tf_op jit(solution)/shard_map/ppermute | solution.py:660
  42.2 10.1 %collective-permute-start.4 = (f32[8,4,8,128]{3,2,0,1:T(8,128)S(1)}, f32[8,4,8,128]{3,2,0,1:T(8,128)S(1)}, u32[]{:S(2)}, u32[]{:S(2)}) collective-permute-start(f32[8,4,8,128]{3,2,0,1:T(8,128)S(1)} %bitcast.45), channel_id=1, source_target_pairs={{0,3},{1,0},{2,1},{3,2},{4,7},{5,4},{6,5},{7,6},{8,11},{9,8},{10,9... | collective-permute-start | bytes 393224 | tf_op jit(solution)/shard_map/ppermute | solution.py:660
  52.3 4.5 %collective-permute-start.5 = (f32[8,8,128]{2,1,0:T(8,128)S(1)}, f32[8,8,128]{2,1,0:T(8,128)S(1)}, u32[]{:S(2)}, u32[]{:S(2)}) collective-permute-start(f32[8,8,128]{2,1,0:T(8,128)S(1)} %get-tuple-element.34), channel_id=1, source_target_pairs={{0,8},{4,12},{8,16},{12,20},{16,24},{20,28},{24,0},{28,4},{32,40},... | collective-permute-start | bytes 98312 | tf_op jit(solution)/shard_map/ppermute | solution.py:660
  53.0 3.8 %collective-permute-start.7 = (f32[8,8,128]{2,1,0:T(8,128)S(1)}, f32[8,8,128]{2,1,0:T(8,128)S(1)}, u32[]{:S(2)}, u32[]{:S(2)}) collective-permute-start(f32[8,8,128]{2,1,0:T(8,128)S(1)} %get-tuple-element.35), channel_id=1, source_target_pairs={{0,24},{4,28},{8,0},{12,4},{16,8},{20,12},{24,16},{28,20},{32,56},... | collective-permute-start | bytes 98312 | tf_op jit(solution)/shard_map/ppermute | solution.py:660
  55.1 5.0 %collective-permute-start.6 = (f32[8,8,128]{2,1,0:T(8,128)S(1)}, f32[8,8,128]{2,1,0:T(8,128)S(1)}, u32[]{:S(2)}, u32[]{:S(2)}) collective-permute-start(f32[8,8,128]{2,1,0:T(8,128)S(1)} %get-tuple-element.36), channel_id=1, source_target_pairs={{0,16},{4,20},{8,24},{12,28},{16,0},{20,4},{24,8},{28,12},{32,48},... | collective-permute-start | bytes 98312 | tf_op jit(solution)/shard_map/ppermute | solution.py:660
  84.3 1.3 copy-start
  152.5 56.0 %all-to-all-start.4 = ((f32[128,32,128]{2,1,0:T(8,128)}), f32[128,32,128]{2,1,0:T(8,128)S(1)}, u32[]{:S(2)}, u32[]{:S(2)}) async-start(f32[128,32,128]{2,1,0:T(8,128)} %bitcast.42), calls=%async_computation.4 | async-start | bytes 4194304 | tf_op jit(solution)/shard_map/all_to_all | solution.py:592
  208.6 6.6 %collective-permute-start.8 = (f32[128,16,128]{2,1,0:T(8,128)S(1)}, f32[128,16,128]{2,1,0:T(8,128)S(1)}, u32[]{:S(2)}, u32[]{:S(2)}) collective-permute-start(f32[128,16,128]{2,1,0:T(8,128)S(1)} %constant_dynamic-slice_fusion), channel_id=1, source_target_pairs={{0,4},{4,0},{8,12},{12,8},{16,20},{20,16},{24,28},{28,24},{32,36},... | collective-permute-start | bytes 3145736 | tf_op jit(solution)/shard_map/ppermute | solution.py:648

commit v5 on v3

--- a/solution.py
+++ b/solution.py
@@ -67,10 +67,7 @@
     kinetic = shifted_blocks(kinetic_taps, np.eye(G)) + shifted_blocks(
         (1.0,), banded(G, kinetic_taps)
     )
-    return (
-        split_constant(np.concatenate([magic, kinetic], axis=1)),
-        split_constant(magic),
-    )
+    return np.concatenate(split_constant(np.concatenate([magic, kinetic], axis=1)), axis=1)
 
 
 def plane_filter(read, first, taps):
@@ -86,24 +83,19 @@
     occupation_ref,
     bounds_hbm,
     orbital_hbm,
-    both_high_hbm,
-    both_low_hbm,
+    filters_hbm,
     potential_hbm,
-    magic_high_hbm,
-    magic_low_hbm,
     keep_ref,
     give_ref,
     density_ref,
     bounds_ref,
     orbital_ref,
-    both_high_ref,
-    both_low_ref,
+    filters_ref,
     potential_ref,
-    magic_high_ref,
-    magic_low_ref,
     source,
     filtered,
     kinetic,
+    lines_ref,
     sems,
 ):
     margin = len(kinetic_taps) // 2
@@ -114,11 +106,8 @@
             (
                 (bounds_hbm, bounds_ref),
                 (orbital_hbm, orbital_ref),
-                (both_high_hbm, both_high_ref),
-                (both_low_hbm, both_low_ref),
+                (filters_hbm, filters_ref),
                 (potential_hbm, potential_ref),
-                (magic_high_hbm, magic_high_ref),
-                (magic_low_hbm, magic_low_ref),
             )
         )
     ]
@@ -135,7 +124,7 @@
     filtered[:margin] = zeros
     filtered[margin + G :] = zeros
 
-    def product(x, high_ref, low_ref):
+    def product(x, width):
         shifted = jnp.concatenate(
             [
                 source[pl.ds(margin + x, STRIP), PAD + s : PAD + s + PAIRS].reshape(
@@ -148,7 +137,9 @@
         high = shifted.astype(jnp.bfloat16)
         low = (shifted - high.astype(jnp.float32)).astype(jnp.bfloat16)
         dot = functools.partial(jnp.dot, preferred_element_type=jnp.float32)
-        return dot(high, high_ref[...]) + (dot(low, high_ref[...]) + dot(high, low_ref[...]))
+        high_filter = filters_ref[:, :width]
+        low_filter = filters_ref[:, 2 * LANES : 2 * LANES + width]
+        return dot(high, high_filter) + (dot(low, high_filter) + dot(high, low_filter))
 
     def own(x):
         return source[pl.ds(margin + x, STRIP), PAD : PAD + PAIRS]
@@ -159,8 +150,10 @@
     copies[0].wait()
     copies[1].wait()
     planes = lax.broadcasted_iota(jnp.int32, (STRIP * PAIRS, LANES), 0) // PAIRS
-    bounds = bounds_ref[pl.ds(position, 1), :]
-    begin, end = bounds[:, 0:1], bounds[:, 1:2]
+    bounds = bounds_ref[...]
+    own_place = lax.broadcasted_iota(jnp.int32, bounds.shape, 1) == position
+    bounds = jnp.sum(jnp.where(own_place, bounds, 0), axis=1, keepdims=True)
+    begin, end = bounds[0:1], bounds[1:2]
     blocks = STRIP * PAIRS // ROWS
     half_planes = G // 2
 
@@ -182,13 +175,14 @@
 
     @pl.loop(0, G, step=STRIP)
     def _(x):
-        both = product(x, both_high_ref, both_low_ref)
+        cells = pl.ds(pl.multiple_of(x * G, STRIP * G), STRIP * G)
+        lines_ref[cells, :] = potential_ref[:, cells].T
+        both = product(x, 2 * LANES)
         filtered[pl.ds(margin + x, STRIP)] = both[:, :LANES].reshape(STRIP, PAIRS, LANES)
         kinetic[pl.ds(x, STRIP)] = both[:, LANES:].reshape(STRIP, PAIRS, LANES) + plane_filter(
             own, x, kinetic_taps
         )
 
-    copies[4].wait()
     scale = occupation_ref[position] * (1.0 / occupation_ref.shape[0])
     lines = STRIP * G // 2
 
@@ -197,16 +191,13 @@
         realspace = plane_filter(half, x, magic_taps)
         density_ref[pl.ds(x, STRIP)] = scale * realspace * realspace
         potential = jnp.concatenate(
-            [potential_ref[pl.ds(x * G + odd, lines, stride=2), :] for odd in range(2)], axis=1
+            [lines_ref[pl.ds(x * G + odd, lines, stride=2), :] for odd in range(2)], axis=1
         ).reshape(STRIP, PAIRS, LANES)
         source[pl.ds(margin + x, STRIP), PAD : PAD + PAIRS] = realspace * potential
 
-    copies[5].wait()
-    copies[6].wait()
-
     @pl.loop(0, G, step=STRIP)
     def _(x):
-        filtered[pl.ds(margin + x, STRIP)] = product(x, magic_high_ref, magic_low_ref).reshape(
+        filtered[pl.ds(margin + x, STRIP)] = product(x, LANES).reshape(
             STRIP, PAIRS, LANES
         )
 
@@ -231,11 +222,10 @@
 
 
 def apply_hamiltonian(place, region_bounds, occupation, orbital, potential):
-    (both_high, both_low), (magic_high, magic_low) = filter_constants()
     margin = len(kinetic_taps) // 2
     side = jax.ShapeDtypeStruct((G * PAIRS // ROWS // 2, 2 * ROWS, LANES), jnp.float32)
     grid = jax.ShapeDtypeStruct((G, PAIRS, LANES), jnp.float32)
-    far = (region_bounds, orbital, both_high, both_low, potential, magic_high, magic_low)
+    far = (region_bounds.T, orbital, filter_constants(), potential.T)
     far = [jnp.asarray(values) for values in far]
     return pl.pallas_call(
         hamiltonian_kernel,
@@ -247,9 +237,10 @@
             pltpu.VMEM((G + 2 * margin, PAIRS + 2 * PAD, LANES), jnp.float32),
             pltpu.VMEM((G + 2 * margin, PAIRS, LANES), jnp.float32),
             pltpu.VMEM((G, PAIRS, LANES), jnp.float32),
+            pltpu.VMEM((G * G, G), jnp.float32),
             pltpu.SemaphoreType.DMA((len(far),)),
         ],
-        compiler_params=pltpu.CompilerParams(vmem_limit_bytes=40 * 2**20),
+        compiler_params=pltpu.CompilerParams(vmem_limit_bytes=50 * 2**20),
         cost_estimate=pl.CostEstimate(
             flops=6 * 2048 * 640 * 384, bytes_accessed=5 * 2**20, transcendentals=0
         ),
@@ -267,32 +258,28 @@
 LINES = 4
 
 
-def natural_rows(flat_ref, natural_ref, core, gather, part=0, parts=1):
+def natural_rows(flat_ref, natural_ref, core, gather):
     planes, orbitals, _ = natural_ref.shape
-    groups = orbitals // (CORES * LINES * parts)
+    groups = orbitals // (CORES * LINES)
     stride = CORES * LINES * planes
     for slot in range(CORES):
         for line in range(LINES):
             for plane in range(planes):
-                inner = (line * CORES + slot) * planes + plane + part * groups * stride
-                inner = pl.ds(inner, groups, stride=stride)
-                outer = (slot ^ core) * LINES + line + part * groups * CORES * LINES
-                outer = pl.ds(outer, groups, stride=CORES * LINES)
+                inner = pl.ds((line * CORES + slot) * planes + plane, groups, stride=stride)
+                outer = pl.ds((slot ^ core) * LINES + line, groups, stride=CORES * LINES)
                 if gather:
                     natural_ref[plane, outer, :] = flat_ref[inner, :]
                 else:
                     flat_ref[inner, :] = natural_ref[plane, outer, :]
 
 
-def overlap_kernel(core_ref, flat_ref, natural_hbm, packed_ref, natural_ref, sem):
+def overlap_kernel(core_ref, flat_ref, natural_ref, packed_ref):
     for core in range(CORES):
 
         @pl.when(core_ref[0] == core)
         def _(core=core):
             natural_rows(flat_ref, natural_ref, core, True)
 
-    copy = pltpu.make_async_copy(natural_ref, natural_hbm, sem)
-    copy.start()
     planes, size, _ = natural_ref.shape
     half = planes // 2
     total = None
@@ -316,7 +303,6 @@
     packed_ref[:, size // LANES * ROWS :, :] = jnp.broadcast_to(
         diagonal, (size, LANES)
     ).reshape(chunks, ROWS, LANES)
-    copy.wait()
 
 
 def overlap(core, arrived):
@@ -330,11 +316,7 @@
             jax.ShapeDtypeStruct((size // ROWS, (size // LANES + 1) * ROWS, LANES), jnp.float32),
         ),
         in_specs=[smem(), vmem()],
-        out_specs=(far_away(), vmem()),
-        scratch_shapes=[
-            pltpu.VMEM((planes, size, lanes), jnp.float32),
-            pltpu.SemaphoreType.DMA,
-        ],
+        out_specs=(vmem(), vmem()),
         compiler_params=pltpu.CompilerParams(vmem_limit_bytes=40 * 2**20),
         cost_estimate=pl.CostEstimate(
             flops=24 * 256 * 256 * 1024, bytes_accessed=4 * 2**20, transcendentals=0
@@ -420,19 +402,12 @@
 def solve_kernel(
     cells,
     summed_ref,
-    natural_hbm,
-    flat_hbm,
+    natural_ref,
+    flat_ref,
     subspace_ref,
     work,
-    natural_ref,
     mixed,
-    flat_ref,
-    in_sem,
-    out_sems,
 ):
-    arrival = pltpu.make_async_copy(natural_hbm, natural_ref, in_sem)
-    arrival.start()
-
     def dot(a, b):
         return jnp.dot(a, b, precision=precise, preferred_element_type=jnp.float32)
 
@@ -459,7 +434,6 @@
     subspace_ref[...] = subspace
     planes = natural_ref.shape[0]
     half = planes // 2
-    arrival.wait()
     for plane in range(0, half, 2):
         both = [
             dot(
@@ -472,17 +446,7 @@
         for k, part in enumerate(both):
             mixed[plane + k] = part[:, :LANES]
             mixed[half + plane + k] = part[:, LANES:] - product[:, k * LANES : (k + 1) * LANES]
-    parts = 4
-    rows = flat_ref.shape[0] // parts
-    copies = []
-    for part in range(parts):
-        natural_rows(flat_ref, mixed, 0, False, part, parts)
-        here = pl.ds(part * rows, rows)
-        copy = pltpu.make_async_copy(flat_ref.at[here], flat_hbm.at[here], out_sems.at[part])
-        copy.start()
-        copies.append(copy)
-    for copy in copies:
-        copy.wait()
+    natural_rows(flat_ref, mixed, 0, False)
 
 
 def solve(summed, natural, cells):
@@ -493,15 +457,11 @@
             jax.ShapeDtypeStruct((planes * size, lanes), jnp.float32),
             jax.ShapeDtypeStruct((size, size), jnp.float32),
         ),
-        in_specs=[vmem(), far_away()],
-        out_specs=(far_away(), vmem()),
+        in_specs=[vmem(), vmem()],
+        out_specs=(vmem(), vmem()),
         scratch_shapes=[
             pltpu.VMEM((size, 2 * size), jnp.float32),
             pltpu.VMEM(natural.shape, jnp.float32),
-            pltpu.VMEM(natural.shape, jnp.float32),
-            pltpu.VMEM((planes * size, lanes), jnp.float32),
-            pltpu.SemaphoreType.DMA,
-            pltpu.SemaphoreType.DMA((4,)),
         ],
         compiler_params=pltpu.CompilerParams(vmem_limit_bytes=48 * 2**20),
         cost_estimate=pl.CostEstimate(
@@ -673,13 +633,14 @@
     summed, density = sum_everywhere(packed, slabs, layout)
     mixed, subspace = solve(summed, natural, cell_total)
     back = exchange(mixed.reshape(-1, 4 * ROWS, LANES), layout.chips())
+    back, density = lax.optimization_barrier((back, density.reshape(-1, G)))
     other = lax.dynamic_slice_in_dim(back, (1 - core[0]) * 2 * ROWS, 2 * ROWS, 1)
     orthonormal, gradient = assemble(core, back, layout.swap_cores(other))
     return (
         orthonormal.reshape(1, cell_total),
         gradient.reshape(1, cell_total),
         subspace,
-        density.reshape(-1, G),
+        density,
     )
 
 

time: 219 us -> 213 us (0.973)
  local copies, waits for them, and re-layouts: 12.2 us -> 6.91 us
    unnamed x20 -> x12, local copies, waits for them, and re-layouts: 9.42 us -> 5.13 us
where the time goes in v5:
time: 213 us; the launch traced here: 212 us
  waiting for transfers between devices  92 us (43%)
  blocking collectives  43.5 us (20%)
  starting transfers between devices  37.3 us (18%)
  Pallas kernels  28.6 us (13%)
  local copies, waits for them, and re-layouts  6.91 us (3%)
  other arithmetic  2.93 us (1%)
    all_to_all x2, waiting for transfers between devices, exchange(): lax.all_to_all(blocks, axes, split_axis=0, concat_axis=0, tiled=True, axi...  73.3 us
    all_to_all x3, blocking collectives, exchange(): lax.all_to_all(blocks, axes, split_axis=0, concat_axis=0, tiled=True, axi...  43.5 us
    all_to_all x2, starting transfers between devices, exchange(): lax.all_to_all(blocks, axes, split_axis=0, concat_axis=0, tiled=True, axi...  20 us
    pallas_call x1, Pallas kernels, solve(): pl.pallas_call(functools.partial(solve_kernel, cells), out_shape=(jax.Sha...  15.1 us
    ppermute x7, waiting for transfers between devices, stage(): lax.ppermute(lax.dynamic_index_in_dim(values, (index + k) % count, dim, k...  14 us
    ppermute x7, starting transfers between devices, stage(): lax.ppermute(lax.dynamic_index_in_dim(values, (index + k) % count, dim, k...  9.65 us
    pallas_call x1, Pallas kernels, apply_hamiltonian(): pl.pallas_call(hamiltonian_kernel, out_shape=(side, side, grid), in_specs...  8.9 us
    ppermute x2, starting transfers between devices, swap_cores(): return lax.ppermute(values, 'orb', pairs)  7.69 us
  transfers between devices with their start and end apart: 11, of which 8 were waited for; matrix products, arithmetic and copies ran while one was open for 1% of the time, Pallas kernels for 0%

profile of v5, /device:TPU:1, one launch (start us, length us, event | category | flops | bytes accessed | tf_op | source)
XLA Modules:
  0.0 212.2 jit_solution(1215234833150274546)
XLA Ops:
  3.2 8.9 %hamiltonian.1 = (f32[128,16,128]{2,1,0:T(8,128)S(1)}, f32[128,16,128]{2,1,0:T(8,128)S(1)}, f32[64,32,128]{2,1,0:T(8,128)S(1)}) custom-call(s32[2]{0:T(128)S(1)} %pad_add_fusion.place_ref, f32[256]{0:T(256)S(1)} %copy-done.2, s32[2,256]{1,0:T(2,128)S(1)} %bitcast.45, f32[64,32,128]{2,1,0:T(8,128)} %bitcast.49, bf16[640,512]{1,0:T(8,128)(2,1)S(1)} %copy-done.3, ...), custom_call_target="tpu_custom_call" | custom-call | flops 3019898880 | bytes 5242880 | tf_op jit(solution)/shard_map/hamiltonian/pallas_call | solution.py:230
  12.1 3.3 %collective-permute-start = (f32[128,16,128]{2,1,0:T(8,128)S(1)}, f32[128,16,128]{2,1,0:T(8,128)S(1)}, u32[]{:S(2)}, u32[]{:S(2)}) collective-permute-start(f32[128,16,128]{2,1,0:T(8,128)S(1)} %get-tuple-element.18), channel_id=1, source_target_pairs={{0,4},{4,0},{8,12},{12,8},{16,20},{20,16},{24,28},{28,24},{32,36},... | collective-permute-start | bytes 3145736 | tf_op jit(solution)/shard_map/ppermute | solution.py:570
  15.4 2.3 %collective-permute-done = f32[128,16,128]{2,1,0:T(8,128)S(1)} collective-permute-done((f32[128,16,128]{2,1,0:T(8,128)S(1)}, f32[128,16,128]{2,1,0:T(8,128)S(1)}, u32[]{:S(2)}, u32[]{:S(2)}) %collective-permute-start) | collective-permute-done | bytes 1048608 | tf_op jit(solution)/shard_map/ppermute | solution.py:570
  17.7 1.6 pad_maximum_fusion
  19.3 13.8 %all-to-all-start = ((f32[128,32,128]{2,1,0:T(8,128)}), f32[128,32,128]{2,1,0:T(8,128)S(1)}, u32[]{:S(2)}, u32[]{:S(2)}) async-start(f32[128,32,128]{2,1,0:T(8,128)} %pad_maximum_fusion), calls=%async_computation | async-start | bytes 4194304 | tf_op jit(solution)/shard_map/all_to_all | solution.py:514
  34.6 1.9 collective-permute-done.1
  38.7 2.4 %collective-permute-start.3 = (f32[8,4,8,128]{3,2,0,1:T(8,128)S(1)}, f32[8,4,8,128]{3,2,0,1:T(8,128)S(1)}, u32[]{:S(2)}, u32[]{:S(2)}) collective-permute-start(f32[8,4,8,128]{3,2,0,1:T(8,128)S(1)} %bitcast.47), channel_id=1, source_target_pairs={{0,2},{1,3},{2,0},{3,1},{4,6},{5,7},{6,4},{7,5},{8,10},{9,11},{10,... | collective-permute-start | bytes 393224 | tf_op jit(solution)/shard_map/ppermute | solution.py:582
  42.3 3.1 %collective-permute-done.2 = f32[8,4,8,128]{3,2,0,1:T(8,128)S(1)} collective-permute-done((f32[8,4,8,128]{3,2,0,1:T(8,128)S(1)}, f32[8,4,8,128]{3,2,0,1:T(8,128)S(1)}, u32[]{:S(2)}, u32[]{:S(2)}) %collective-permute-start.2) | collective-permute-done | bytes 131104 | tf_op jit(solution)/shard_map/ppermute | solution.py:582
  45.3 5.8 %collective-permute-done.3 = f32[8,4,8,128]{3,2,0,1:T(8,128)S(1)} collective-permute-done((f32[8,4,8,128]{3,2,0,1:T(8,128)S(1)}, f32[8,4,8,128]{3,2,0,1:T(8,128)S(1)}, u32[]{:S(2)}, u32[]{:S(2)}) %collective-permute-start.3) | collective-permute-done | bytes 131104 | tf_op jit(solution)/shard_map/ppermute | solution.py:582
  51.9 2.1 collective-permute-start.7
  54.0 1.7 collective-permute-start.6
  55.7 3.2 %collective-permute-done.6 = f32[8,8,128]{2,1,0:T(8,128)S(1)} collective-permute-done((f32[8,8,128]{2,1,0:T(8,128)S(1)}, f32[8,8,128]{2,1,0:T(8,128)S(1)}, u32[]{:S(2)}, u32[]{:S(2)}) %collective-permute-start.6) | collective-permute-done | bytes 32800 | tf_op jit(solution)/shard_map/ppermute | solution.py:582
  59.0 24.2 %all-to-all-done = f32[128,32,128]{2,1,0:T(8,128)S(1)} async-done(((f32[128,32,128]{2,1,0:T(8,128)}), f32[128,32,128]{2,1,0:T(8,128)S(1)}, u32[]{:S(2)}, u32[]{:S(2)}) %all-to-all-start) | async-done | bytes 2097184 | tf_op jit(solution)/shard_map/all_to_all | solution.py:514
  83.2 3.3 %overlap.1 = (f32[16,256,128]{2,1,0:T(8,128)S(1)}, f32[32,24,128]{2,1,0:T(8,128)S(1)}) custom-call(s32[1]{0:T(128)} %bitcast.core_ref, f32[4096,128]{1,0:T(8,128)S(1)} %bitcast.41), custom_call_target="tpu_custom_call" | custom-call | flops 1610612736 | bytes 4194304 | tf_op jit(solution)/shard_map/overlap/pallas_call | solution.py:312
  86.5 1.3 copy-done.4
  87.8 17.5 %all_to_all.25 = f32[32,24,128]{2,1,0:T(8,128)S(1)} all-to-all(f32[32,24,128]{2,1,0:T(8,128)S(1)} %get-tuple-element.21), channel_id=1, replica_groups={{0,1,2,3,4,5,6,7,8,9,10,11,12,13,14,15,16,17,18,19,20,21,22,23,24,25,26..., dimensions={0} | all-to-all | bytes 786432 | tf_op jit(solution)/shard_map/all_to_all | solution.py:514
  105.5 10.4 %all_to_all.26 = f32[8,32,128]{2,1,0:T(8,128)S(1)} all-to-all(f32[8,32,128]{2,1,0:T(8,128)S(1)} %pad_maximum_fusion.1), channel_id=1, replica_groups={{0,32,64,96,128,160,192,224},{4,36,68,100,132,164,196,228},{8,40,72,104..., dimensions={0} | all-to-all | bytes 262144 | tf_op jit(solution)/shard_map/all_to_all | solution.py:514
  115.9 15.6 %all_to_all.27.summed_ref = f32[32,24,128]{2,1,0:T(8,128)S(1)} all-to-all(f32[32,24,128]{2,1,0:T(8,128)S(1)} %broadcast_in_dim.5), channel_id=1, replica_groups={{0,1,2,3,4,5,6,7,8,9,10,11,12,13,14,15,16,17,18,19,20,21,22,23,24,25,26..., dimensions={0} | all-to-all | bytes 786432 | tf_op jit(solution)/shard_map/all_to_all | solution.py:514
  131.5 15.1 %solve.1 = (f32[4096,128]{1,0:T(8,128)S(1)}, f32[256,256]{1,0:T(8,128)}) custom-call(f32[32,24,128]{2,1,0:T(8,128)S(1)} %all_to_all.27.summed_ref, f32[16,256,128]{2,1,0:T(8,128)S(1)} %copy-done.5), custom_call_target="tpu_custom_call" | custom-call | flops 20000000000 | bytes 6291456 | tf_op jit(solution)/shard_map/solve/pallas_call | solution.py:454
  147.9 6.2 %all-to-all-start.4 = ((f32[128,32,128]{2,1,0:T(8,128)}), f32[128,32,128]{2,1,0:T(8,128)S(1)}, u32[]{:S(2)}, u32[]{:S(2)}) async-start(f32[128,32,128]{2,1,0:T(8,128)} %bitcast.42), calls=%async_computation.4 | async-start | bytes 4194304 | tf_op jit(solution)/shard_map/all_to_all | solution.py:514
  154.8 49.1 %all-to-all-done.4.arrived_ref = f32[128,32,128]{2,1,0:T(8,128)S(1)} async-done(((f32[128,32,128]{2,1,0:T(8,128)}), f32[128,32,128]{2,1,0:T(8,128)S(1)}, u32[]{:S(2)}, u32[]{:S(2)}) %all-to-all-start.4) | async-done | bytes 2097184 | tf_op jit(solution)/shard_map/all_to_all | solution.py:514
  204.1 4.4 %collective-permute-start.8 = (f32[128,16,128]{2,1,0:T(8,128)S(1)}, f32[128,16,128]{2,1,0:T(8,128)S(1)}, u32[]{:S(2)}, u32[]{:S(2)}) collective-permute-start(f32[128,16,128]{2,1,0:T(8,128)S(1)} %constant_dynamic-slice_fusion), channel_id=1, source_target_pairs={{0,4},{4,0},{8,12},{12,8},{16,20},{20,16},{24,28},{28,24},{32,36},... | collective-permute-start | bytes 3145736 | tf_op jit(solution)/shard_map/ppermute | solution.py:570
  208.4 2.3 %collective-permute-done.8.received_ref = f32[128,16,128]{2,1,0:T(8,128)S(1)} collective-permute-done((f32[128,16,128]{2,1,0:T(8,128)S(1)}, f32[128,16,128]{2,1,0:T(8,128)S(1)}, u32[]{:S(2)}, u32[]{:S(2)}) %collective-permute-start.8) | collective-permute-done | bytes 1048608 | tf_op jit(solution)/shard_map/ppermute | solution.py:570
  210.7 1.4 assemble.1
  (37 shorter events, 10.3 us)
Async XLA Ops:
  0.7 0.7 copy-start.1
  1.4 0.7 copy-start.2
  2.1 1.1 copy-start.3
  12.1 5.6 %collective-permute-start = (f32[128,16,128]{2,1,0:T(8,128)S(1)}, f32[128,16,128]{2,1,0:T(8,128)S(1)}, u32[]{:S(2)}, u32[]{:S(2)}) collective-permute-start(f32[128,16,128]{2,1,0:T(8,128)S(1)} %get-tuple-element.18), channel_id=1, source_target_pairs={{0,4},{4,0},{8,12},{12,8},{16,20},{20,16},{24,28},{28,24},{32,36},... | collective-permute-start | bytes 3145736 | tf_op jit(solution)/shard_map/ppermute | solution.py:570
  19.3 63.9 %all-to-all-start = ((f32[128,32,128]{2,1,0:T(8,128)}), f32[128,32,128]{2,1,0:T(8,128)S(1)}, u32[]{:S(2)}, u32[]{:S(2)}) async-start(f32[128,32,128]{2,1,0:T(8,128)} %pad_maximum_fusion), calls=%async_computation | async-start | bytes 4194304 | tf_op jit(solution)/shard_map/all_to_all | solution.py:514
  34.0 2.5 %collective-permute-start.1 = (f32[8,4,4,8,128]{4,3,2,1,0:T(8,128)}, f32[8,4,4,8,128]{4,3,2,1,0:T(8,128)}, u32[]{:S(2)}, u32[]{:S(2)}) collective-permute-start(f32[8,4,4,8,128]{4,3,2,1,0:T(8,128)} %dynamic-slice_bitcast_fusion), channel_id=1, source_target_pairs={{0,4},{4,0},{8,12},{12,8},{16,20},{20,16},{24,28},{28,24},{32,36},... | collective-permute-start | bytes 1572872 | tf_op jit(solution)/shard_map/ppermute | solution.py:582
  37.8 7.6 %collective-permute-start.2 = (f32[8,4,8,128]{3,2,0,1:T(8,128)S(1)}, f32[8,4,8,128]{3,2,0,1:T(8,128)S(1)}, u32[]{:S(2)}, u32[]{:S(2)}) collective-permute-start(f32[8,4,8,128]{3,2,0,1:T(8,128)S(1)} %bitcast.48), channel_id=1, source_target_pairs={{0,1},{1,2},{2,3},{3,0},{4,5},{5,6},{6,7},{7,4},{8,9},{9,10},{10,1... | collective-permute-start | bytes 393224 | tf_op jit(solution)/shard_map/ppermute | solution.py:582
  38.7 12.5 %collective-permute-start.3 = (f32[8,4,8,128]{3,2,0,1:T(8,128)S(1)}, f32[8,4,8,128]{3,2,0,1:T(8,128)S(1)}, u32[]{:S(2)}, u32[]{:S(2)}) collective-permute-start(f32[8,4,8,128]{3,2,0,1:T(8,128)S(1)} %bitcast.47), channel_id=1, source_target_pairs={{0,2},{1,3},{2,0},{3,1},{4,6},{5,7},{6,4},{7,5},{8,10},{9,11},{10,... | collective-permute-start | bytes 393224 | tf_op jit(solution)/shard_map/ppermute | solution.py:582
  41.1 10.1 %collective-permute-start.4 = (f32[8,4,8,128]{3,2,0,1:T(8,128)S(1)}, f32[8,4,8,128]{3,2,0,1:T(8,128)S(1)}, u32[]{:S(2)}, u32[]{:S(2)}) collective-permute-start(f32[8,4,8,128]{3,2,0,1:T(8,128)S(1)} %bitcast.46), channel_id=1, source_target_pairs={{0,3},{1,0},{2,1},{3,2},{4,7},{5,4},{6,5},{7,6},{8,11},{9,8},{10,9... | collective-permute-start | bytes 393224 | tf_op jit(solution)/shard_map/ppermute | solution.py:582
  51.2 4.5 %collective-permute-start.5 = (f32[8,8,128]{2,1,0:T(8,128)S(1)}, f32[8,8,128]{2,1,0:T(8,128)S(1)}, u32[]{:S(2)}, u32[]{:S(2)}) collective-permute-start(f32[8,8,128]{2,1,0:T(8,128)S(1)} %get-tuple-element.34), channel_id=1, source_target_pairs={{0,8},{4,12},{8,16},{12,20},{16,24},{20,28},{24,0},{28,4},{32,40},... | collective-permute-start | bytes 98312 | tf_op jit(solution)/shard_map/ppermute | solution.py:582
  51.9 3.8 %collective-permute-start.7 = (f32[8,8,128]{2,1,0:T(8,128)S(1)}, f32[8,8,128]{2,1,0:T(8,128)S(1)}, u32[]{:S(2)}, u32[]{:S(2)}) collective-permute-start(f32[8,8,128]{2,1,0:T(8,128)S(1)} %get-tuple-element.35), channel_id=1, source_target_pairs={{0,24},{4,28},{8,0},{12,4},{16,8},{20,12},{24,16},{28,20},{32,56},... | collective-permute-start | bytes 98312 | tf_op jit(solution)/shard_map/ppermute | solution.py:582
  54.0 5.0 %collective-permute-start.6 = (f32[8,8,128]{2,1,0:T(8,128)S(1)}, f32[8,8,128]{2,1,0:T(8,128)S(1)}, u32[]{:S(2)}, u32[]{:S(2)}) collective-permute-start(f32[8,8,128]{2,1,0:T(8,128)S(1)} %get-tuple-element.36), channel_id=1, source_target_pairs={{0,16},{4,20},{8,24},{12,28},{16,0},{20,4},{24,8},{28,12},{32,48},... | collective-permute-start | bytes 98312 | tf_op jit(solution)/shard_map/ppermute | solution.py:582
  86.5 1.3 copy-start.4
  87.8 43.7 %copy-start.5 = (f32[16,256,128]{2,1,0:T(8,128)S(1)}, f32[16,256,128]{2,1,0:T(8,128)}, u32[]{:S(2)}) copy-start(f32[16,256,128]{2,1,0:T(8,128)} %copy-done.4) | copy-start | bytes 6291460
  146.6 1.3 copy-start
  147.9 56.0 %all-to-all-start.4 = ((f32[128,32,128]{2,1,0:T(8,128)}), f32[128,32,128]{2,1,0:T(8,128)S(1)}, u32[]{:S(2)}, u32[]{:S(2)}) async-start(f32[128,32,128]{2,1,0:T(8,128)} %bitcast.42), calls=%async_computation.4 | async-start | bytes 4194304 | tf_op jit(solution)/shard_map/all_to_all | solution.py:514
  204.1 6.6 %collective-permute-start.8 = (f32[128,16,128]{2,1,0:T(8,128)S(1)}, f32[128,16,128]{2,1,0:T(8,128)S(1)}, u32[]{:S(2)}, u32[]{:S(2)}) collective-permute-start(f32[128,16,128]{2,1,0:T(8,128)S(1)} %constant_dynamic-slice_fusion), channel_id=1, source_target_pairs={{0,4},{4,0},{8,12},{12,8},{16,20},{20,16},{24,28},{28,24},{32,36},... | collective-permute-start | bytes 3145736 | tf_op jit(solution)/shard_map/ppermute | solution.py:570

commit v6 on v5

--- a/solution.py
+++ b/solution.py
@@ -80,7 +80,6 @@
 
 def hamiltonian_kernel(
     place_ref,
-    occupation_ref,
     bounds_hbm,
     orbital_hbm,
     filters_hbm,
@@ -183,13 +182,12 @@
             own, x, kinetic_taps
         )
 
-    scale = occupation_ref[position] * (1.0 / occupation_ref.shape[0])
     lines = STRIP * G // 2
 
     @pl.loop(0, G, step=STRIP)
     def _(x):
         realspace = plane_filter(half, x, magic_taps)
-        density_ref[pl.ds(x, STRIP)] = scale * realspace * realspace
+        density_ref[pl.ds(x, STRIP)] = realspace * realspace
         potential = jnp.concatenate(
             [lines_ref[pl.ds(x * G + odd, lines, stride=2), :] for odd in range(2)], axis=1
         ).reshape(STRIP, PAIRS, LANES)
@@ -221,7 +219,7 @@
     return pl.BlockSpec(memory_space=pltpu.HBM)
 
 
-def apply_hamiltonian(place, region_bounds, occupation, orbital, potential):
+def apply_hamiltonian(place, region_bounds, orbital, potential):
     margin = len(kinetic_taps) // 2
     side = jax.ShapeDtypeStruct((G * PAIRS // ROWS // 2, 2 * ROWS, LANES), jnp.float32)
     grid = jax.ShapeDtypeStruct((G, PAIRS, LANES), jnp.float32)
@@ -230,7 +228,7 @@
     return pl.pallas_call(
         hamiltonian_kernel,
         out_shape=(side, side, grid),
-        in_specs=[smem()] * 2 + [far_away()] * len(far),
+        in_specs=[smem()] + [far_away()] * len(far),
         out_specs=(vmem(),) * 3,
         scratch_shapes=[pltpu.VMEM(values.shape, values.dtype) for values in far]
         + [
@@ -245,7 +243,7 @@
             flops=6 * 2048 * 640 * 384, bytes_accessed=5 * 2**20, transcendentals=0
         ),
         name="hamiltonian",
-    )(place, occupation, *far)
+    )(place, *far)
 
 
 def transposed_dot(a, b):
@@ -273,7 +271,7 @@
                     flat_ref[inner, :] = natural_ref[plane, outer, :]
 
 
-def overlap_kernel(core_ref, flat_ref, natural_ref, packed_ref):
+def overlap_kernel(core_ref, flat_ref, natural_ref, packed_ref, square):
     for core in range(CORES):
 
         @pl.when(core_ref[0] == core)
@@ -294,15 +292,21 @@
     column = lax.broadcasted_iota(jnp.int32, (size, size), 1)
     hamilton = total[:, size:]
     packed = jnp.where(row <= column, total[:, :size], hamilton)
-    diagonal = jnp.sum(jnp.where(row == column, hamilton, 0.0), axis=1, keepdims=True)
+    diagonal = jnp.where(row == column, hamilton, 0.0)
     chunks = size // ROWS
-    for part in range(size // LANES):
-        packed_ref[:, part * ROWS : (part + 1) * ROWS, :] = packed[
-            :, part * LANES : (part + 1) * LANES
-        ].reshape(chunks, ROWS, LANES)
-    packed_ref[:, size // LANES * ROWS :, :] = jnp.broadcast_to(
-        diagonal, (size, LANES)
-    ).reshape(chunks, ROWS, LANES)
+    parts = size // LANES
+    lane_sum = 0.0
+    for part in range(parts):
+        lanes = slice(part * LANES, (part + 1) * LANES)
+        square[part] = packed[:, lanes]
+        lane_sum += diagonal[:, lanes]
+        for line in range(ROWS):
+            packed_ref[pl.ds(part * ROWS + line, chunks, stride=parts * ROWS + 1), :] = square[
+                part, pl.ds(line, chunks, stride=ROWS), :
+            ]
+    packed_ref[pl.ds(parts * ROWS, chunks, stride=parts * ROWS + 1), :] = jnp.sum(
+        lane_sum.reshape(chunks, ROWS, LANES), axis=1
+    )
 
 
 def overlap(core, arrived):
@@ -313,10 +317,11 @@
         overlap_kernel,
         out_shape=(
             jax.ShapeDtypeStruct((planes, size, lanes), jnp.float32),
-            jax.ShapeDtypeStruct((size // ROWS, (size // LANES + 1) * ROWS, LANES), jnp.float32),
+            jax.ShapeDtypeStruct((size // ROWS * (size // LANES * ROWS + 1), LANES), jnp.float32),
         ),
         in_specs=[smem(), vmem()],
         out_specs=(vmem(), vmem()),
+        scratch_shapes=[pltpu.VMEM((size // LANES, size, LANES), jnp.float32)],
         compiler_params=pltpu.CompilerParams(vmem_limit_bytes=40 * 2**20),
         cost_estimate=pl.CostEstimate(
             flops=24 * 256 * 256 * 1024, bytes_accessed=4 * 2**20, transcendentals=0
@@ -407,18 +412,24 @@
     subspace_ref,
     work,
     mixed,
+    square,
 ):
     def dot(a, b):
         return jnp.dot(a, b, precision=precise, preferred_element_type=jnp.float32)
 
     size = work.shape[0]
     parts = size // LANES
-    tiles = [
-        summed_ref[:, part * ROWS : (part + 1) * ROWS, :].reshape(size, LANES)
-        for part in range(parts + 1)
-    ]
-    packed = jnp.concatenate(tiles[:parts], axis=1) * (1.0 / cells)
-    diagonal = jnp.concatenate(tiles[parts:] * parts, axis=1) * (1.0 / cells)
+    chunks = size // ROWS
+    stride = parts * ROWS + 1
+    for part in range(parts):
+        for line in range(ROWS):
+            square[part, pl.ds(line, chunks, stride=ROWS), :] = summed_ref[
+                pl.ds(part * ROWS + line, chunks, stride=stride), :
+            ]
+    diagonal = summed_ref[pl.ds(parts * ROWS, chunks, stride=stride), :]
+    diagonal = jnp.broadcast_to(diagonal[:, None, :], (chunks, ROWS, LANES)).reshape(size, LANES)
+    diagonal = jnp.concatenate([diagonal] * parts, axis=1) * (1.0 / cells)
+    packed = jnp.concatenate([square[part] for part in range(parts)], axis=1) * (1.0 / cells)
     row = lax.broadcasted_iota(jnp.int32, (size, size), 0)
     column = lax.broadcasted_iota(jnp.int32, (size, size), 1)
     turned = packed.T
@@ -462,6 +473,7 @@
         scratch_shapes=[
             pltpu.VMEM((size, 2 * size), jnp.float32),
             pltpu.VMEM(natural.shape, jnp.float32),
+            pltpu.VMEM((size // LANES, size, LANES), jnp.float32),
         ],
         compiler_params=pltpu.CompilerParams(vmem_limit_bytes=48 * 2**20),
         cost_estimate=pl.CostEstimate(
@@ -606,13 +618,16 @@
 
 
 def sum_everywhere(chunks, slabs, layout):
-    count, rows, lanes = chunks.shape
-    part = jnp.sum(exchange(chunks, layout.planes()), axis=0, keepdims=True)
-    part = jnp.broadcast_to(part, (layout.z, rows, lanes))
-    part = exchange(jnp.concatenate([part, slabs], axis=1), layout.columns(), "orb")
+    count = layout.total // layout.z
+    flat = chunks.reshape(count, 1, -1)
+    length = flat.shape[2]
+    part = jnp.sum(exchange(flat, layout.planes()), axis=0, keepdims=True)
+    part = jnp.broadcast_to(part, (layout.z, 1, length))
+    slabs = slabs.reshape(layout.z, 1, -1)
+    part = exchange(jnp.concatenate([part, slabs], axis=2), layout.columns(), "orb")
     total = jnp.sum(part, axis=0)
-    everywhere = jnp.broadcast_to(total[None, :rows], (count, rows, lanes))
-    return exchange(everywhere, layout.planes()), total[rows:]
+    everywhere = jnp.broadcast_to(total[None, :, :length], (count, 1, length))
+    return exchange(everywhere, layout.planes()).reshape(chunks.shape), total[:, length:]
 
 
 def on_device(layout, orbitals, potential, occupation, region_bounds):
@@ -623,10 +638,11 @@
     place = jnp.stack([position, core]).astype(jnp.int32)
     core = core.reshape(1).astype(jnp.int32)
     keep, give, density_part = apply_hamiltonian(
-        place, region_bounds, occupation, orbitals.reshape(G, PAIRS, LANES), potential
+        place, region_bounds, orbitals.reshape(G, PAIRS, LANES), potential
     )
+    scale = lax.dynamic_slice_in_dim(occupation, position, 1, 0) / layout.total
     sent = jnp.concatenate([keep, layout.swap_cores(give)], axis=1)
-    slabs = reduce_slab(density_part, layout)
+    slabs = reduce_slab(scale * density_part, layout)
     arrived = exchange(sent, layout.chips())
     arrived, slabs = lax.optimization_barrier((arrived, slabs))
     natural, packed = overlap(core, arrived.reshape(-1, LANES))

time: 213 us -> 210 us (0.986)
  waiting for transfers between devices: 92 us -> 89.4 us
  blocking collectives: 43.5 us -> 41 us
    all_to_all x2, waiting for transfers between devices: 73.3 us -> 70.7 us  [exchange(): lax.all_to_all(blocks, axes, split_axis=0, concat_axis=0, tiled=True, axi...]
    all_to_all x3, blocking collectives: 43.5 us -> 41 us  [exchange(): lax.all_to_all(blocks, axes, split_axis=0, concat_axis=0, tiled=True, axi...]
    unnamed x12 -> x14, local copies, waits for them, and re-layouts: 5.13 us -> 5.23 us
  transfers between devices with their start and end apart: 11 -> 11, of which waited for: 8 -> 10; matrix products, arithmetic and copies ran while one was open for 1% -> 2% of each run, Pallas kernels for 0% -> 0%
where the time goes in v6:
time: 210 us; the launch traced here: 209 us
  waiting for transfers between devices  89.4 us (43%)
  blocking collectives  41 us (20%)
  starting transfers between devices  37.8 us (18%)
  Pallas kernels  28.6 us (14%)
  local copies, waits for them, and re-layouts  7.79 us (4%)
  other arithmetic  3.29 us (2%)
    all_to_all x2, waiting for transfers between devices, exchange(): lax.all_to_all(blocks, axes, split_axis=0, concat_axis=0, tiled=True, axi...  70.7 us
    all_to_all x3, blocking collectives, exchange(): lax.all_to_all(blocks, axes, split_axis=0, concat_axis=0, tiled=True, axi...  41 us
    all_to_all x2, starting transfers between devices, exchange(): lax.all_to_all(blocks, axes, split_axis=0, concat_axis=0, tiled=True, axi...  20.1 us
    pallas_call x1, Pallas kernels, solve(): pl.pallas_call(functools.partial(solve_kernel, cells), out_shape=(jax.Sha...  15.1 us
    ppermute x7, waiting for transfers between devices, stage(): lax.ppermute(lax.dynamic_index_in_dim(values, (index + k) % count, dim, k...  14.1 us
    ppermute x7, starting transfers between devices, stage(): lax.ppermute(lax.dynamic_index_in_dim(values, (index + k) % count, dim, k...  10.4 us
    pallas_call x1, Pallas kernels, apply_hamiltonian(): pl.pallas_call(hamiltonian_kernel, out_shape=(side, side, grid), in_specs...  8.89 us
    ppermute x2, starting transfers between devices, swap_cores(): return lax.ppermute(values, 'orb', pairs)  7.27 us
  transfers between devices with their start and end apart: 11, of which 10 were waited for; matrix products, arithmetic and copies ran while one was open for 2% of the time, Pallas kernels for 0%

profile of v6, /device:TPU:1, one launch (start us, length us, event | category | flops | bytes accessed | tf_op | source)
XLA Modules:
  0.0 209.5 jit_solution(4385642894012072273)
XLA Ops:
  2.5 8.9 %hamiltonian.1 = (f32[128,16,128]{2,1,0:T(8,128)S(1)}, f32[128,16,128]{2,1,0:T(8,128)S(1)}, f32[64,32,128]{2,1,0:T(8,128)S(1)}) custom-call(s32[2]{0:T(128)S(1)} %pad_add_fusion.place_ref, s32[2,256]{1,0:T(2,128)S(1)} %bitcast.47, f32[64,32,128]{2,1,0:T(8,128)} %bitcast.50, bf16[640,512]{1,0:T(8,128)(2,1)S(1)} %copy-done.2, f32[64,4096]{1,0:T(8,128)} %bitcast.51), custom_call_target="tpu_custom_call" | custom-call | flops 3019898880 | bytes 5242880 | tf_op jit(solution)/shard_map/hamiltonian/pallas_call | solution.py:228
  11.4 3.3 %collective-permute-start = (f32[128,16,128]{2,1,0:T(8,128)S(1)}, f32[128,16,128]{2,1,0:T(8,128)S(1)}, u32[]{:S(2)}, u32[]{:S(2)}) collective-permute-start(f32[128,16,128]{2,1,0:T(8,128)S(1)} %get-tuple-element.18), channel_id=1, source_target_pairs={{0,4},{4,0},{8,12},{12,8},{16,20},{20,16},{24,28},{28,24},{32,36},... | collective-permute-start | bytes 3145736 | tf_op jit(solution)/shard_map/ppermute | solution.py:582
  14.7 2.3 %collective-permute-done = f32[128,16,128]{2,1,0:T(8,128)S(1)} collective-permute-done((f32[128,16,128]{2,1,0:T(8,128)S(1)}, f32[128,16,128]{2,1,0:T(8,128)S(1)}, u32[]{:S(2)}, u32[]{:S(2)}) %collective-permute-start) | collective-permute-done | bytes 1048608 | tf_op jit(solution)/shard_map/ppermute | solution.py:582
  17.0 1.7 pad_maximum_fusion
  18.7 13.9 %all-to-all-start = ((f32[128,32,128]{2,1,0:T(8,128)}), f32[128,32,128]{2,1,0:T(8,128)S(1)}, u32[]{:S(2)}, u32[]{:S(2)}) async-start(f32[128,32,128]{2,1,0:T(8,128)} %pad_maximum_fusion), calls=%async_computation | async-start | bytes 4194304 | tf_op jit(solution)/shard_map/all_to_all | solution.py:526
  35.6 1.7 collective-permute-done.1
  40.2 1.8 collective-permute-start.4
  43.2 4.0 %collective-permute-done.2 = f32[8,4,8,128]{3,2,1,0:T(8,128)S(1)} collective-permute-done((f32[8,4,8,128]{3,2,1,0:T(8,128)S(1)}, f32[8,4,8,128]{3,2,1,0:T(8,128)S(1)}, u32[]{:S(2)}, u32[]{:S(2)}) %collective-permute-start.2) | collective-permute-done | bytes 131104 | tf_op jit(solution)/shard_map/ppermute | solution.py:594
  47.7 3.8 %collective-permute-done.3 = f32[8,4,8,128]{3,2,1,0:T(8,128)S(1)} collective-permute-done((f32[8,4,8,128]{3,2,1,0:T(8,128)S(1)}, f32[8,4,8,128]{3,2,1,0:T(8,128)S(1)}, u32[]{:S(2)}, u32[]{:S(2)}) %collective-permute-start.3) | collective-permute-done | bytes 131104 | tf_op jit(solution)/shard_map/ppermute | solution.py:594
  51.6 2.4 %collective-permute-start.5 = (f32[8,8,128]{2,1,0:T(8,128)S(1)}, f32[8,8,128]{2,1,0:T(8,128)S(1)}, u32[]{:S(2)}, u32[]{:S(2)}) collective-permute-start(f32[8,8,128]{2,1,0:T(8,128)S(1)} %get-tuple-element.35), channel_id=1, source_target_pairs={{0,8},{4,12},{8,16},{12,20},{16,24},{20,28},{24,0},{28,4},{32,40},... | collective-permute-start | bytes 98312 | tf_op jit(solution)/shard_map/ppermute | solution.py:594
  53.9 2.4 %collective-permute-start.7 = (f32[8,8,128]{2,1,0:T(8,128)S(1)}, f32[8,8,128]{2,1,0:T(8,128)S(1)}, u32[]{:S(2)}, u32[]{:S(2)}) collective-permute-start(f32[8,8,128]{2,1,0:T(8,128)S(1)} %get-tuple-element.36), channel_id=1, source_target_pairs={{0,24},{4,28},{8,0},{12,4},{16,8},{20,12},{24,16},{28,20},{32,56},... | collective-permute-start | bytes 98312 | tf_op jit(solution)/shard_map/ppermute | solution.py:594
  58.1 3.3 %collective-permute-done.6 = f32[8,8,128]{2,1,0:T(8,128)S(1)} collective-permute-done((f32[8,8,128]{2,1,0:T(8,128)S(1)}, f32[8,8,128]{2,1,0:T(8,128)S(1)}, u32[]{:S(2)}, u32[]{:S(2)}) %collective-permute-start.6) | collective-permute-done | bytes 32800 | tf_op jit(solution)/shard_map/ppermute | solution.py:594
  61.5 21.2 %all-to-all-done = f32[128,32,128]{2,1,0:T(8,128)S(1)} async-done(((f32[128,32,128]{2,1,0:T(8,128)}), f32[128,32,128]{2,1,0:T(8,128)S(1)}, u32[]{:S(2)}, u32[]{:S(2)}) %all-to-all-start) | async-done | bytes 2097184 | tf_op jit(solution)/shard_map/all_to_all | solution.py:526
  82.7 3.2 %overlap.1 = (f32[16,256,128]{2,1,0:T(8,128)S(1)}, f32[544,128]{1,0:T(8,128)S(1)}) custom-call(s32[1]{0:T(128)} %bitcast.core_ref, f32[4096,128]{1,0:T(8,128)S(1)} %bitcast.43), custom_call_target="tpu_custom_call" | custom-call | flops 1610612736 | bytes 4194304 | tf_op jit(solution)/shard_map/overlap/pallas_call | solution.py:316
  87.3 16.4 %all_to_all.25 = f32[32,1,2176]{2,1,0:T(1,128)S(1)} all-to-all(f32[32,1,2176]{2,1,0:T(1,128)S(1)} %bitcast.46), channel_id=1, replica_groups={{0,1,2,3,4,5,6,7,8,9,10,11,12,13,14,15,16,17,18,19,20,21,22,23,24,25,26..., dimensions={0} | all-to-all | bytes 557056 | tf_op jit(solution)/shard_map/all_to_all | solution.py:526
  104.0 10.1 %all_to_all.26 = f32[8,1,3200]{2,1,0:T(1,128)S(1)} all-to-all(f32[8,1,3200]{2,1,0:T(1,128)S(1)} %pad_maximum_fusion.1), channel_id=1, replica_groups={{0,32,64,96,128,160,192,224},{4,36,68,100,132,164,196,228},{8,40,72,104..., dimensions={0} | all-to-all | bytes 204800 | tf_op jit(solution)/shard_map/all_to_all | solution.py:526
  114.4 14.4 %all_to_all.27 = f32[32,1,2176]{2,1,0:T(1,128)S(1)} all-to-all(f32[32,1,2176]{2,1,0:T(1,128)S(1)} %broadcast_in_dim.8), channel_id=1, replica_groups={{0,1,2,3,4,5,6,7,8,9,10,11,12,13,14,15,16,17,18,19,20,21,22,23,24,25,26..., dimensions={0} | all-to-all | bytes 557056 | tf_op jit(solution)/shard_map/all_to_all | solution.py:526
  128.8 15.1 %solve.1 = (f32[4096,128]{1,0:T(8,128)S(1)}, f32[256,256]{1,0:T(8,128)}) custom-call(f32[544,128]{1,0:T(8,128)S(1)} %bitcast.45, f32[16,256,128]{2,1,0:T(8,128)S(1)} %copy-done.4), custom_call_target="tpu_custom_call" | custom-call | flops 20000000000 | bytes 6291456 | tf_op jit(solution)/shard_map/solve/pallas_call | solution.py:465
  143.9 1.3 copy-done
  145.2 6.2 %all-to-all-start.4 = ((f32[128,32,128]{2,1,0:T(8,128)}), f32[128,32,128]{2,1,0:T(8,128)S(1)}, u32[]{:S(2)}, u32[]{:S(2)}) async-start(f32[128,32,128]{2,1,0:T(8,128)} %bitcast.44), calls=%async_computation.4 | async-start | bytes 4194304 | tf_op jit(solution)/shard_map/all_to_all | solution.py:526
  152.2 49.5 %all-to-all-done.4.arrived_ref = f32[128,32,128]{2,1,0:T(8,128)S(1)} async-done(((f32[128,32,128]{2,1,0:T(8,128)}), f32[128,32,128]{2,1,0:T(8,128)S(1)}, u32[]{:S(2)}, u32[]{:S(2)}) %all-to-all-start.4) | async-done | bytes 2097184 | tf_op jit(solution)/shard_map/all_to_all | solution.py:526
  201.7 3.9 %collective-permute-start.8 = (f32[128,16,128]{2,1,0:T(8,128)S(1)}, f32[128,16,128]{2,1,0:T(8,128)S(1)}, u32[]{:S(2)}, u32[]{:S(2)}) collective-permute-start(f32[128,16,128]{2,1,0:T(8,128)S(1)} %constant_dynamic-slice_fusion), channel_id=1, source_target_pairs={{0,4},{4,0},{8,12},{12,8},{16,20},{20,16},{24,28},{28,24},{32,36},... | collective-permute-start | bytes 3145736 | tf_op jit(solution)/shard_map/ppermute | solution.py:582
  205.7 2.3 %collective-permute-done.8.received_ref = f32[128,16,128]{2,1,0:T(8,128)S(1)} collective-permute-done((f32[128,16,128]{2,1,0:T(8,128)S(1)}, f32[128,16,128]{2,1,0:T(8,128)S(1)}, u32[]{:S(2)}, u32[]{:S(2)}) %collective-permute-start.8) | collective-permute-done | bytes 1048608 | tf_op jit(solution)/shard_map/ppermute | solution.py:582
  207.9 1.4 assemble.1
  (40 shorter events, 13.1 us)
Async XLA Ops:
  0.7 0.7 copy-start.1
  1.4 1.1 copy-start.2
  11.4 5.6 %collective-permute-start = (f32[128,16,128]{2,1,0:T(8,128)S(1)}, f32[128,16,128]{2,1,0:T(8,128)S(1)}, u32[]{:S(2)}, u32[]{:S(2)}) collective-permute-start(f32[128,16,128]{2,1,0:T(8,128)S(1)} %get-tuple-element.18), channel_id=1, source_target_pairs={{0,4},{4,0},{8,12},{12,8},{16,20},{20,16},{24,28},{28,24},{32,36},... | collective-permute-start | bytes 3145736 | tf_op jit(solution)/shard_map/ppermute | solution.py:582
  18.7 14.0 %copy-start.6 = (f32[256]{0:T(256)S(1)}, f32[256]{0:T(256)}, u32[]{:S(2)}) copy-start(f32[256]{0:T(256)} %param.7) | copy-start | bytes 3076
  18.7 64.0 %all-to-all-start = ((f32[128,32,128]{2,1,0:T(8,128)}), f32[128,32,128]{2,1,0:T(8,128)S(1)}, u32[]{:S(2)}, u32[]{:S(2)}) async-start(f32[128,32,128]{2,1,0:T(8,128)} %pad_maximum_fusion), calls=%async_computation | async-start | bytes 4194304 | tf_op jit(solution)/shard_map/all_to_all | solution.py:526
  34.9 2.4 %collective-permute-start.1 = (f32[8,4,4,8,128]{4,3,1,0,2:T(8,128)}, f32[8,4,4,8,128]{4,3,1,0,2:T(8,128)S(1)}, u32[]{:S(2)}, u32[]{:S(2)}) collective-permute-start(f32[8,4,4,8,128]{4,3,1,0,2:T(8,128)} %bitcast.42), channel_id=1, source_target_pairs={{0,4},{4,0},{8,12},{12,8},{16,20},{20,16},{24,28},{28,24},{32,36},... | collective-permute-start | bytes 1572872 | tf_op jit(solution)/shard_map/ppermute | solution.py:594
  37.3 0.8 copy-start.5
  39.3 7.9 %collective-permute-start.2 = (f32[8,4,8,128]{3,2,1,0:T(8,128)S(1)}, f32[8,4,8,128]{3,2,1,0:T(8,128)S(1)}, u32[]{:S(2)}, u32[]{:S(2)}) collective-permute-start(f32[8,4,8,128]{3,2,1,0:T(8,128)S(1)} %get-tuple-element.32), channel_id=1, source_target_pairs={{0,1},{1,2},{2,3},{3,0},{4,5},{5,6},{6,7},{7,4},{8,9},{9,10},{10,1... | collective-permute-start | bytes 393224 | tf_op jit(solution)/shard_map/ppermute | solution.py:594
  40.2 7.5 %collective-permute-start.4 = (f32[8,4,8,128]{3,2,1,0:T(8,128)S(1)}, f32[8,4,8,128]{3,2,1,0:T(8,128)S(1)}, u32[]{:S(2)}, u32[]{:S(2)}) collective-permute-start(f32[8,4,8,128]{3,2,1,0:T(8,128)S(1)} %get-tuple-element.33), channel_id=1, source_target_pairs={{0,3},{1,0},{2,1},{3,2},{4,7},{5,4},{6,5},{7,6},{8,11},{9,8},{10,9... | collective-permute-start | bytes 393224 | tf_op jit(solution)/shard_map/ppermute | solution.py:594
  42.0 9.5 %collective-permute-start.3 = (f32[8,4,8,128]{3,2,1,0:T(8,128)S(1)}, f32[8,4,8,128]{3,2,1,0:T(8,128)S(1)}, u32[]{:S(2)}, u32[]{:S(2)}) collective-permute-start(f32[8,4,8,128]{3,2,1,0:T(8,128)S(1)} %get-tuple-element.34), channel_id=1, source_target_pairs={{0,2},{1,3},{2,0},{3,1},{4,6},{5,7},{6,4},{7,5},{8,10},{9,11},{10,... | collective-permute-start | bytes 393224 | tf_op jit(solution)/shard_map/ppermute | solution.py:594
  51.6 6.6 %collective-permute-start.5 = (f32[8,8,128]{2,1,0:T(8,128)S(1)}, f32[8,8,128]{2,1,0:T(8,128)S(1)}, u32[]{:S(2)}, u32[]{:S(2)}) collective-permute-start(f32[8,8,128]{2,1,0:T(8,128)S(1)} %get-tuple-element.35), channel_id=1, source_target_pairs={{0,8},{4,12},{8,16},{12,20},{16,24},{20,28},{24,0},{28,4},{32,40},... | collective-permute-start | bytes 98312 | tf_op jit(solution)/shard_map/ppermute | solution.py:594
  53.9 4.2 %collective-permute-start.7 = (f32[8,8,128]{2,1,0:T(8,128)S(1)}, f32[8,8,128]{2,1,0:T(8,128)S(1)}, u32[]{:S(2)}, u32[]{:S(2)}) collective-permute-start(f32[8,8,128]{2,1,0:T(8,128)S(1)} %get-tuple-element.36), channel_id=1, source_target_pairs={{0,24},{4,28},{8,0},{12,4},{16,8},{20,12},{24,16},{28,20},{32,56},... | collective-permute-start | bytes 98312 | tf_op jit(solution)/shard_map/ppermute | solution.py:594
  56.3 5.1 %collective-permute-start.6 = (f32[8,8,128]{2,1,0:T(8,128)S(1)}, f32[8,8,128]{2,1,0:T(8,128)S(1)}, u32[]{:S(2)}, u32[]{:S(2)}) collective-permute-start(f32[8,8,128]{2,1,0:T(8,128)S(1)} %get-tuple-element.37), channel_id=1, source_target_pairs={{0,16},{4,20},{8,24},{12,28},{16,0},{20,4},{24,8},{28,12},{32,48},... | collective-permute-start | bytes 98312 | tf_op jit(solution)/shard_map/ppermute | solution.py:594
  85.9 1.3 copy-start.3
  87.3 41.5 %copy-start.4 = (f32[16,256,128]{2,1,0:T(8,128)S(1)}, f32[16,256,128]{2,1,0:T(8,128)}, u32[]{:S(2)}) copy-start(f32[16,256,128]{2,1,0:T(8,128)} %copy-done.3) | copy-start | bytes 6291460
  143.9 1.3 copy-start
  145.2 56.4 %all-to-all-start.4 = ((f32[128,32,128]{2,1,0:T(8,128)}), f32[128,32,128]{2,1,0:T(8,128)S(1)}, u32[]{:S(2)}, u32[]{:S(2)}) async-start(f32[128,32,128]{2,1,0:T(8,128)} %bitcast.44), calls=%async_computation.4 | async-start | bytes 4194304 | tf_op jit(solution)/shard_map/all_to_all | solution.py:526
  201.7 6.2 %collective-permute-start.8 = (f32[128,16,128]{2,1,0:T(8,128)S(1)}, f32[128,16,128]{2,1,0:T(8,128)S(1)}, u32[]{:S(2)}, u32[]{:S(2)}) collective-permute-start(f32[128,16,128]{2,1,0:T(8,128)S(1)} %constant_dynamic-slice_fusion), channel_id=1, source_target_pairs={{0,4},{4,0},{8,12},{12,8},{16,20},{20,16},{24,28},{28,24},{32,36},... | collective-permute-start | bytes 3145736 | tf_op jit(solution)/shard_map/ppermute | solution.py:582

commit v7 on v6

--- a/solution.py
+++ b/solution.py
@@ -14,6 +14,7 @@
 PAIRS = G * G // LANES
 PAD = 8
 SHIFT = 2
+WINDOW = 2 * SHIFT + 2
 STRIP = 16
 ROWS = 8
 BLOCK = 64
@@ -62,12 +63,23 @@
     return high, low
 
 
+def paired(matrix):
+    blocks = matrix.reshape(2 * SHIFT + 1, LANES, LANES)
+    both = np.zeros((WINDOW, LANES, 2, LANES))
+    for shift in range(2 * SHIFT + 1):
+        for row in range(2):
+            both[shift + row, :, row, :] = blocks[shift]
+    return both.reshape(WINDOW * LANES, 2 * LANES)
+
+
 def filter_constants():
     magic = shifted_blocks(magic_taps, banded(G, magic_taps))
     kinetic = shifted_blocks(kinetic_taps, np.eye(G)) + shifted_blocks(
         (1.0,), banded(G, kinetic_taps)
     )
-    return np.concatenate(split_constant(np.concatenate([magic, kinetic], axis=1)), axis=1)
+    return np.concatenate(
+        split_constant(np.concatenate([paired(magic), paired(kinetic)], axis=1)), axis=1
+    )
 
 
 def plane_filter(read, first, taps):
@@ -123,22 +135,35 @@
     filtered[:margin] = zeros
     filtered[margin + G :] = zeros
 
-    def product(x, width):
+    def product(x, kinds):
         shifted = jnp.concatenate(
             [
-                source[pl.ds(margin + x, STRIP), PAD + s : PAD + s + PAIRS].reshape(
-                    STRIP * PAIRS, LANES
-                )
-                for s in range(-SHIFT, SHIFT + 1)
+                source[
+                    pl.ds(margin + x, STRIP), pl.ds(PAD + s, PAIRS // 2, stride=2), :
+                ].reshape(STRIP * PAIRS // 2, LANES)
+                for s in range(-SHIFT, WINDOW - SHIFT)
             ],
             axis=1,
         )
         high = shifted.astype(jnp.bfloat16)
         low = (shifted - high.astype(jnp.float32)).astype(jnp.bfloat16)
         dot = functools.partial(jnp.dot, preferred_element_type=jnp.float32)
+        width = 2 * kinds * LANES
         high_filter = filters_ref[:, :width]
-        low_filter = filters_ref[:, 2 * LANES : 2 * LANES + width]
-        return dot(high, high_filter) + (dot(low, high_filter) + dot(high, low_filter))
+        low_filter = filters_ref[:, 4 * LANES : 4 * LANES + width]
+        out = dot(high, high_filter) + (dot(low, high_filter) + dot(high, low_filter))
+        return [
+            [
+                out[:, (2 * kind + odd) * LANES : (2 * kind + odd + 1) * LANES].reshape(
+                    STRIP, PAIRS // 2, LANES
+                )
+                for odd in range(2)
+            ]
+            for kind in range(kinds)
+        ]
+
+    def every_second(odd):
+        return pl.ds(odd, PAIRS // 2, stride=2)
 
     def own(x):
         return source[pl.ds(margin + x, STRIP), PAD : PAD + PAIRS]
@@ -176,11 +201,11 @@
     def _(x):
         cells = pl.ds(pl.multiple_of(x * G, STRIP * G), STRIP * G)
         lines_ref[cells, :] = potential_ref[:, cells].T
-        both = product(x, 2 * LANES)
-        filtered[pl.ds(margin + x, STRIP)] = both[:, :LANES].reshape(STRIP, PAIRS, LANES)
-        kinetic[pl.ds(x, STRIP)] = both[:, LANES:].reshape(STRIP, PAIRS, LANES) + plane_filter(
-            own, x, kinetic_taps
-        )
+        kinetic[pl.ds(x, STRIP)] = plane_filter(own, x, kinetic_taps)
+        magic_rows, kinetic_rows = product(x, 2)
+        for odd in range(2):
+            filtered[pl.ds(margin + x, STRIP), every_second(odd), :] = magic_rows[odd]
+            kinetic[pl.ds(x, STRIP), every_second(odd), :] += kinetic_rows[odd]
 
     lines = STRIP * G // 2
 
@@ -195,9 +220,9 @@
 
     @pl.loop(0, G, step=STRIP)
     def _(x):
-        filtered[pl.ds(margin + x, STRIP)] = product(x, LANES).reshape(
-            STRIP, PAIRS, LANES
-        )
+        (magic_rows,) = product(x, 1)
+        for odd in range(2):
+            filtered[pl.ds(margin + x, STRIP), every_second(odd), :] = magic_rows[odd]
 
     for side, out_ref in ((core, keep_ref), (1 - core, give_ref)):
         for strip in range(0, half_planes, STRIP):

time: 210 us -> 209 us (level)
    unnamed x14 -> x12, local copies, waits for them, and re-layouts: 5.23 us -> 4.15 us
where the time goes in v7:
time: 209 us; the launch traced here: 208 us
  waiting for transfers between devices  89.4 us (43%)
  blocking collectives  41 us (20%)
  starting transfers between devices  37.8 us (18%)
  Pallas kernels  28.3 us (14%)
  local copies, waits for them, and re-layouts  6.71 us (3%)
  other arithmetic  3.29 us (2%)
    all_to_all x2, waiting for transfers between devices, exchange(): lax.all_to_all(blocks, axes, split_axis=0, concat_axis=0, tiled=True, axi...  70.7 us
    all_to_all x3, blocking collectives, exchange(): lax.all_to_all(blocks, axes, split_axis=0, concat_axis=0, tiled=True, axi...  41 us
    all_to_all x2, starting transfers between devices, exchange(): lax.all_to_all(blocks, axes, split_axis=0, concat_axis=0, tiled=True, axi...  20.1 us
    pallas_call x1, Pallas kernels, solve(): pl.pallas_call(functools.partial(solve_kernel, cells), out_shape=(jax.Sha...  15.1 us
    ppermute x7, waiting for transfers between devices, stage(): lax.ppermute(lax.dynamic_index_in_dim(values, (index + k) % count, dim, k...  14.1 us
    ppermute x7, starting transfers between devices, stage(): lax.ppermute(lax.dynamic_index_in_dim(values, (index + k) % count, dim, k...  10.4 us
    pallas_call x1, Pallas kernels, apply_hamiltonian(): pl.pallas_call(hamiltonian_kernel, out_shape=(side, side, grid), in_specs...  8.64 us
    ppermute x2, starting transfers between devices, swap_cores(): return lax.ppermute(values, 'orb', pairs)  7.28 us
  transfers between devices with their start and end apart: 11, of which 10 were waited for; matrix products, arithmetic and copies ran while one was open for 2% of the time, Pallas kernels for 0%

profile of v7, /device:TPU:1, one launch (start us, length us, event | category | flops | bytes accessed | tf_op | source)
XLA Modules:
  0.0 208.1 jit_solution(14978328913303854388)
XLA Ops:
  1.4 8.6 %hamiltonian.1 = (f32[128,16,128]{2,1,0:T(8,128)S(1)}, f32[128,16,128]{2,1,0:T(8,128)S(1)}, f32[64,32,128]{2,1,0:T(8,128)S(1)}) custom-call(s32[2]{0:T(128)S(1)} %pad_add_fusion.place_ref, s32[2,256]{1,0:T(2,128)S(1)} %bitcast.47, f32[64,32,128]{2,1,0:T(8,128)} %bitcast.50, bf16[768,1024]{1,0:T(8,128)(2,1)} %constant.116.clone.filters_hbm, f32[64,4096]{1,0:T(8,128)} %bitcast.51), custom_call_target="tpu_custom_call" | custom-call | flops 3019898880 | bytes 5242880 | tf_op jit(solution)/shard_map/hamiltonian/pallas_call | solution.py:253
  10.1 3.3 %collective-permute-start = (f32[128,16,128]{2,1,0:T(8,128)S(1)}, f32[128,16,128]{2,1,0:T(8,128)S(1)}, u32[]{:S(2)}, u32[]{:S(2)}) collective-permute-start(f32[128,16,128]{2,1,0:T(8,128)S(1)} %get-tuple-element.18), channel_id=1, source_target_pairs={{0,4},{4,0},{8,12},{12,8},{16,20},{20,16},{24,28},{28,24},{32,36},... | collective-permute-start | bytes 3145736 | tf_op jit(solution)/shard_map/ppermute | solution.py:607
  13.4 2.3 %collective-permute-done = f32[128,16,128]{2,1,0:T(8,128)S(1)} collective-permute-done((f32[128,16,128]{2,1,0:T(8,128)S(1)}, f32[128,16,128]{2,1,0:T(8,128)S(1)}, u32[]{:S(2)}, u32[]{:S(2)}) %collective-permute-start) | collective-permute-done | bytes 1048608 | tf_op jit(solution)/shard_map/ppermute | solution.py:607
  15.7 1.7 pad_maximum_fusion
  17.3 13.9 %all-to-all-start = ((f32[128,32,128]{2,1,0:T(8,128)}), f32[128,32,128]{2,1,0:T(8,128)S(1)}, u32[]{:S(2)}, u32[]{:S(2)}) async-start(f32[128,32,128]{2,1,0:T(8,128)} %pad_maximum_fusion), calls=%async_computation | async-start | bytes 4194304 | tf_op jit(solution)/shard_map/all_to_all | solution.py:551
  34.2 1.7 collective-permute-done.1
  38.8 1.8 collective-permute-start.4
  41.8 4.0 %collective-permute-done.2 = f32[8,4,8,128]{3,2,1,0:T(8,128)S(1)} collective-permute-done((f32[8,4,8,128]{3,2,1,0:T(8,128)S(1)}, f32[8,4,8,128]{3,2,1,0:T(8,128)S(1)}, u32[]{:S(2)}, u32[]{:S(2)}) %collective-permute-start.2) | collective-permute-done | bytes 131104 | tf_op jit(solution)/shard_map/ppermute | solution.py:619
  46.3 3.8 %collective-permute-done.3 = f32[8,4,8,128]{3,2,1,0:T(8,128)S(1)} collective-permute-done((f32[8,4,8,128]{3,2,1,0:T(8,128)S(1)}, f32[8,4,8,128]{3,2,1,0:T(8,128)S(1)}, u32[]{:S(2)}, u32[]{:S(2)}) %collective-permute-start.3) | collective-permute-done | bytes 131104 | tf_op jit(solution)/shard_map/ppermute | solution.py:619
  50.2 2.4 %collective-permute-start.5 = (f32[8,8,128]{2,1,0:T(8,128)S(1)}, f32[8,8,128]{2,1,0:T(8,128)S(1)}, u32[]{:S(2)}, u32[]{:S(2)}) collective-permute-start(f32[8,8,128]{2,1,0:T(8,128)S(1)} %get-tuple-element.35), channel_id=1, source_target_pairs={{0,8},{4,12},{8,16},{12,20},{16,24},{20,28},{24,0},{28,4},{32,40},... | collective-permute-start | bytes 98312 | tf_op jit(solution)/shard_map/ppermute | solution.py:619
  52.6 2.4 %collective-permute-start.7 = (f32[8,8,128]{2,1,0:T(8,128)S(1)}, f32[8,8,128]{2,1,0:T(8,128)S(1)}, u32[]{:S(2)}, u32[]{:S(2)}) collective-permute-start(f32[8,8,128]{2,1,0:T(8,128)S(1)} %get-tuple-element.36), channel_id=1, source_target_pairs={{0,24},{4,28},{8,0},{12,4},{16,8},{20,12},{24,16},{28,20},{32,56},... | collective-permute-start | bytes 98312 | tf_op jit(solution)/shard_map/ppermute | solution.py:619
  56.8 3.3 %collective-permute-done.6 = f32[8,8,128]{2,1,0:T(8,128)S(1)} collective-permute-done((f32[8,8,128]{2,1,0:T(8,128)S(1)}, f32[8,8,128]{2,1,0:T(8,128)S(1)}, u32[]{:S(2)}, u32[]{:S(2)}) %collective-permute-start.6) | collective-permute-done | bytes 32800 | tf_op jit(solution)/shard_map/ppermute | solution.py:619
  60.1 21.2 %all-to-all-done = f32[128,32,128]{2,1,0:T(8,128)S(1)} async-done(((f32[128,32,128]{2,1,0:T(8,128)}), f32[128,32,128]{2,1,0:T(8,128)S(1)}, u32[]{:S(2)}, u32[]{:S(2)}) %all-to-all-start) | async-done | bytes 2097184 | tf_op jit(solution)/shard_map/all_to_all | solution.py:551
  81.4 3.2 %overlap.1 = (f32[16,256,128]{2,1,0:T(8,128)S(1)}, f32[544,128]{1,0:T(8,128)S(1)}) custom-call(s32[1]{0:T(128)} %bitcast.core_ref, f32[4096,128]{1,0:T(8,128)S(1)} %bitcast.43), custom_call_target="tpu_custom_call" | custom-call | flops 1610612736 | bytes 4194304 | tf_op jit(solution)/shard_map/overlap/pallas_call | solution.py:341
  85.9 16.4 %all_to_all.25 = f32[32,1,2176]{2,1,0:T(1,128)S(1)} all-to-all(f32[32,1,2176]{2,1,0:T(1,128)S(1)} %bitcast.46), channel_id=1, replica_groups={{0,1,2,3,4,5,6,7,8,9,10,11,12,13,14,15,16,17,18,19,20,21,22,23,24,25,26..., dimensions={0} | all-to-all | bytes 557056 | tf_op jit(solution)/shard_map/all_to_all | solution.py:551
  102.6 10.1 %all_to_all.26 = f32[8,1,3200]{2,1,0:T(1,128)S(1)} all-to-all(f32[8,1,3200]{2,1,0:T(1,128)S(1)} %pad_maximum_fusion.1), channel_id=1, replica_groups={{0,32,64,96,128,160,192,224},{4,36,68,100,132,164,196,228},{8,40,72,104..., dimensions={0} | all-to-all | bytes 204800 | tf_op jit(solution)/shard_map/all_to_all | solution.py:551
  113.0 14.4 %all_to_all.27 = f32[32,1,2176]{2,1,0:T(1,128)S(1)} all-to-all(f32[32,1,2176]{2,1,0:T(1,128)S(1)} %broadcast_in_dim.8), channel_id=1, replica_groups={{0,1,2,3,4,5,6,7,8,9,10,11,12,13,14,15,16,17,18,19,20,21,22,23,24,25,26..., dimensions={0} | all-to-all | bytes 557056 | tf_op jit(solution)/shard_map/all_to_all | solution.py:551
  127.5 15.1 %solve.1 = (f32[4096,128]{1,0:T(8,128)S(1)}, f32[256,256]{1,0:T(8,128)}) custom-call(f32[544,128]{1,0:T(8,128)S(1)} %bitcast.45, f32[16,256,128]{2,1,0:T(8,128)S(1)} %copy-done.3), custom_call_target="tpu_custom_call" | custom-call | flops 20000000000 | bytes 6291456 | tf_op jit(solution)/shard_map/solve/pallas_call | solution.py:490
  142.6 1.3 copy-done
  143.9 6.2 %all-to-all-start.4 = ((f32[128,32,128]{2,1,0:T(8,128)}), f32[128,32,128]{2,1,0:T(8,128)S(1)}, u32[]{:S(2)}, u32[]{:S(2)}) async-start(f32[128,32,128]{2,1,0:T(8,128)} %bitcast.44), calls=%async_computation.4 | async-start | bytes 4194304 | tf_op jit(solution)/shard_map/all_to_all | solution.py:551
  150.8 49.5 %all-to-all-done.4.arrived_ref = f32[128,32,128]{2,1,0:T(8,128)S(1)} async-done(((f32[128,32,128]{2,1,0:T(8,128)}), f32[128,32,128]{2,1,0:T(8,128)S(1)}, u32[]{:S(2)}, u32[]{:S(2)}) %all-to-all-start.4) | async-done | bytes 2097184 | tf_op jit(solution)/shard_map/all_to_all | solution.py:551
  200.4 3.9 %collective-permute-start.8 = (f32[128,16,128]{2,1,0:T(8,128)S(1)}, f32[128,16,128]{2,1,0:T(8,128)S(1)}, u32[]{:S(2)}, u32[]{:S(2)}) collective-permute-start(f32[128,16,128]{2,1,0:T(8,128)S(1)} %constant_dynamic-slice_fusion), channel_id=1, source_target_pairs={{0,4},{4,0},{8,12},{12,8},{16,20},{20,16},{24,28},{28,24},{32,36},... | collective-permute-start | bytes 3145736 | tf_op jit(solution)/shard_map/ppermute | solution.py:607
  204.3 2.3 %collective-permute-done.8.received_ref = f32[128,16,128]{2,1,0:T(8,128)S(1)} collective-permute-done((f32[128,16,128]{2,1,0:T(8,128)S(1)}, f32[128,16,128]{2,1,0:T(8,128)S(1)}, u32[]{:S(2)}, u32[]{:S(2)}) %collective-permute-start.8) | collective-permute-done | bytes 1048608 | tf_op jit(solution)/shard_map/ppermute | solution.py:607
  206.6 1.4 assemble.1
  (38 shorter events, 12.0 us)
Async XLA Ops:
  0.7 0.7 copy-start.1
  10.1 5.6 %collective-permute-start = (f32[128,16,128]{2,1,0:T(8,128)S(1)}, f32[128,16,128]{2,1,0:T(8,128)S(1)}, u32[]{:S(2)}, u32[]{:S(2)}) collective-permute-start(f32[128,16,128]{2,1,0:T(8,128)S(1)} %get-tuple-element.18), channel_id=1, source_target_pairs={{0,4},{4,0},{8,12},{12,8},{16,20},{20,16},{24,28},{28,24},{32,36},... | collective-permute-start | bytes 3145736 | tf_op jit(solution)/shard_map/ppermute | solution.py:607
  17.3 13.9 %copy-start.5 = (f32[256]{0:T(256)S(1)}, f32[256]{0:T(256)}, u32[]{:S(2)}) copy-start(f32[256]{0:T(256)} %param.7) | copy-start | bytes 3076
  17.3 64.0 %all-to-all-start = ((f32[128,32,128]{2,1,0:T(8,128)}), f32[128,32,128]{2,1,0:T(8,128)S(1)}, u32[]{:S(2)}, u32[]{:S(2)}) async-start(f32[128,32,128]{2,1,0:T(8,128)} %pad_maximum_fusion), calls=%async_computation | async-start | bytes 4194304 | tf_op jit(solution)/shard_map/all_to_all | solution.py:551
  33.6 2.4 %collective-permute-start.1 = (f32[8,4,4,8,128]{4,3,1,0,2:T(8,128)}, f32[8,4,4,8,128]{4,3,1,0,2:T(8,128)S(1)}, u32[]{:S(2)}, u32[]{:S(2)}) collective-permute-start(f32[8,4,4,8,128]{4,3,1,0,2:T(8,128)} %bitcast.42), channel_id=1, source_target_pairs={{0,4},{4,0},{8,12},{12,8},{16,20},{20,16},{24,28},{28,24},{32,36},... | collective-permute-start | bytes 1572872 | tf_op jit(solution)/shard_map/ppermute | solution.py:619
  36.0 0.8 copy-start.4
  37.9 7.9 %collective-permute-start.2 = (f32[8,4,8,128]{3,2,1,0:T(8,128)S(1)}, f32[8,4,8,128]{3,2,1,0:T(8,128)S(1)}, u32[]{:S(2)}, u32[]{:S(2)}) collective-permute-start(f32[8,4,8,128]{3,2,1,0:T(8,128)S(1)} %get-tuple-element.32), channel_id=1, source_target_pairs={{0,1},{1,2},{2,3},{3,0},{4,5},{5,6},{6,7},{7,4},{8,9},{9,10},{10,1... | collective-permute-start | bytes 393224 | tf_op jit(solution)/shard_map/ppermute | solution.py:619
  38.8 7.5 %collective-permute-start.4 = (f32[8,4,8,128]{3,2,1,0:T(8,128)S(1)}, f32[8,4,8,128]{3,2,1,0:T(8,128)S(1)}, u32[]{:S(2)}, u32[]{:S(2)}) collective-permute-start(f32[8,4,8,128]{3,2,1,0:T(8,128)S(1)} %get-tuple-element.33), channel_id=1, source_target_pairs={{0,3},{1,0},{2,1},{3,2},{4,7},{5,4},{6,5},{7,6},{8,11},{9,8},{10,9... | collective-permute-start | bytes 393224 | tf_op jit(solution)/shard_map/ppermute | solution.py:619
  40.7 9.5 %collective-permute-start.3 = (f32[8,4,8,128]{3,2,1,0:T(8,128)S(1)}, f32[8,4,8,128]{3,2,1,0:T(8,128)S(1)}, u32[]{:S(2)}, u32[]{:S(2)}) collective-permute-start(f32[8,4,8,128]{3,2,1,0:T(8,128)S(1)} %get-tuple-element.34), channel_id=1, source_target_pairs={{0,2},{1,3},{2,0},{3,1},{4,6},{5,7},{6,4},{7,5},{8,10},{9,11},{10,... | collective-permute-start | bytes 393224 | tf_op jit(solution)/shard_map/ppermute | solution.py:619
  50.2 6.6 %collective-permute-start.5 = (f32[8,8,128]{2,1,0:T(8,128)S(1)}, f32[8,8,128]{2,1,0:T(8,128)S(1)}, u32[]{:S(2)}, u32[]{:S(2)}) collective-permute-start(f32[8,8,128]{2,1,0:T(8,128)S(1)} %get-tuple-element.35), channel_id=1, source_target_pairs={{0,8},{4,12},{8,16},{12,20},{16,24},{20,28},{24,0},{28,4},{32,40},... | collective-permute-start | bytes 98312 | tf_op jit(solution)/shard_map/ppermute | solution.py:619
  52.6 4.2 %collective-permute-start.7 = (f32[8,8,128]{2,1,0:T(8,128)S(1)}, f32[8,8,128]{2,1,0:T(8,128)S(1)}, u32[]{:S(2)}, u32[]{:S(2)}) collective-permute-start(f32[8,8,128]{2,1,0:T(8,128)S(1)} %get-tuple-element.36), channel_id=1, source_target_pairs={{0,24},{4,28},{8,0},{12,4},{16,8},{20,12},{24,16},{28,20},{32,56},... | collective-permute-start | bytes 98312 | tf_op jit(solution)/shard_map/ppermute | solution.py:619
  55.0 5.1 %collective-permute-start.6 = (f32[8,8,128]{2,1,0:T(8,128)S(1)}, f32[8,8,128]{2,1,0:T(8,128)S(1)}, u32[]{:S(2)}, u32[]{:S(2)}) collective-permute-start(f32[8,8,128]{2,1,0:T(8,128)S(1)} %get-tuple-element.37), channel_id=1, source_target_pairs={{0,16},{4,20},{8,24},{12,28},{16,0},{20,4},{24,8},{28,12},{32,48},... | collective-permute-start | bytes 98312 | tf_op jit(solution)/shard_map/ppermute | solution.py:619
  84.6 1.3 copy-start.2
  85.9 41.5 %copy-start.3 = (f32[16,256,128]{2,1,0:T(8,128)S(1)}, f32[16,256,128]{2,1,0:T(8,128)}, u32[]{:S(2)}) copy-start(f32[16,256,128]{2,1,0:T(8,128)} %copy-done.2) | copy-start | bytes 6291460
  142.6 1.3 copy-start
  143.9 56.4 %all-to-all-start.4 = ((f32[128,32,128]{2,1,0:T(8,128)}), f32[128,32,128]{2,1,0:T(8,128)S(1)}, u32[]{:S(2)}, u32[]{:S(2)}) async-start(f32[128,32,128]{2,1,0:T(8,128)} %bitcast.44), calls=%async_computation.4 | async-start | bytes 4194304 | tf_op jit(solution)/shard_map/all_to_all | solution.py:551
  200.4 6.2 %collective-permute-start.8 = (f32[128,16,128]{2,1,0:T(8,128)S(1)}, f32[128,16,128]{2,1,0:T(8,128)S(1)}, u32[]{:S(2)}, u32[]{:S(2)}) collective-permute-start(f32[128,16,128]{2,1,0:T(8,128)S(1)} %constant_dynamic-slice_fusion), channel_id=1, source_target_pairs={{0,4},{4,0},{8,12},{12,8},{16,20},{20,16},{24,28},{28,24},{32,36},... | collective-permute-start | bytes 3145736 | tf_op jit(solution)/shard_map/ppermute | solution.py:607

commit v8 on v7

--- a/solution.py
+++ b/solution.py
@@ -15,7 +15,7 @@
 PAD = 8
 SHIFT = 2
 WINDOW = 2 * SHIFT + 2
-STRIP = 16
+STRIP = 32
 ROWS = 8
 BLOCK = 64
 

time: 209 us -> 208 us (level)
  no operation moved by 1% of the time
where the time goes in v8:
time: 208 us; the launch traced here: 207 us
  waiting for transfers between devices  89.4 us (43%)
  blocking collectives  40.8 us (20%)
  starting transfers between devices  37.8 us (18%)
  Pallas kernels  27.7 us (13%)
  local copies, waits for them, and re-layouts  6.71 us (3%)
  other arithmetic  3.29 us (2%)
    all_to_all x2, waiting for transfers between devices, exchange(): lax.all_to_all(blocks, axes, split_axis=0, concat_axis=0, tiled=True, axi...  70.7 us
    all_to_all x3, blocking collectives, exchange(): lax.all_to_all(blocks, axes, split_axis=0, concat_axis=0, tiled=True, axi...  40.8 us
    all_to_all x2, starting transfers between devices, exchange(): lax.all_to_all(blocks, axes, split_axis=0, concat_axis=0, tiled=True, axi...  20.1 us
    pallas_call x1, Pallas kernels, solve(): pl.pallas_call(functools.partial(solve_kernel, cells), out_shape=(jax.Sha...  15.1 us
    ppermute x7, waiting for transfers between devices, stage(): lax.ppermute(lax.dynamic_index_in_dim(values, (index + k) % count, dim, k...  14.1 us
    ppermute x7, starting transfers between devices, stage(): lax.ppermute(lax.dynamic_index_in_dim(values, (index + k) % count, dim, k...  10.4 us
    pallas_call x1, Pallas kernels, apply_hamiltonian(): pl.pallas_call(hamiltonian_kernel, out_shape=(side, side, grid), in_specs...  7.98 us
    ppermute x2, starting transfers between devices, swap_cores(): return lax.ppermute(values, 'orb', pairs)  7.28 us
  transfers between devices with their start and end apart: 11, of which 10 were waited for; matrix products, arithmetic and copies ran while one was open for 2% of the time, Pallas kernels for 0%

profile of v8, /device:TPU:1, one launch (start us, length us, event | category | flops | bytes accessed | tf_op | source)
XLA Modules:
  0.0 207.3 jit_solution(1086976914478682831)
XLA Ops:
  1.4 8.0 %hamiltonian.1 = (f32[128,16,128]{2,1,0:T(8,128)S(1)}, f32[128,16,128]{2,1,0:T(8,128)S(1)}, f32[64,32,128]{2,1,0:T(8,128)S(1)}) custom-call(s32[2]{0:T(128)S(1)} %pad_add_fusion.place_ref, s32[2,256]{1,0:T(2,128)S(1)} %bitcast.47, f32[64,32,128]{2,1,0:T(8,128)} %bitcast.50, bf16[768,1024]{1,0:T(8,128)(2,1)} %constant.116.clone.filters_hbm, f32[64,4096]{1,0:T(8,128)} %bitcast.51), custom_call_target="tpu_custom_call" | custom-call | flops 3019898880 | bytes 5242880 | tf_op jit(solution)/shard_map/hamiltonian/pallas_call | solution.py:253
  9.4 3.3 %collective-permute-start = (f32[128,16,128]{2,1,0:T(8,128)S(1)}, f32[128,16,128]{2,1,0:T(8,128)S(1)}, u32[]{:S(2)}, u32[]{:S(2)}) collective-permute-start(f32[128,16,128]{2,1,0:T(8,128)S(1)} %get-tuple-element.18), channel_id=1, source_target_pairs={{0,4},{4,0},{8,12},{12,8},{16,20},{20,16},{24,28},{28,24},{32,36},... | collective-permute-start | bytes 3145736 | tf_op jit(solution)/shard_map/ppermute | solution.py:607
  12.7 2.3 %collective-permute-done = f32[128,16,128]{2,1,0:T(8,128)S(1)} collective-permute-done((f32[128,16,128]{2,1,0:T(8,128)S(1)}, f32[128,16,128]{2,1,0:T(8,128)S(1)}, u32[]{:S(2)}, u32[]{:S(2)}) %collective-permute-start) | collective-permute-done | bytes 1048608 | tf_op jit(solution)/shard_map/ppermute | solution.py:607
  15.0 1.7 pad_maximum_fusion
  16.7 13.9 %all-to-all-start = ((f32[128,32,128]{2,1,0:T(8,128)}), f32[128,32,128]{2,1,0:T(8,128)S(1)}, u32[]{:S(2)}, u32[]{:S(2)}) async-start(f32[128,32,128]{2,1,0:T(8,128)} %pad_maximum_fusion), calls=%async_computation | async-start | bytes 4194304 | tf_op jit(solution)/shard_map/all_to_all | solution.py:551
  33.6 1.7 collective-permute-done.1
  38.2 1.8 collective-permute-start.4
  41.2 4.0 %collective-permute-done.2 = f32[8,4,8,128]{3,2,1,0:T(8,128)S(1)} collective-permute-done((f32[8,4,8,128]{3,2,1,0:T(8,128)S(1)}, f32[8,4,8,128]{3,2,1,0:T(8,128)S(1)}, u32[]{:S(2)}, u32[]{:S(2)}) %collective-permute-start.2) | collective-permute-done | bytes 131104 | tf_op jit(solution)/shard_map/ppermute | solution.py:619
  45.6 3.8 %collective-permute-done.3 = f32[8,4,8,128]{3,2,1,0:T(8,128)S(1)} collective-permute-done((f32[8,4,8,128]{3,2,1,0:T(8,128)S(1)}, f32[8,4,8,128]{3,2,1,0:T(8,128)S(1)}, u32[]{:S(2)}, u32[]{:S(2)}) %collective-permute-start.3) | collective-permute-done | bytes 131104 | tf_op jit(solution)/shard_map/ppermute | solution.py:619
  49.5 2.4 %collective-permute-start.5 = (f32[8,8,128]{2,1,0:T(8,128)S(1)}, f32[8,8,128]{2,1,0:T(8,128)S(1)}, u32[]{:S(2)}, u32[]{:S(2)}) collective-permute-start(f32[8,8,128]{2,1,0:T(8,128)S(1)} %get-tuple-element.35), channel_id=1, source_target_pairs={{0,8},{4,12},{8,16},{12,20},{16,24},{20,28},{24,0},{28,4},{32,40},... | collective-permute-start | bytes 98312 | tf_op jit(solution)/shard_map/ppermute | solution.py:619
  51.9 2.4 %collective-permute-start.7 = (f32[8,8,128]{2,1,0:T(8,128)S(1)}, f32[8,8,128]{2,1,0:T(8,128)S(1)}, u32[]{:S(2)}, u32[]{:S(2)}) collective-permute-start(f32[8,8,128]{2,1,0:T(8,128)S(1)} %get-tuple-element.36), channel_id=1, source_target_pairs={{0,24},{4,28},{8,0},{12,4},{16,8},{20,12},{24,16},{28,20},{32,56},... | collective-permute-start | bytes 98312 | tf_op jit(solution)/shard_map/ppermute | solution.py:619
  56.1 3.3 %collective-permute-done.6 = f32[8,8,128]{2,1,0:T(8,128)S(1)} collective-permute-done((f32[8,8,128]{2,1,0:T(8,128)S(1)}, f32[8,8,128]{2,1,0:T(8,128)S(1)}, u32[]{:S(2)}, u32[]{:S(2)}) %collective-permute-start.6) | collective-permute-done | bytes 32800 | tf_op jit(solution)/shard_map/ppermute | solution.py:619
  59.5 21.2 %all-to-all-done = f32[128,32,128]{2,1,0:T(8,128)S(1)} async-done(((f32[128,32,128]{2,1,0:T(8,128)}), f32[128,32,128]{2,1,0:T(8,128)S(1)}, u32[]{:S(2)}, u32[]{:S(2)}) %all-to-all-start) | async-done | bytes 2097184 | tf_op jit(solution)/shard_map/all_to_all | solution.py:551
  80.7 3.2 %overlap.1 = (f32[16,256,128]{2,1,0:T(8,128)S(1)}, f32[544,128]{1,0:T(8,128)S(1)}) custom-call(s32[1]{0:T(128)} %bitcast.core_ref, f32[4096,128]{1,0:T(8,128)S(1)} %bitcast.43), custom_call_target="tpu_custom_call" | custom-call | flops 1610612736 | bytes 4194304 | tf_op jit(solution)/shard_map/overlap/pallas_call | solution.py:341
  85.3 16.3 %all_to_all.25 = f32[32,1,2176]{2,1,0:T(1,128)S(1)} all-to-all(f32[32,1,2176]{2,1,0:T(1,128)S(1)} %bitcast.46), channel_id=1, replica_groups={{0,1,2,3,4,5,6,7,8,9,10,11,12,13,14,15,16,17,18,19,20,21,22,23,24,25,26..., dimensions={0} | all-to-all | bytes 557056 | tf_op jit(solution)/shard_map/all_to_all | solution.py:551
  101.8 10.1 %all_to_all.26 = f32[8,1,3200]{2,1,0:T(1,128)S(1)} all-to-all(f32[8,1,3200]{2,1,0:T(1,128)S(1)} %pad_maximum_fusion.1), channel_id=1, replica_groups={{0,32,64,96,128,160,192,224},{4,36,68,100,132,164,196,228},{8,40,72,104..., dimensions={0} | all-to-all | bytes 204800 | tf_op jit(solution)/shard_map/all_to_all | solution.py:551
  112.2 14.4 %all_to_all.27 = f32[32,1,2176]{2,1,0:T(1,128)S(1)} all-to-all(f32[32,1,2176]{2,1,0:T(1,128)S(1)} %broadcast_in_dim.8), channel_id=1, replica_groups={{0,1,2,3,4,5,6,7,8,9,10,11,12,13,14,15,16,17,18,19,20,21,22,23,24,25,26..., dimensions={0} | all-to-all | bytes 557056 | tf_op jit(solution)/shard_map/all_to_all | solution.py:551
  126.6 15.1 %solve.1 = (f32[4096,128]{1,0:T(8,128)S(1)}, f32[256,256]{1,0:T(8,128)}) custom-call(f32[544,128]{1,0:T(8,128)S(1)} %bitcast.45, f32[16,256,128]{2,1,0:T(8,128)S(1)} %copy-done.3), custom_call_target="tpu_custom_call" | custom-call | flops 20000000000 | bytes 6291456 | tf_op jit(solution)/shard_map/solve/pallas_call | solution.py:490
  141.7 1.3 copy-done
  143.1 6.2 %all-to-all-start.4 = ((f32[128,32,128]{2,1,0:T(8,128)}), f32[128,32,128]{2,1,0:T(8,128)S(1)}, u32[]{:S(2)}, u32[]{:S(2)}) async-start(f32[128,32,128]{2,1,0:T(8,128)} %bitcast.44), calls=%async_computation.4 | async-start | bytes 4194304 | tf_op jit(solution)/shard_map/all_to_all | solution.py:551
  150.0 49.5 %all-to-all-done.4.arrived_ref = f32[128,32,128]{2,1,0:T(8,128)S(1)} async-done(((f32[128,32,128]{2,1,0:T(8,128)}), f32[128,32,128]{2,1,0:T(8,128)S(1)}, u32[]{:S(2)}, u32[]{:S(2)}) %all-to-all-start.4) | async-done | bytes 2097184 | tf_op jit(solution)/shard_map/all_to_all | solution.py:551
  199.5 4.0 %collective-permute-start.8 = (f32[128,16,128]{2,1,0:T(8,128)S(1)}, f32[128,16,128]{2,1,0:T(8,128)S(1)}, u32[]{:S(2)}, u32[]{:S(2)}) collective-permute-start(f32[128,16,128]{2,1,0:T(8,128)S(1)} %constant_dynamic-slice_fusion), channel_id=1, source_target_pairs={{0,4},{4,0},{8,12},{12,8},{16,20},{20,16},{24,28},{28,24},{32,36},... | collective-permute-start | bytes 3145736 | tf_op jit(solution)/shard_map/ppermute | solution.py:607
  203.5 2.3 %collective-permute-done.8.received_ref = f32[128,16,128]{2,1,0:T(8,128)S(1)} collective-permute-done((f32[128,16,128]{2,1,0:T(8,128)S(1)}, f32[128,16,128]{2,1,0:T(8,128)S(1)}, u32[]{:S(2)}, u32[]{:S(2)}) %collective-permute-start.8) | collective-permute-done | bytes 1048608 | tf_op jit(solution)/shard_map/ppermute | solution.py:607
  205.8 1.4 assemble.1
  (38 shorter events, 12.0 us)
Async XLA Ops:
  0.7 0.7 copy-start.1
  9.4 5.6 %collective-permute-start = (f32[128,16,128]{2,1,0:T(8,128)S(1)}, f32[128,16,128]{2,1,0:T(8,128)S(1)}, u32[]{:S(2)}, u32[]{:S(2)}) collective-permute-start(f32[128,16,128]{2,1,0:T(8,128)S(1)} %get-tuple-element.18), channel_id=1, source_target_pairs={{0,4},{4,0},{8,12},{12,8},{16,20},{20,16},{24,28},{28,24},{32,36},... | collective-permute-start | bytes 3145736 | tf_op jit(solution)/shard_map/ppermute | solution.py:607
  16.7 13.9 %copy-start.5 = (f32[256]{0:T(256)S(1)}, f32[256]{0:T(256)}, u32[]{:S(2)}) copy-start(f32[256]{0:T(256)} %param.7) | copy-start | bytes 3076
  16.7 64.0 %all-to-all-start = ((f32[128,32,128]{2,1,0:T(8,128)}), f32[128,32,128]{2,1,0:T(8,128)S(1)}, u32[]{:S(2)}, u32[]{:S(2)}) async-start(f32[128,32,128]{2,1,0:T(8,128)} %pad_maximum_fusion), calls=%async_computation | async-start | bytes 4194304 | tf_op jit(solution)/shard_map/all_to_all | solution.py:551
  32.9 2.4 %collective-permute-start.1 = (f32[8,4,4,8,128]{4,3,1,0,2:T(8,128)}, f32[8,4,4,8,128]{4,3,1,0,2:T(8,128)S(1)}, u32[]{:S(2)}, u32[]{:S(2)}) collective-permute-start(f32[8,4,4,8,128]{4,3,1,0,2:T(8,128)} %bitcast.42), channel_id=1, source_target_pairs={{0,4},{4,0},{8,12},{12,8},{16,20},{20,16},{24,28},{28,24},{32,36},... | collective-permute-start | bytes 1572872 | tf_op jit(solution)/shard_map/ppermute | solution.py:619
  35.3 0.8 copy-start.4
  37.2 7.9 %collective-permute-start.2 = (f32[8,4,8,128]{3,2,1,0:T(8,128)S(1)}, f32[8,4,8,128]{3,2,1,0:T(8,128)S(1)}, u32[]{:S(2)}, u32[]{:S(2)}) collective-permute-start(f32[8,4,8,128]{3,2,1,0:T(8,128)S(1)} %get-tuple-element.32), channel_id=1, source_target_pairs={{0,1},{1,2},{2,3},{3,0},{4,5},{5,6},{6,7},{7,4},{8,9},{9,10},{10,1... | collective-permute-start | bytes 393224 | tf_op jit(solution)/shard_map/ppermute | solution.py:619
  38.2 7.5 %collective-permute-start.4 = (f32[8,4,8,128]{3,2,1,0:T(8,128)S(1)}, f32[8,4,8,128]{3,2,1,0:T(8,128)S(1)}, u32[]{:S(2)}, u32[]{:S(2)}) collective-permute-start(f32[8,4,8,128]{3,2,1,0:T(8,128)S(1)} %get-tuple-element.33), channel_id=1, source_target_pairs={{0,3},{1,0},{2,1},{3,2},{4,7},{5,4},{6,5},{7,6},{8,11},{9,8},{10,9... | collective-permute-start | bytes 393224 | tf_op jit(solution)/shard_map/ppermute | solution.py:619
  40.0 9.5 %collective-permute-start.3 = (f32[8,4,8,128]{3,2,1,0:T(8,128)S(1)}, f32[8,4,8,128]{3,2,1,0:T(8,128)S(1)}, u32[]{:S(2)}, u32[]{:S(2)}) collective-permute-start(f32[8,4,8,128]{3,2,1,0:T(8,128)S(1)} %get-tuple-element.34), channel_id=1, source_target_pairs={{0,2},{1,3},{2,0},{3,1},{4,6},{5,7},{6,4},{7,5},{8,10},{9,11},{10,... | collective-permute-start | bytes 393224 | tf_op jit(solution)/shard_map/ppermute | solution.py:619
  49.5 6.6 %collective-permute-start.5 = (f32[8,8,128]{2,1,0:T(8,128)S(1)}, f32[8,8,128]{2,1,0:T(8,128)S(1)}, u32[]{:S(2)}, u32[]{:S(2)}) collective-permute-start(f32[8,8,128]{2,1,0:T(8,128)S(1)} %get-tuple-element.35), channel_id=1, source_target_pairs={{0,8},{4,12},{8,16},{12,20},{16,24},{20,28},{24,0},{28,4},{32,40},... | collective-permute-start | bytes 98312 | tf_op jit(solution)/shard_map/ppermute | solution.py:619
  51.9 4.2 %collective-permute-start.7 = (f32[8,8,128]{2,1,0:T(8,128)S(1)}, f32[8,8,128]{2,1,0:T(8,128)S(1)}, u32[]{:S(2)}, u32[]{:S(2)}) collective-permute-start(f32[8,8,128]{2,1,0:T(8,128)S(1)} %get-tuple-element.36), channel_id=1, source_target_pairs={{0,24},{4,28},{8,0},{12,4},{16,8},{20,12},{24,16},{28,20},{32,56},... | collective-permute-start | bytes 98312 | tf_op jit(solution)/shard_map/ppermute | solution.py:619
  54.3 5.1 %collective-permute-start.6 = (f32[8,8,128]{2,1,0:T(8,128)S(1)}, f32[8,8,128]{2,1,0:T(8,128)S(1)}, u32[]{:S(2)}, u32[]{:S(2)}) collective-permute-start(f32[8,8,128]{2,1,0:T(8,128)S(1)} %get-tuple-element.37), channel_id=1, source_target_pairs={{0,16},{4,20},{8,24},{12,28},{16,0},{20,4},{24,8},{28,12},{32,48},... | collective-permute-start | bytes 98312 | tf_op jit(solution)/shard_map/ppermute | solution.py:619
  83.9 1.3 copy-start.2
  85.3 41.3 %copy-start.3 = (f32[16,256,128]{2,1,0:T(8,128)S(1)}, f32[16,256,128]{2,1,0:T(8,128)}, u32[]{:S(2)}) copy-start(f32[16,256,128]{2,1,0:T(8,128)} %copy-done.2) | copy-start | bytes 6291460
  141.7 1.3 copy-start
  143.1 56.4 %all-to-all-start.4 = ((f32[128,32,128]{2,1,0:T(8,128)}), f32[128,32,128]{2,1,0:T(8,128)S(1)}, u32[]{:S(2)}, u32[]{:S(2)}) async-start(f32[128,32,128]{2,1,0:T(8,128)} %bitcast.44), calls=%async_computation.4 | async-start | bytes 4194304 | tf_op jit(solution)/shard_map/all_to_all | solution.py:551
  199.5 6.2 %collective-permute-start.8 = (f32[128,16,128]{2,1,0:T(8,128)S(1)}, f32[128,16,128]{2,1,0:T(8,128)S(1)}, u32[]{:S(2)}, u32[]{:S(2)}) collective-permute-start(f32[128,16,128]{2,1,0:T(8,128)S(1)} %constant_dynamic-slice_fusion), channel_id=1, source_target_pairs={{0,4},{4,0},{8,12},{12,8},{16,20},{20,16},{24,28},{28,24},{32,36},... | collective-permute-start | bytes 3145736 | tf_op jit(solution)/shard_map/ppermute | solution.py:607
